TPU v7x, 32 devices: a whole 2x2x4 slice. The times are simulated.
32 devices in a mesh: blk: 8 (over z, y), head: 4 (over x, core).
Axes of the slice: x: 2, y: 2, z: 4, core: 2. Of those that a mesh axis runs over, the one named last changes fastest.
Arguments:
- inputs: bfloat16 [4096, 704], P('blk'), may hold values from -6 to 6
- out_queries: bfloat16 [8192, 1026], P('blk'), may hold values from -6 to 6
- clip_lengths: int32 [6], replicated, may hold values from 1 to 7767, as said below
- labels: int32 [8192], P('blk'), may hold values from 0 to 703
- modality: int32 [8192], P('blk'), may hold values from 0 to 2
- labeled: int32 [8192], P('blk'), may hold values from 0 to 1
- head_params: float32 [4751360], P(('head', 'blk')), may hold values from -4 to 4
- head_first: float32 [4751360], P(('head', 'blk')), may hold values from -1 to 1
- head_second: float32 [4751360], P(('head', 'blk')), may hold values from 0 to 1
- common_params: float32 [928768], P('blk'), may hold values from -4 to 4
- common_first: float32 [928768], P('blk'), may hold values from -1 to 1
- common_second: float32 [928768], P('blk'), may hold values from 0 to 1
Outputs:
- head_new: float32 [4751360], P(('head', 'blk'))
- head_first_new: float32 [4751360], P(('head', 'blk'))
- head_second_new: float32 [4751360], P(('head', 'blk'))
- head_copy: bfloat16 [4751360], P(('head', 'blk'))
- common_new: float32 [928768], P('blk')
- common_first_new: float32 [928768], P('blk')
- common_second_new: float32 [928768], P('blk')
- common_copy: bfloat16 [928768], P('blk')
- loss_sums: float32 [3], replicated
- label_counts: float32 [3], replicated
- clip_norm: float32 [], replicated
Inputs may be any that keep to these rules, and one draw needn't show every extreme that they name: `clip_lengths`: 6 lengths summing to 8192; one clip, at a place drawn from the seed, holds exactly the largest length and runs from the rows of the first index of blk to those of the last; the others hold together (5) * (85) rows, each fewer than 170.
All inputs are finite; a program needn't handle non-finite values.
Results may differ from a plain program's by a relative error of at most 0.017.
Values may be sent and summed in bfloat16 or wider, within the bound.
A program may use at most 192 MiB of HBM per device.

v0:
```python
import functools

import jax
import jax.numpy as jnp
from jax import lax
from jax.experimental import pallas as pl
from jax.experimental.pallas import tpu as pltpu
from jax.sharding import PartitionSpec as P

D = 512
HEADS = 8
HD = 64
FF = 2048
DI = 704
DQ = 1026
C = 704
LAT = 784
MODES = 3
STEP = 10
LANES = 128
TILE = 16

norm_eps = 1e-05
learn_rate = 0.1
beta_one = 0.9
beta_two = 0.999
adam_eps = 1e-08
weight_decay = 0.01
clip_limit = 0.05
big_negative = -1e30
low = jnp.bfloat16
MESH = pl.DeviceIdType.MESH
MIB = 1 << 20
VMEM_SPEC = pl.BlockSpec(memory_space=pltpu.VMEM)
SMEM_SPEC = pl.BlockSpec(memory_space=pltpu.SMEM)
ANY_SPEC = pl.BlockSpec(memory_space=pl.ANY)


def shape_of(shape, dtype=low):
    return jax.ShapeDtypeStruct(shape, dtype)


def round_up(n, unit):
    return -(-n // unit) * unit


def grid_of(n_blk, n_head):
    cores = 2 if n_head % 2 == 0 else 1
    x = n_head // cores
    y = x if n_blk % x == 0 else 1
    return (n_blk // y, y, x, cores)


def my_place(dims):
    blk, head = lax.axis_index("blk"), lax.axis_index("head")
    return (blk // dims[1], lax.rem(blk, dims[1]), head // dims[3], lax.rem(head, dims[3]))


def shifted(dims, me, offset, sign):
    return tuple(
        m if o == 0 else lax.rem(m + (o if sign > 0 else n - o), n)
        for m, o, n in zip(me, offset, dims)
    )


def blk_of(dims, place):
    return place[0] * dims[1] + place[1]


def head_of(dims, place):
    return place[2] * dims[3] + place[3]


def device_of(dims, place):
    return {"blk": blk_of(dims, place), "head": head_of(dims, place)}


def along(axis, d):
    return tuple(d if a == axis else 0 for a in range(4))


def greet(dims, me, offsets):
    barrier = pltpu.get_barrier_semaphore()
    for offset in offsets:
        pl.semaphore_signal(
            barrier,
            inc=1,
            device_id=device_of(dims, shifted(dims, me, offset, 1)),
            device_id_type=MESH,
        )
    pl.semaphore_wait(barrier, len(offsets))


def axis_peers(dims, axes):
    return [along(axis, d) for axis in axes for d in range(1, dims[axis])]


def remote(src, dst, send_sem, recv_sem, place, dims):
    return pltpu.make_async_remote_copy(
        src_ref=src,
        dst_ref=dst,
        send_sem=send_sem,
        recv_sem=recv_sem,
        device_id=device_of(dims, place),
        device_id_type=MESH,
    )


AHEAD = 10
RING = 0


def in_order(first, follow, size_of, ahead, result):
    queues, busy, flight = {}, {}, {}
    now = 0.0

    def ready(messages):
        for message in messages:
            queues.setdefault(message[1], []).append(message)

    ready(first)
    while True:
        for axis in sorted(queues):
            queue, going = queues[axis], flight.setdefault(axis, [])
            while queue and (not going or busy[axis] < now + ahead):
                message = min(queue)
                queue.remove(message)
                busy[axis] = max(now, busy.get(axis, 0.0)) + size_of(message)
                going.append((busy[axis] + 1.5, message))
                result.append((True, message))
        arrivals = [min(going) for going in flight.values() if going]
        if not arrivals:
            return now
        arrival = min(arrivals)
        flight[arrival[1][1]].remove(arrival)
        now = max(now, arrival[0])
        result.append((False, arrival[1]))
        ready(follow(arrival[1]))


def time_of(rows, axis):
    return rows * LANES * 2 / (300e3 if axis == 3 else 45e3)


def with_at(offset, axis, d):
    return offset[:axis] + (d,) + offset[axis + 1 :]


def gather_order(dims, parts):
    def onward(p, offset, position):
        order = parts[p][3]
        result = []
        for k in range(max(position, 0), 4):
            axis = order[k]
            n = dims[axis]
            if k > position:
                steps = [1] if axis == RING else range(1, n)
                steps = [d for d in steps if d < n]
            else:
                steps = [offset[axis] + 1] if axis == RING and offset[axis] + 1 < n else []
            for d in steps:
                result.append(((k, sum(offset), p), axis, p, with_at(offset, axis, d)))
        return result

    def follow(message):
        rank, axis, p, offset = message
        return onward(p, offset, rank[0])

    first = [m for p in range(len(parts)) for m in onward(p, (0, 0, 0, 0), -1)]
    result = []
    now = in_order(first, follow, lambda m: time_of(parts[m[2]][2], m[1]), AHEAD, result)
    return result, now


def gather_kernel(
    dims,
    parts,
    labels,
    modality,
    labeled,
    head_params,
    common_params,
    head_all,
    common_all,
    head_low,
    common_low,
    common_wide,
    send_sem,
    recv_sem,
    own_sem,
):
    me = my_place(dims)
    my_head = head_of(dims, me)
    n_head = dims[2] * dims[3]
    shard_rows, common_rows = head_params.shape[0], common_params.shape[0]
    per_head = labels.shape[0] // n_head
    row = lax.broadcasted_iota(jnp.int32, labels.shape, 0)
    mine = (row >= my_head * per_head) & (row < (my_head + 1) * per_head) & (labeled[...] == 1)
    lane = lax.broadcasted_iota(jnp.int32, (1, LANES), 1)
    counts = jnp.zeros((1, LANES), jnp.float32)
    for m in range(MODES):
        member = jnp.where(mine & (modality[...] == m), 1.0, 0.0)
        counts = counts + jnp.where(lane == m, jnp.sum(member, (0, 1), keepdims=True), 0.0)
    padding = head_low.shape[0] - shard_rows
    tail = shard_rows // TILE * TILE
    head_low[:tail] = head_params[:tail].astype(low)
    last = [jnp.broadcast_to(counts, (padding, LANES))]
    if shard_rows > tail:
        last = [head_params[tail:]] + last
    head_low[tail:] = jnp.concatenate(last, 0).astype(low)
    common_wide[...] = jnp.zeros(common_wide.shape, jnp.float32)
    common_wide[:common_rows] = common_params[...]
    piece = common_low.shape[0]
    common_low[...] = common_wide[pl.ds(pl.multiple_of(my_head * piece, TILE), piece)].astype(low)

    greet(dims, me, ring_and_others(dims))
    srcs, outs = (head_low, common_low), (head_all, common_all)
    copies = {}

    def block(p, offset):
        place = shifted(dims, me, offset, -1)
        array, first, rows, order = parts[p]
        return outs[array].at[blk_of(dims, place), head_of(dims, place), pl.ds(first, rows)]

    own = []
    for is_send, (rank, axis, p, offset) in gather_order(dims, parts)[0]:
        if is_send:
            step = 1 if axis == RING else offset[axis]
            before = with_at(offset, axis, offset[axis] - step)
            array, first, rows, order = parts[p]
            source = block(p, before) if any(before) else srcs[array].at[pl.ds(first, rows)]
            i = len(copies)
            copies[(p, offset)] = remote(
                source,
                block(p, before),
                send_sem.at[i],
                recv_sem.at[i],
                shifted(dims, me, along(axis, step), 1),
                dims,
            )
            copies[(p, offset)].start()
        else:
            if not own:
                for array in range(2):
                    copy = pltpu.make_async_copy(
                        srcs[array], outs[array].at[blk_of(dims, me), my_head], own_sem.at[array]
                    )
                    copy.start()
                    own.append(copy)
            copies[(p, offset)].wait_recv()
    for copy in copies.values():
        copy.wait_send()
    for copy in own:
        copy.wait()


def ring_and_others(dims):
    ring = {along(RING, 1 % dims[RING]), along(RING, (dims[RING] - 1) % dims[RING])}
    return sorted(ring - {(0, 0, 0, 0)}) + axis_peers(dims, (1, 2, 3))


def cut(array, rows, shares):
    result = []
    first, so_far = 0, 0
    whole = sum(share for share, order in shares)
    for share, order in shares:
        so_far += share
        end = rows * so_far // whole // TILE * TILE if so_far < whole else rows
        if end > first:
            result.append((array, first, end - first, order))
        first = end
    return tuple(result)


ZYXC, ZXYC, YXZC, XYZC = (0, 1, 2, 3), (0, 2, 1, 3), (1, 2, 0, 3), (2, 1, 0, 3)
GATHER_SHARES = ((8, ZYXC), (6, ZXYC), (2, YXZC), (2, XYZC))
REDUCE_SHARES = ((7, ZYXC), (7, ZXYC), (2, YXZC), (2, XYZC))


def gather_all(dims, marks, params, rows, collective_id):
    z, y, x, cores = dims
    parts = cut(0, rows[0], GATHER_SHARES) + cut(1, rows[1], ((1, ZXYC),))
    count = len(parts) * (z * y * x * cores - 1)
    return pl.pallas_call(
        functools.partial(gather_kernel, dims, parts),
        out_shape=[shape_of((z * y, x * cores, n, LANES)) for n in rows],
        in_specs=[VMEM_SPEC] * 5,
        out_specs=[ANY_SPEC] * 2,
        scratch_shapes=[pltpu.VMEM((n, LANES), low) for n in rows]
        + [
            pltpu.VMEM((x * cores * rows[1], LANES), jnp.float32),
            pltpu.SemaphoreType.DMA((count,)),
            pltpu.SemaphoreType.DMA((count,)),
            pltpu.SemaphoreType.DMA((2,)),
        ],
        compiler_params=pltpu.CompilerParams(collective_id=collective_id, has_side_effects=True),
        name="gather_weights",
    )(*marks, *params)


def reduce_order(dims, parts):
    ready, arrived, order = set(), set(), []

    def message(p, position, offset):
        z = offset[RING]
        rank = (dims[RING] - z if z else dims[RING], position, tuple(-o for o in offset), p)
        return (rank, parts[p][3][position], p, position, offset)

    def done(p, position, offset):
        ready.add((p, position, offset))
        if position == 4:
            return []
        axis = parts[p][3][position]
        d = offset[axis]
        first = d != 0 and (axis != RING or d == dims[axis] - 1)
        return ([message(p, position, offset)] if first else []) + advance(p, position, offset)

    def advance(p, position, offset):
        axis = parts[p][3][position]
        n = dims[axis]
        start = with_at(offset, axis, 0)
        if axis == RING:
            here = (p, position, offset)
            if here in ready and here in arrived:
                order.append((None, here))
                if offset[axis]:
                    return [message(p, position, offset)]
                return done(p, position + 1, offset)
        elif (p, position, start) in ready and (p, position + 1, start) not in ready:
            if all((p, position, with_at(start, axis, d)) in arrived for d in range(1, n)):
                order.append((None, (p, position, start)))
                return done(p, position + 1, start)
        return []

    def follow(sent):
        rank, axis, p, position, offset = sent
        here = with_at(offset, axis, offset[axis] - 1) if axis == RING else offset
        arrived.add((p, position, here))
        return advance(p, position, here)

    first = []
    for p in range(len(parts)):
        for offset in all_offsets(dims, range(4)):
            first += done(p, 0, offset)
    now = in_order(first, follow, lambda m: time_of(parts[m[2]][2], m[1]), AHEAD, order)
    return order, now


def all_offsets(dims, axes):
    offsets = [(0, 0, 0, 0)]
    for a in axes:
        offsets = [with_at(o, a, d) for o in offsets for d in range(dims[a])]
    return offsets


def reduce_kernel(dims, parts, *refs):
    srcs, tile = refs[:2], refs[2]
    head_out, common_out, totals = refs[3:6]
    places = len(parts) * 4
    buffers = refs[6 : 6 + places]
    head_sum, common_sum, shares, send_sem, recv_sem, near_tiles, far_tiles = refs[6 + places :]
    sums = (head_sum, common_sum)
    me = my_place(dims)
    z, y, x, cores = dims
    across = peers_across(dims)
    others = [o for o in all_offsets(dims, (0, 1)) if any(o)]
    met = ring_and_others(dims)
    greet(dims, me, met + [o for o in across + others if o not in met])
    push = Pushes(dims, me, send_sem, recv_sem)
    copies = {}

    def slot(p, position, offset):
        order = parts[p][3]
        axis = order[position]
        rest = [o for o in all_offsets(dims, order[position + 1 :])]
        k = rest.index(with_at(offset, axis, 0))
        return buffers[p * 4 + position].at[k, max(offset[axis] - 1, 0)]

    def summed(p, position, offset):
        array, first, rows, order = parts[p]
        if position == 0:
            place = shifted(dims, me, offset, 1)
            return srcs[array].at[blk_of(dims, place), head_of(dims, place), pl.ds(first, rows)]
        return slot(p, position - 1, offset)

    def ring_slot(p, position, offset):
        axis = parts[p][3][position]
        return slot(p, position, with_at(offset, axis, offset[axis] + 1))

    def add(p, position, offset):
        array, first, rows, order = parts[p]
        axis = order[position]
        if axis == RING:
            arrivals = [ring_slot(p, position, offset)]
        else:
            arrivals = [slot(p, position, with_at(offset, axis, d)) for d in range(1, dims[axis])]
        mine = summed(p, position, offset)
        step = row_chunk(rows)

        @pl.loop(0, rows // step)
        def some_rows(n):
            at = pl.ds(pl.multiple_of(n * step, step), step)
            total = mine[at].astype(jnp.float32)
            for arrival in arrivals:
                total = total + arrival[at].astype(jnp.float32)
            if position == 3 and not any(offset):
                sums[array][pl.ds(pl.multiple_of(first + n * step, TILE), step)] = total
            else:
                arrivals[0][at] = total.astype(low)

    for is_send, what in reduce_order(dims, parts)[0]:
        if is_send is None:
            add(*what)
        elif is_send:
            rank, axis, p, position, offset = what
            d = offset[axis]
            started = axis != RING or d == dims[axis] - 1
            source = summed(p, position, offset) if started else ring_slot(p, position, offset)
            step = along(axis, 1 if axis == RING else d)
            copies[what] = push(source, slot(p, position, offset), step)
        else:
            copies[what].wait_recv()
    my_head, my_blk = head_of(dims, me), blk_of(dims, me)
    shares[my_head] = common_sum[...].astype(low)
    share_copies = [push(shares.at[my_head], shares.at[my_head], o) for o in across]
    amount = head_out.shape[0]
    head_out[...] = head_sum[:amount]
    squares = jnp.sum(head_sum[:amount] * head_sum[:amount], 0, keepdims=True)
    squares = squares + jnp.sum(common_sum[...] * common_sum[...], 0, keepdims=True)
    lane = lax.broadcasted_iota(jnp.int32, (1, LANES), 1)
    near_tiles[my_head] = tile[...] + jnp.where(
        lane == MODES, jnp.sum(squares, 1, keepdims=True), 0.0
    )
    near = [push(near_tiles.at[my_head], near_tiles.at[my_head], o) for o in across]
    for copy in near:
        copy.wait_recv()
    far_tiles[my_blk] = jnp.sum(near_tiles[...], 0)
    far = [push(far_tiles.at[my_blk], far_tiles.at[my_blk], o) for o in others]
    for copy in share_copies:
        copy.wait_recv()
    piece = shares.shape[1]
    for k in range(x * cores):
        amount = min(piece, common_out.shape[0] - k * piece)
        common_out[k * piece : k * piece + amount] = shares[k].astype(jnp.float32)[:amount]
    for copy in far:
        copy.wait_recv()
    totals[...] = jnp.sum(far_tiles[...], 0)
    push.finish()


def row_chunk(rows):
    for count in (4, 3, 2):
        if rows % (count * TILE) == 0:
            return rows // count
    return rows


def reduce_all(dims, arrays, valid, tile, collective_id):
    z, y, x, cores = dims
    rows = [array.shape[2] for array in arrays]
    parts = cut(0, rows[0], [(share, order[::-1]) for share, order in REDUCE_SHARES])
    parts = parts + cut(1, rows[1], ((1, ZXYC[::-1]),))
    scratch = []
    for array, first, amount, order in parts:
        for position, axis in enumerate(order):
            rest = len(all_offsets(dims, order[position + 1 :]))
            scratch.append(pltpu.VMEM((rest, dims[axis] - 1, amount, LANES), low))
    count = len(parts) * (z * y * x * cores - 1) + 2 * (x * cores - 1) + z * y - 1
    return pl.pallas_call(
        functools.partial(reduce_kernel, dims, parts),
        out_shape=[
            shape_of((valid[0], LANES), jnp.float32),
            shape_of((valid[1], LANES), jnp.float32),
            shape_of((8, LANES), jnp.float32),
        ],
        in_specs=[VMEM_SPEC] * 3,
        out_specs=[VMEM_SPEC] * 3,
        scratch_shapes=scratch
        + [pltpu.VMEM((n, LANES), jnp.float32) for n in rows]
        + [
            pltpu.VMEM((x * cores, rows[1], LANES), low),
            pltpu.SemaphoreType.DMA((count,)),
            pltpu.SemaphoreType.DMA((count,)),
            pltpu.VMEM((x * cores, 8, LANES), jnp.float32),
            pltpu.VMEM((z * y, 8, LANES), jnp.float32),
        ],
        compiler_params=pltpu.CompilerParams(
            collective_id=collective_id, has_side_effects=True, vmem_limit_bytes=60 * MIB
        ),
        name="reduce_gradients",
    )(*arrays, tile)


def contract_first(a, b):
    return lax.dot_general(a, b, (((0,), (0,)), ((), ())), preferred_element_type=jnp.float32)


def product(a, b):
    return jnp.dot(a, b, preferred_element_type=jnp.float32)


def against(a, b):
    return lax.dot_general(a, b, (((1,), (1,)), ((), ())), preferred_element_type=jnp.float32)


def clip_bounds(lengths):
    result, first = [], 0
    for clip in range(lengths.shape[0]):
        end = first + lengths[clip]
        result.append((first, end))
        first = end
    return result


def clip_borders(bounds, place):
    opening = jnp.zeros(place.shape, jnp.int32)
    ending = jnp.full(place.shape, 1 << 30, jnp.int32)
    for clip, (begin, end) in enumerate(bounds):
        here = place == clip
        opening = jnp.where(here, begin, opening)
        ending = jnp.where(here, end, ending)
    return opening, ending


def lane_of_tail(a):
    return HD if a % 2 == 0 else 0


def in_head(a, axis):
    shape = (1, LANES) if axis else (LANES, 1)
    lane = lax.broadcasted_iota(jnp.int32, shape, axis)
    return (lane >= a * HD) & (lane < (a + 1) * HD)


def all_lanes(block, first, width):
    piece = block[:, first : first + width]
    if width < LANES:
        piece = jnp.concatenate([piece, jnp.zeros((piece.shape[0], LANES - width), piece.dtype)], 1)
    return piece


def with_key_tail(bounds, a, first_row, columns):
    clips = len(bounds)
    place = lax.broadcasted_iota(jnp.int32, (1, LANES), 1) - lane_of_tail(a)
    opening, ending = clip_borders(bounds, place)
    ones = jnp.where((place >= clips) & (place < clips + 3), 1.0, 0.0)
    row = first_row + lax.broadcasted_iota(jnp.int32, columns.shape, 0)
    tail = jnp.where((row >= opening) & (row < ending), ones, big_negative)
    return jnp.where(in_head(a, 1), columns.astype(jnp.float32), tail).astype(low)


def in_three(place, value):
    top = value.astype(low).astype(jnp.float32)
    middle = (value - top).astype(low).astype(jnp.float32)
    bottom = value - top - middle
    return (
        jnp.where(place == 0, top, 0.0)
        + jnp.where(place == 1, middle, 0.0)
        + jnp.where(place == 2, bottom, 0.0)
    )


def with_tail(a, rows, tail):
    return jnp.concatenate([rows, tail] if lane_of_tail(a) else [tail, rows], 0)


def with_query_tail(bounds, a, first_row, rows, extra):
    clips = len(bounds)
    place = lax.broadcasted_iota(jnp.int32, (HD, 1), 0)
    opening, ending = clip_borders(bounds, place)
    row = first_row + lax.broadcasted_iota(jnp.int32, (1, rows.shape[1]), 1)
    inside = (place < clips) & (row >= opening) & (row < ending)
    tail = jnp.where(inside, 1.0, 0.0)
    if extra is not None:
        tail = tail + in_three(place - clips, -extra)
    return with_tail(a, rows * HD ** (-0.5), tail).astype(low)


class Pushes:
    def __init__(self, dims, me, send_sem, recv_sem):
        self.dims, self.me, self.send_sem, self.recv_sem = dims, me, send_sem, recv_sem
        self.started = []

    def __call__(self, src, dst, offset):
        i = len(self.started)
        place = shifted(self.dims, self.me, offset, 1)
        copy = remote(src, dst, self.send_sem.at[i], self.recv_sem.at[i], place, self.dims)
        copy.start()
        self.started.append(copy)
        return copy

    def finish(self):
        for copy in self.started:
            copy.wait_send()


def peers_across(dims):
    z, y, x, cores = dims
    across = [(0, 0, a, c) for a in range(x) for c in range(cores) if (a, c) != (0, 0)]
    return sorted(across, key=lambda o: (o[2] == 0, o[3]))


def ring_and_sides(dims):
    z = dims[0]
    ring = sorted({along(0, 1 % z), along(0, (z - 1) % z)} - {(0, 0, 0, 0)})
    return ring + axis_peers(dims, (1,))


def attend_kernel(
    dims,
    heads,
    key_step,
    query_step,
    lengths,
    q_in,
    kv_in,
    o_out,
    lse,
    out_t,
    q_all,
    kv_all,
    keys,
    values_t,
    queries,
    top,
    accum,
    o_mine,
    send_sem,
    recv_sem,
    own_sem,
):
    z, y, x, cores = dims
    me = my_place(dims)
    bounds = clip_bounds(lengths)
    n_head = x * cores
    rows, width = q_in.shape[1], heads * HD
    amount = n_head * rows
    my_blk, my_head = blk_of(dims, me), head_of(dims, me)
    across = peers_across(dims)
    sides = axis_peers(dims, (1,))
    greet(dims, me, across + ring_and_sides(dims))
    push = Pushes(dims, me, send_sem, recv_sem)
    own_kv = pltpu.make_async_copy(kv_in.at[my_head], kv_all.at[my_blk, my_head], own_sem.at[0])
    own_q = pltpu.make_async_copy(q_in.at[my_head], q_all.at[my_head], own_sem.at[1])
    own_kv.start()
    own_q.start()

    def to_head(src, dst, o):
        return push(src.at[head_of(dims, shifted(dims, me, o, 1))], dst, o)

    kv_copies = {o: to_head(kv_in, kv_all.at[my_blk, my_head], o) for o in across}
    q_copies = [to_head(q_in, q_all.at[my_head], o) for o in across]
    ring, side = {}, {}
    pieces = [(0, 0, 0, 0)] + across[::-1]

    def send_on(s, n):
        block = kv_all.at[
            blk_of(dims, shifted(dims, me, along(0, s), -1)),
            head_of(dims, shifted(dims, me, pieces[n], -1)),
        ]
        if s < z - 1:
            ring[(s + 1, n)] = push(block, block, along(0, 1))
        for o in sides:
            side[(s, n, o)] = push(block, block, o)

    def compute(offset):
        blk = blk_of(dims, shifted(dims, me, offset, -1))

        @pl.loop(0, n_head)
        def build(h):
            at = pl.ds(pl.multiple_of(h * rows, rows), rows)
            block = kv_all[blk, h]
            k_block, v_block = all_lanes(block, 0, width), all_lanes(block, width, width)
            v_t = v_block.astype(jnp.float32).T
            for a in range(heads):
                keys[a, at, :] = with_key_tail(bounds, a, blk * amount + h * rows, k_block)
                values_t[a, :HD, at] = v_t[a * HD : (a + 1) * HD].astype(low)

        @pl.loop(0, amount // query_step)
        def query_block(n):
            at = pl.ds(pl.multiple_of(n * query_step, query_step), query_step)
            for a in range(heads):
                query = queries[a, :, at]
                highest = jnp.full((8, query_step), -1e38, jnp.float32)
                for k in range(0, amount, key_step):
                    scores = product(keys[a, k : k + key_step, :], query)
                    highest = jnp.maximum(
                        highest, jnp.max(scores.reshape(key_step // 8, 8, query_step), 0)
                    )
                old = top[a, :, at]
                new = jnp.maximum(old, jnp.max(highest, 0, keepdims=True))
                top[a, :, at] = new
                total = accum[a, :, at] * jnp.exp(old - new)
                for k in range(0, amount, key_step):
                    scores = product(keys[a, k : k + key_step, :], query)
                    probs = jnp.exp(scores - new).astype(low)
                    total = total + product(values_t[a, :, k : k + key_step], probs)
                accum[a, :, at] = total

    for a in range(heads):
        values_t[a, HD:, :] = jnp.ones((values_t.shape[1] - HD, amount), low)
        top[a] = jnp.full((1, amount), -1e38, jnp.float32)
        accum[a] = jnp.zeros(accum.shape[1:], jnp.float32)
    own_kv.wait()
    send_on(0, 0)
    for n in range(1, n_head):
        kv_copies[pieces[n]].wait_recv()
        send_on(0, n)
    own_q.wait()
    for copy in q_copies:
        copy.wait_recv()
    for a in range(heads):
        for h in range(n_head):
            q_t = all_lanes(q_all[h], 0, width).astype(jnp.float32).T
            queries[a, :, h * rows : (h + 1) * rows] = with_query_tail(
                bounds, a, my_blk * amount + h * rows, q_t[a * HD : (a + 1) * HD], None
            )
    compute((0, 0, 0, 0))
    for s in range(1, z + 1):
        if s < z:
            for n in range(n_head):
                ring[(s, n)].wait_recv()
                send_on(s, n)
            compute(along(0, s))
        for o in sides:
            for n in range(n_head):
                side[(s - 1, n, o)].wait_recv()
            compute((s - 1, o[1], 0, 0))
    for a in range(heads):
        total = accum[a, HD : HD + 1, :]
        out_t[a * HD : (a + 1) * HD, :] = accum[a, :HD, :] / total
        lse[a : a + 1, :] = top[a] + jnp.log(total)
    for h in range(n_head):
        o_mine[h] = out_t[:, h * rows : (h + 1) * rows].T.astype(low)
    o_copies = [to_head(o_mine, o_out.at[my_head], o) for o in across]
    own_o = pltpu.make_async_copy(o_mine.at[my_head], o_out.at[my_head], own_sem.at[2])
    own_o.start()
    own_o.wait()
    for copy in o_copies:
        copy.wait_recv()
    push.finish()


def attend(dims, lengths, q, kv, heads, collective_id):
    z, y, x, cores = dims
    n_head, rows, width = q.shape
    amount = n_head * rows
    count = 3 * (n_head - 1) + n_head * (z - 1 + z * (y - 1))
    return pl.pallas_call(
        functools.partial(attend_kernel, dims, heads, 256, 256),
        out_shape=(
            jax.ShapeDtypeStruct(q.shape, low),
            jax.ShapeDtypeStruct((heads, amount), jnp.float32),
            jax.ShapeDtypeStruct((width, amount), jnp.float32),
            jax.ShapeDtypeStruct(q.shape, low),
            jax.ShapeDtypeStruct((z * y,) + kv.shape, low),
        ),
        in_specs=[SMEM_SPEC, VMEM_SPEC, VMEM_SPEC],
        out_specs=[VMEM_SPEC] * 5,
        scratch_shapes=[
            pltpu.VMEM((heads, amount, LANES), low),
            pltpu.VMEM((heads, HD + TILE, amount), low),
            pltpu.VMEM((heads, LANES, amount), low),
            pltpu.VMEM((heads, 1, amount), jnp.float32),
            pltpu.VMEM((heads, HD + TILE, amount), jnp.float32),
            pltpu.VMEM(q.shape, low),
            pltpu.SemaphoreType.DMA((count,)),
            pltpu.SemaphoreType.DMA((count,)),
            pltpu.SemaphoreType.DMA((3,)),
        ],
        compiler_params=pltpu.CompilerParams(
            collective_id=collective_id, has_side_effects=True, vmem_limit_bytes=56 * MIB
        ),
        name="attend",
    )(lengths, q, kv)


def attend_back_kernel(
    dims,
    heads,
    key_step,
    lengths,
    q_all,
    kv_all,
    do_in,
    out_t,
    lse,
    d_q_out,
    d_kv_out,
    do_all,
    keys,
    keys_t,
    values,
    queries,
    douts,
    d_q_t,
    q_rows,
    do_rows,
    side_out,
    side_in,
    ring_out,
    ring_in,
    mine,
    d_q_mine,
    d_kv_mine,
    send_sem,
    recv_sem,
    own_sem,
):
    z, y, x, cores = dims
    me = my_place(dims)
    bounds = clip_bounds(lengths)
    n_head, rows, width = q_all.shape
    amount = n_head * rows
    my_blk, my_head = blk_of(dims, me), head_of(dims, me)
    across = peers_across(dims)
    sides = axis_peers(dims, (1,))
    greet(dims, me, across + ring_and_sides(dims))
    push = Pushes(dims, me, send_sem, recv_sem)

    def to_head(src, dst, o):
        return push(src.at[head_of(dims, shifted(dims, me, o, 1))], dst, o)

    do_copies = [to_head(do_in, do_all.at[my_head], o) for o in across]
    own_do = pltpu.make_async_copy(do_in.at[my_head], do_all.at[my_head], own_sem.at[0])
    own_do.start()
    place = lax.broadcasted_iota(jnp.int32, (HD, 1), 0)

    def at_head(h):
        return slice(h * rows, (h + 1) * rows)

    for h in range(n_head):
        block = all_lanes(q_all[h], 0, width).astype(jnp.float32)
        q_t = block.T
        for a in range(heads):
            queries[a, :, at_head(h)] = with_query_tail(
                bounds,
                a,
                my_blk * amount + h * rows,
                q_t[a * HD : (a + 1) * HD],
                lse[a : a + 1, at_head(h)],
            )
            q_rows[a, at_head(h), :] = jnp.where(in_head(a, 1), block * HD ** (-0.5), 0.0).astype(low)
    for a in range(heads):
        d_q_t[a] = jnp.zeros(d_q_t.shape[1:], jnp.float32)
    own_do.wait()
    for copy in do_copies:
        copy.wait_recv()
    for h in range(n_head):
        block = all_lanes(do_all[h], 0, width).astype(jnp.float32)
        do_t = block.T
        for a in range(heads):
            part = do_t[a * HD : (a + 1) * HD]
            delta = jnp.sum(part * out_t[a * HD : (a + 1) * HD, at_head(h)], 0, keepdims=True)
            douts[a, :, at_head(h)] = with_tail(a, part, in_three(place, -delta)).astype(low)
            do_rows[a, at_head(h), :] = jnp.where(in_head(a, 1), block, 0.0).astype(low)

    def compute(offset, target):
        blk = blk_of(dims, shifted(dims, me, offset, 1))

        @pl.loop(0, n_head)
        def build(h):
            at = pl.ds(pl.multiple_of(h * rows, rows), rows)
            block = kv_all[blk, h]
            k_block, v_block = all_lanes(block, 0, width), all_lanes(block, width, width)
            k_t = k_block.astype(jnp.float32).T
            lane = lax.broadcasted_iota(jnp.int32, (1, LANES), 1)
            for a in range(heads):
                keys[a, at, :] = with_key_tail(bounds, a, blk * amount + h * rows, k_block)
                keys_t[a, :, at] = k_t[a * HD : (a + 1) * HD].astype(low)
                tail = lane - lane_of_tail(a)
                ones = jnp.where((tail >= 0) & (tail < 3), 1.0, 0.0)
                values[a, at, :] = jnp.where(
                    in_head(a, 1), v_block.astype(jnp.float32), ones
                ).astype(low)

        @pl.loop(0, amount // key_step)
        def key_block(k):
            at = pl.ds(pl.multiple_of(k * key_step, key_step), key_step)
            d_key = jnp.zeros((key_step, LANES), jnp.float32)
            d_value = jnp.zeros((key_step, LANES), jnp.float32)
            for a in range(heads):
                probs = jnp.exp(product(keys[a, at, :], queries[a]))
                d_probs = product(values[a, at, :], douts[a])
                d_scores = (probs * d_probs).astype(low)
                d_value = d_value + product(probs.astype(low), do_rows[a])
                d_key = d_key + product(d_scores, q_rows[a])
                d_q_t[a] = d_q_t[a] + product(keys_t[a, :, at], d_scores)
            target[at, :] = jnp.concatenate([d_key[:, :width], d_value[:, :width]], 1).astype(
                target.dtype
            )

    side, ring = {}, {}

    def send_sides(s):
        for o in sides:
            compute((z - s, o[1], 0, 0), side_out.at[s - 1, o[1] - 1])
            side[(s, o)] = push(side_out.at[s - 1, o[1] - 1], side_in.at[s - 1, o[1] - 1], o)

    def combine(s):
        for o in sides:
            side[(s, o)].wait_recv()
        if s > 1:
            ring[s - 1].wait_recv()

        for h in range(n_head):
            total = mine[(s - 1) % 2, at_head(h), :]
            for o in sides:
                total = total + side_in[s - 1, o[1] - 1, at_head(h), :].astype(jnp.float32)
            if s > 1:
                total = total + ring_in[s - 2, at_head(h), :].astype(jnp.float32)
            if s < z:
                ring_out[s - 1, at_head(h), :] = total.astype(low)
            else:
                d_kv_mine[h] = total.astype(low)
        if s < z:
            ring[s] = push(ring_out.at[s - 1], ring_in.at[s - 1], along(0, 1))

    for s in range(1, z + 1):
        send_sides(s)
        if s > 1:
            combine(s - 1)
        compute((z - s if s < z else 0, 0, 0, 0), mine.at[(s - 1) % 2])
    for h in range(n_head):
        block = jnp.concatenate([d_q_t[a, :, at_head(h)] for a in range(heads)], 0) * HD ** (-0.5)
        d_q_mine[h] = block.T.astype(low)
    copies = [to_head(d_q_mine, d_q_out.at[my_head], o) for o in across]
    own_q = pltpu.make_async_copy(d_q_mine.at[my_head], d_q_out.at[my_head], own_sem.at[1])
    own_q.start()
    combine(z)
    copies += [to_head(d_kv_mine, d_kv_out.at[my_head], o) for o in across]
    own_kv = pltpu.make_async_copy(d_kv_mine.at[my_head], d_kv_out.at[my_head], own_sem.at[2])
    own_kv.start()
    own_q.wait()
    own_kv.wait()
    for copy in copies:
        copy.wait_recv()
    push.finish()


def attend_back(dims, lengths, q, kv, dout, out_t, lse, heads, collective_id):
    z, y, x, cores = dims
    n_head, rows, width = q.shape
    amount = n_head * rows
    count = 3 * (n_head - 1) + z * (y - 1) + z - 1
    block = (amount, 2 * width)
    others = max(y - 1, 1)
    return pl.pallas_call(
        functools.partial(attend_back_kernel, dims, heads, 256),
        out_shape=(
            jax.ShapeDtypeStruct(q.shape, low),
            jax.ShapeDtypeStruct((n_head, rows, 2 * width), low),
        ),
        in_specs=[SMEM_SPEC] + [VMEM_SPEC] * 5,
        out_specs=[VMEM_SPEC] * 2,
        scratch_shapes=[
            pltpu.VMEM(q.shape, low),
            pltpu.VMEM((heads, amount, LANES), low),
            pltpu.VMEM((heads, HD, amount), low),
            pltpu.VMEM((heads, amount, LANES), low),
            pltpu.VMEM((heads, LANES, amount), low),
            pltpu.VMEM((heads, LANES, amount), low),
            pltpu.VMEM((heads, HD, amount), jnp.float32),
            pltpu.VMEM((heads, amount, LANES), low),
            pltpu.VMEM((heads, amount, LANES), low),
            pltpu.VMEM((z, others) + block, low),
            pltpu.VMEM((z, others) + block, low),
            pltpu.VMEM((max(z - 1, 1),) + block, low),
            pltpu.VMEM((max(z - 1, 1),) + block, low),
            pltpu.VMEM((2,) + block, jnp.float32),
            pltpu.VMEM(q.shape, low),
            pltpu.VMEM((n_head, rows, 2 * width), low),
            pltpu.SemaphoreType.DMA((count,)),
            pltpu.SemaphoreType.DMA((count,)),
            pltpu.SemaphoreType.DMA((3,)),
        ],
        compiler_params=pltpu.CompilerParams(
            collective_id=collective_id, has_side_effects=True, vmem_limit_bytes=60 * MIB
        ),
        name="attend_back",
    )(lengths, q, kv, dout, out_t, lse)


def part_shapes(n_head):
    width = HEADS // n_head * HD
    hidden = FF // n_head
    return (
        (D, width, True),
        (DI, 2 * width, True),
        (width, D, False),
        (D, 3 * width, True),
        (width, D, False),
        (D, hidden, True),
        (hidden, D, False),
        (D, C // n_head, True),
    )


def borders(n_head):
    result = [0]
    for rows, columns, joined in part_shapes(n_head):
        result.append(result[-1] + rows * columns // LANES)
    return result


def period(columns):
    amount = 1
    while amount * columns % LANES:
        amount *= 2
    return amount


def segments(start, amount, unit):
    result = []
    while amount > 0:
        which, at = divmod(start, unit)
        size = min(unit - at, amount)
        result.append((which, at, at + size))
        start, amount = start + size, amount - size
    return result


def joined_lanes(pieces):
    return pieces[0] if len(pieces) == 1 else jnp.concatenate(pieces, 1)


def lane_blocks(value):
    rows, columns = value.shape
    missing = -columns % LANES
    if missing:
        value = jnp.concatenate([value, jnp.zeros((rows, missing), value.dtype)], 1)
    return [value[:, i : i + LANES] for i in range(0, columns + missing, LANES)]


def every(first, amount, stride):
    return pl.ds(first, amount) if stride == 1 else pl.ds(first, amount, stride=stride)


def matrix_of(stage, first, rows, columns, line):
    if columns % LANES == 0:
        stride = columns // LANES
        for j in range(stride):
            yield j * LANES, stage[every(first + j, rows, stride), :]
        return
    height = period(columns)
    stride = height * columns // LANES
    for k in range(height):
        pieces = [
            stage[every(first + which, rows // height, stride), :][:, begin:end]
            for which, begin, end in segments(k * columns, columns, LANES)
        ]
        for i, piece in enumerate(lane_blocks(joined_lanes(pieces))):
            line[i, every(k, rows // height, height), :] = piece
    for i in range(-(-columns // LANES)):
        yield i * LANES, line[i, :rows, : min(columns - i * LANES, LANES)]


def matrix_into(stage, first, value, line):
    rows, columns = value.shape
    if columns % LANES == 0:
        stride = columns // LANES
        for j in range(stride):
            stage[every(first + j, rows, stride), :] = value[:, j * LANES : (j + 1) * LANES]
        return
    height = period(columns)
    stride = height * columns // LANES
    for i, piece in enumerate(lane_blocks(value)):
        line[i, :rows, :] = piece
    for i in range(stride):
        pieces = [
            line[which, every(k, rows // height, height), :][:, begin:end]
            for k, first_lane, last_lane in segments(i * LANES, LANES, columns)
            for which, begin, end in segments(first_lane, last_lane - first_lane, LANES)
        ]
        stage[every(first + i, rows // height, stride), :] = joined_lanes(pieces)


def load_stage(stage, held, first_shard, shard_rows, group):
    for b in range(held.shape[0]):
        stage[pl.ds(b * shard_rows, shard_rows), :] = held[b, group, :shard_rows, :].astype(jnp.float32)


def load_common(stage, held, valid):
    piece = held.shape[2]
    for b in range(held.shape[0]):
        for k in range(held.shape[1]):
            amount = min(piece, valid - k * piece)
            stage[b * valid + k * piece : b * valid + k * piece + amount, :] = held[b, k].astype(
                jnp.float32
            )[:amount]


def common_blocks(first_row, last_row, valid):
    return first_row // valid, -(-last_row // valid) - first_row // valid


def load_matrices(stage, first_row, n_head, group, which, targets, line):
    starts, shapes = borders(n_head), part_shapes(n_head)
    for m, target in zip(which, targets):
        rows, columns, joined = shapes[m]
        row = 0 if joined else group * rows
        column = group * columns if joined else 0
        for j, value in matrix_of(stage, starts[m] - first_row, rows, columns, line):
            size = value.shape[1]
            target[row : row + rows, column + j : column + j + size] = value.astype(target.dtype)


def normalized(x):
    centre = x - jnp.mean(x, -1, keepdims=True)
    rate = lax.rsqrt(jnp.mean(centre * centre, -1, keepdims=True) + norm_eps)
    return centre * rate, rate


def layer_norm(x, gain):
    return normalized(x)[0] * gain


def norm_pullback(x, gain, grad):
    unit, rate = normalized(x)
    inside = grad * gain
    both = jnp.mean(inside * unit, -1, keepdims=True)
    d_x = rate * (inside - jnp.mean(inside, -1, keepdims=True) - unit * both)
    return d_x, jnp.sum(grad * unit, 0, keepdims=True)


def head_lanes(group, heads, value):
    width = heads * HD
    block = value[:, group * width : (group + 1) * width]
    lane = lax.broadcasted_iota(jnp.int32, (1, width), 1)
    result = []
    for a in range(heads):
        here = (lane >= a * HD) & (lane < (a + 1) * HD)
        result.append((here, jnp.where(here, block, jnp.zeros_like(block))))
    return result


def place_of(bounds, first, amount):
    row = first + lax.broadcasted_iota(jnp.int32, (amount, 1), 0)
    opening = jnp.zeros((amount, 1), jnp.int32)
    for begin, end in bounds:
        opening = jnp.where((row >= begin) & (row < end), begin, opening)
    offset = row - opening
    turns = jnp.floor((offset.astype(jnp.float32) + 0.5) * (1.0 / LAT)).astype(jnp.int32)
    return offset - turns * LAT


def picked_rows(bounds, rows, n_head):
    first = lax.axis_index("blk") * (rows * n_head) + lax.axis_index("head") * rows
    lane = lax.broadcasted_iota(jnp.int32, (rows, LAT), 1)
    return jnp.where(lane == place_of(bounds, first, rows), 1.0, 0.0).astype(low)


def enc_scores(q_head, keys):
    return against(q_head, keys) * HD ** (-0.5)


def encode_kernel(
    n_head,
    shard_rows,
    valid,
    rows,
    lengths,
    weights,
    common,
    inputs_t,
    enc_query,
    enc_keyval,
    enc_output,
    self_project,
    gains,
    z_zero,
    h_zero,
    x_norm_t,
    q_enc,
    kv_enc,
    o_enc,
    z_one,
    h_one,
    q_self,
    kv_self,
    counts,
    held,
    held_common,
    held_counts,
    stage,
    stage_common,
    line,
    latent_table,
    sems,
):
    heads = HEADS // n_head
    width = heads * HD
    shards = held.shape[0]
    bounds = clip_bounds(lengths)
    first = DQ * D // LANES
    block, blocks = common_blocks(first, first + (LAT + 4) * D // LANES, valid)
    tail = shard_rows // TILE * TILE
    copies = [
        pltpu.make_async_copy(common.at[pl.ds(block, blocks)], held_common, sems.at[0]),
        pltpu.make_async_copy(weights.at[pl.ds(0, shards)], held, sems.at[1]),
        pltpu.make_async_copy(weights.at[:, :, pl.ds(tail, TILE)], held_counts, sems.at[2]),
    ]
    for copy in copies:
        copy.start()
    centre = inputs_t[...].astype(jnp.float32)
    centre = centre - jnp.mean(centre, 0, keepdims=True)
    rate = lax.rsqrt(jnp.mean(centre * centre, 0, keepdims=True) + norm_eps)
    x_norm_t[...] = (centre * rate).astype(low)
    copies[0].wait()
    load_common(stage_common, held_common, valid)
    first = first - block * valid
    for j, value in matrix_of(stage_common, first, LAT, D, line):
        latent_table[:, j : j + LANES] = value.astype(low)
    for j, value in matrix_of(stage_common, first + LAT * D // LANES, 4, D, line):
        gains[:, j : j + LANES] = value
    picked = picked_rows(bounds, rows, n_head)
    z_zero[...] = product(picked, latent_table[...])
    h_zero[...] = layer_norm(z_zero[...], gains[0:1, :]).astype(low)
    copies[2].wait()
    counted = held_counts[...].astype(jnp.float32)[:, :, shard_rows - tail : shard_rows - tail + 1]
    counts[...] = jnp.broadcast_to(jnp.sum(counted, (0, 1)), counts.shape)
    copies[1].wait()
    for g in range(n_head):
        load_stage(stage, held, 0, shard_rows, g)
        load_matrices(
            stage, 0, n_head, g, (0, 1, 2, 3), (enc_query, enc_keyval, enc_output, self_project), line
        )
    q_enc[...] = product(h_zero[...], enc_query[...]).astype(low)
    kv_enc[...] = contract_first(x_norm_t[...], enc_keyval[...]).astype(low)
    for g in range(n_head):
        keys = kv_enc[:, 2 * g * width : (2 * g + 1) * width]
        values = kv_enc[:, (2 * g + 1) * width : (2 * g + 2) * width]
        outcome = jnp.zeros((rows, width), jnp.float32)
        for here, q_head in head_lanes(g, heads, q_enc[...]):
            scores = enc_scores(q_head, keys)
            probs = jnp.exp(scores - jnp.max(scores, 1, keepdims=True))
            total = jnp.sum(probs, 1, keepdims=True)
            outcome = jnp.where(here, product(probs.astype(low), values) / total, outcome)
        o_enc[:, g * width : (g + 1) * width] = outcome.astype(low)
    z_one[...] = z_zero[...] + product(o_enc[...], enc_output[...])
    h_one[...] = layer_norm(z_one[...], gains[1:2, :]).astype(low)
    projected = product(h_one[...], self_project[...]).astype(low)
    for g in range(n_head):
        q_self[g] = projected[:, 3 * g * width : (3 * g + 1) * width]
        kv_self[g] = projected[:, (3 * g + 1) * width : (3 * g + 3) * width]


LINE = pltpu.VMEM((4, round_up(max(D, DI), 8), LANES), jnp.float32)


def shards_of(n_head, shard_rows, first, last):
    starts = borders(n_head)
    begin = starts[first] // shard_rows
    return begin, -(-starts[last] // shard_rows) - begin


def encode(lengths, weights, common, inputs_t, valid, rows, n_head, shard_rows):
    width = HEADS // n_head * HD
    begin, shards = shards_of(n_head, shard_rows, 0, 4)
    query_rows = DQ * D // LANES
    block, blocks = common_blocks(query_rows, query_rows + (LAT + 4) * D // LANES, valid)
    keys = inputs_t.shape[1]
    return pl.pallas_call(
        functools.partial(encode_kernel, n_head, shard_rows, valid, rows),
        out_shape=[
            shape_of((D, D)),
            shape_of((DI, 2 * D)),
            shape_of((D, D)),
            shape_of((D, 3 * D)),
            shape_of((4, D), jnp.float32),
            shape_of((rows, D), jnp.float32),
            shape_of((rows, D)),
            shape_of(inputs_t.shape),
            shape_of((rows, D)),
            shape_of((keys, 2 * D)),
            shape_of((rows, D)),
            shape_of((rows, D), jnp.float32),
            shape_of((rows, D)),
            shape_of((n_head, rows, width)),
            shape_of((n_head, rows, 2 * width)),
            shape_of((8, LANES), jnp.float32),
        ],
        in_specs=[SMEM_SPEC, ANY_SPEC, ANY_SPEC, VMEM_SPEC],
        out_specs=[VMEM_SPEC] * 16,
        scratch_shapes=[
            pltpu.VMEM((shards,) + weights.shape[1:], low),
            pltpu.VMEM((blocks,) + common.shape[1:], low),
            pltpu.VMEM(weights.shape[:2] + (TILE, LANES), low),
            pltpu.VMEM((shards * shard_rows, LANES), jnp.float32),
            pltpu.VMEM((blocks * valid, LANES), jnp.float32),
            LINE,
            pltpu.VMEM((LAT, D), low),
            pltpu.SemaphoreType.DMA((3,)),
        ],
        compiler_params=pltpu.CompilerParams(vmem_limit_bytes=56 * MIB),
        name="encode",
    )(lengths, weights, common, inputs_t)


def gelu_and_slope(x):
    rate = (2.0 / jnp.pi) ** 0.5
    cubic = 0.044715
    t = jnp.tanh(rate * (x + cubic * x * x * x))
    slope = 0.5 * (1.0 + t) + 0.5 * x * (1.0 - t * t) * rate * (1.0 + 3.0 * cubic * x * x)
    return 0.5 * x * (1.0 + t), slope


def my_column(marks, rows):
    turned = marks[...].astype(jnp.float32).T
    column = lax.broadcasted_iota(jnp.int32, turned.shape, 1)
    per_head = rows // LANES
    first = lax.axis_index("head") * per_head
    picked = [
        jnp.sum(jnp.where(column == first + k, turned, 0.0), 1, keepdims=True)
        for k in range(per_head)
    ]
    return jnp.concatenate(picked, 0) if per_head > 1 else picked[0]


def middle_kernel(
    n_head,
    shard_rows,
    valid,
    first_shard,
    rows,
    counts,
    weights,
    common,
    z_one,
    o_self,
    out_queries_t,
    labels,
    modality,
    labeled,
    gains,
    dout,
    d_two_out,
    tile,
    query_grad,
    gain_grads,
    grads,
    held,
    held_common,
    stage,
    stage_common,
    line,
    self_output,
    hidden_in,
    hidden_out,
    class_table,
    query_table,
    slope,
    activ,
    sems,
):
    heads = HEADS // n_head
    width, hidden, classes = heads * HD, FF // n_head, C // n_head
    shards = held.shape[0]
    first_row = first_shard * shard_rows
    starts = borders(n_head)
    copies = [
        pltpu.make_async_copy(common.at[pl.ds(0, held_common.shape[0])], held_common, sems.at[0]),
        pltpu.make_async_copy(weights.at[pl.ds(first_shard, shards)], held, sems.at[1]),
    ]
    for copy in copies:
        copy.start()
    copies[0].wait()
    load_common(stage_common, held_common, valid)
    for j, value in matrix_of(stage_common, 0, DQ, D, line):
        query_table[:, j : j + LANES] = value.astype(low)
    copies[1].wait()
    for g in range(n_head):
        load_stage(stage, held, first_shard, shard_rows, g)
        load_matrices(
            stage, first_row, n_head, g, (4, 5, 6, 7), (self_output, hidden_in, hidden_out, class_table), line
        )
    gain_two, gain_three = gains[2:3, :], gains[3:4, :]
    o_low = jnp.concatenate([o_self[g] for g in range(n_head)], 1)
    z_two = z_one[...] + product(o_low, self_output[...])
    h_two = layer_norm(z_two, gain_two).astype(low)
    value, bend = gelu_and_slope(product(h_two, hidden_in[...]))
    activ[...] = value.astype(low)
    slope[...] = bend
    z_three = z_two + product(activ[...], hidden_out[...])
    queries_t = out_queries_t[...]
    decoded = layer_norm(z_three, gain_three) + contract_first(queries_t, query_table[...])
    decoded = decoded.astype(low)
    logits = product(decoded, class_table[...])
    label, kind, counted = (my_column(marks, rows) for marks in (labels, modality, labeled))
    lane = lax.broadcasted_iota(jnp.int32, (rows, C), 1).astype(jnp.float32)
    is_target = jnp.where(lane == label, 1.0, 0.0)
    row_top = jnp.max(logits, 1, keepdims=True)
    row_lse = row_top + jnp.log(jnp.sum(jnp.exp(logits - row_top), 1, keepdims=True))
    loss = row_lse - jnp.sum(is_target * logits, 1, keepdims=True)
    weight = jnp.zeros((rows, 1), jnp.float32)
    place = lax.broadcasted_iota(jnp.int32, (1, LANES), 1)
    losses = jnp.zeros((1, LANES), jnp.float32)
    for m in range(MODES):
        member = jnp.where((kind == m) & (counted == 1.0), 1.0, 0.0)
        weight = weight + member / jnp.maximum(counts[0:1, m : m + 1], 1.0)
        losses = losses + jnp.where(place == m, jnp.sum(loss * member, 0, keepdims=True), 0.0)
    tile[...] = jnp.broadcast_to(losses, tile.shape)
    dlogits = (weight * (jnp.exp(logits - row_lse) - is_target)).astype(low)
    d_decoded = against(dlogits, class_table[...])
    matrix_into(query_grad, 0, product(queries_t, d_decoded.astype(low)), line)
    d_three, gain_three_grad = norm_pullback(z_three, gain_three, d_decoded)
    d_branch = d_three.astype(low)
    d_pre = (slope[...] * against(d_branch, hidden_out[...])).astype(low)
    d_middle, gain_two_grad = norm_pullback(z_two, gain_two, against(d_pre, hidden_in[...]))
    d_two = d_three + d_middle
    d_two_out[...] = d_two
    gain_grads[...] = jnp.concatenate([gain_two_grad, gain_three_grad], 0)
    d_two_low = d_two.astype(low)
    d_o = against(d_two_low, self_output[...]).astype(low)
    for g in range(n_head):
        dout[g] = d_o[:, g * width : (g + 1) * width]
    for g in range(n_head):
        results = (
            contract_first(o_self[g], d_two_low),
            contract_first(h_two, d_pre[:, g * hidden : (g + 1) * hidden]),
            contract_first(activ[:, g * hidden : (g + 1) * hidden], d_branch),
            contract_first(decoded, dlogits[:, g * classes : (g + 1) * classes]),
        )
        for m, result in zip((4, 5, 6, 7), results):
            matrix_into(stage, starts[m] - first_row, result, line)
        for b in range(shards):
            held[b, g, :shard_rows, :] = stage[pl.ds(b * shard_rows, shard_rows), :].astype(low)
    back = pltpu.make_async_copy(held, grads.at[pl.ds(first_shard, shards)], sems.at[2])
    back.start()
    back.wait()


def middle(counts, weights, common, z_one, o_self, out_queries_t, marks, gains, valid, n_head, shard_rows):
    rows = z_one.shape[0]
    begin, shards = shards_of(n_head, shard_rows, 4, 8)
    query_rows = DQ * D // LANES
    block, blocks = common_blocks(0, query_rows, valid)
    return pl.pallas_call(
        functools.partial(middle_kernel, n_head, shard_rows, valid, begin, rows),
        grid=(1,),
        out_shape=[
            shape_of(o_self.shape),
            shape_of((rows, D), jnp.float32),
            shape_of((8, LANES), jnp.float32),
            shape_of((query_rows, LANES), jnp.float32),
            shape_of((2, D), jnp.float32),
            shape_of(weights.shape),
        ],
        in_specs=[
            VMEM_SPEC,
            ANY_SPEC,
            ANY_SPEC,
            VMEM_SPEC,
            VMEM_SPEC,
            pl.BlockSpec((DQ, rows), lambda i: (0, lax.axis_index("head"))),
            VMEM_SPEC,
            VMEM_SPEC,
            VMEM_SPEC,
            VMEM_SPEC,
        ],
        out_specs=[VMEM_SPEC] * 5 + [ANY_SPEC],
        scratch_shapes=[
            pltpu.VMEM((shards,) + weights.shape[1:], low),
            pltpu.VMEM((blocks,) + common.shape[1:], low),
            pltpu.VMEM((shards * shard_rows, LANES), jnp.float32),
            pltpu.VMEM((blocks * valid, LANES), jnp.float32),
            LINE,
            pltpu.VMEM((D, D), low),
            pltpu.VMEM((D, FF), low),
            pltpu.VMEM((FF, D), low),
            pltpu.VMEM((D, C), low),
            pltpu.VMEM((DQ, D), low),
            pltpu.VMEM((rows, FF), jnp.float32),
            pltpu.VMEM((rows, FF), low),
            pltpu.SemaphoreType.DMA((3,)),
        ],
        compiler_params=pltpu.CompilerParams(vmem_limit_bytes=56 * MIB),
        name="middle",
    )(counts, weights, common, z_one, o_self, out_queries_t, *marks, gains)


def ending_kernel(
    n_head,
    shard_rows,
    valid,
    rows,
    lengths,
    grads_in,
    d_q_self,
    d_kv_self,
    d_two,
    gains,
    gain_grads,
    query_grad,
    enc_query,
    enc_keyval,
    enc_output,
    self_project,
    z_zero,
    h_zero,
    x_norm_t,
    q_enc,
    kv_enc,
    o_enc,
    z_one,
    h_one,
    grads,
    common_grad,
    held,
    stage,
    stage_common,
    line,
    d_q,
    d_kv,
    sems,
):
    heads = HEADS // n_head
    width = heads * HD
    shards = held.shape[0]
    starts = borders(n_head)
    shared = pltpu.make_async_copy(grads_in.at[pl.ds(shards - 1, 1)], held.at[pl.ds(shards - 1, 1)], sems.at[0])
    shared.start()
    d_projected = [jnp.concatenate([d_q_self[g], d_kv_self[g]], 1) for g in range(n_head)]
    whole = jnp.concatenate(d_projected, 1)
    d_middle, gain_one_grad = norm_pullback(
        z_one[...], gains[1:2, :], against(whole, self_project[...])
    )
    d_one = d_two[...] + d_middle
    d_one_low = d_one.astype(low)
    d_o = against(d_one_low, enc_output[...]).astype(low)
    for g in range(n_head):
        keys = kv_enc[:, 2 * g * width : (2 * g + 1) * width]
        values = kv_enc[:, (2 * g + 1) * width : (2 * g + 2) * width]
        d_key = jnp.zeros(keys.shape, jnp.float32)
        d_value = jnp.zeros(keys.shape, jnp.float32)
        d_query = jnp.zeros((rows, width), jnp.float32)
        for (here, q_head), (unused, do_head) in zip(
            head_lanes(g, heads, q_enc[...]), head_lanes(g, heads, d_o)
        ):
            scores = enc_scores(keys, q_head)
            probs = jnp.exp(scores - jnp.max(scores, 0, keepdims=True))
            probs = probs / jnp.sum(probs, 0, keepdims=True)
            d_probs = against(values, do_head)
            delta = jnp.sum(probs * d_probs, 0, keepdims=True)
            d_scores = (probs * (d_probs - delta)).astype(low)
            d_value = d_value + product(probs.astype(low), do_head)
            d_key = d_key + product(d_scores, q_head)
            d_query = jnp.where(here, contract_first(d_scores, keys), d_query)
        d_q[:, g * width : (g + 1) * width] = (d_query * HD ** (-0.5)).astype(low)
        d_kv[:, 2 * g * width : (2 * g + 1) * width] = (d_key * HD ** (-0.5)).astype(low)
        d_kv[:, (2 * g + 1) * width : (2 * g + 2) * width] = d_value.astype(low)
    d_middle, gain_zero_grad = norm_pullback(
        z_zero[...], gains[0:1, :], against(d_q[...], enc_query[...])
    )
    d_zero = d_one + d_middle
    d_zero_top = d_zero.astype(low)
    d_zero_rest = (d_zero - d_zero_top.astype(jnp.float32)).astype(low)
    picked = picked_rows(clip_bounds(lengths), rows, n_head)
    latent_grad = contract_first(picked, d_zero_top) + contract_first(picked, d_zero_rest)
    query_rows = query_grad.shape[0]
    stage_common[:query_rows] = query_grad[...]
    matrix_into(stage_common, query_rows, latent_grad, line)
    all_gains = jnp.concatenate([gain_zero_grad, gain_one_grad, gain_grads[...]], 0)
    matrix_into(stage_common, query_rows + LAT * D // LANES, all_gains, line)
    piece = common_grad.shape[2]
    for b in range(common_grad.shape[0]):
        for k in range(common_grad.shape[1]):
            amount = min(piece, valid - k * piece)
            block = stage_common[b * valid + k * piece : b * valid + k * piece + amount, :]
            if amount < piece:
                block = jnp.concatenate([block, jnp.zeros((piece - amount, LANES), jnp.float32)], 0)
            common_grad[b, k] = block.astype(low)
    shared.wait()
    kept = shards * shard_rows - starts[4]
    for g in range(n_head):
        results = (
            contract_first(h_zero[...], d_q[:, g * width : (g + 1) * width]),
            product(x_norm_t[...], d_kv[:, 2 * g * width : (2 * g + 2) * width]),
            contract_first(o_enc[:, g * width : (g + 1) * width], d_one_low),
            contract_first(h_one[...], d_projected[g]),
        )
        if kept:
            stage[pl.ds((shards - 1) * shard_rows, shard_rows), :] = held[
                shards - 1, g, :shard_rows, :
            ].astype(jnp.float32)
        for m, result in zip((0, 1, 2, 3), results):
            matrix_into(stage, starts[m], result, line)
        for b in range(shards):
            held[b, g, :shard_rows, :] = stage[pl.ds(b * shard_rows, shard_rows), :].astype(low)
    back = pltpu.make_async_copy(held, grads.at[pl.ds(0, shards)], sems.at[1])
    back.start()
    back.wait()


def ending(lengths, grads, d_self, d_two, gains, gain_grads, query_grad, kept, common_shape, valid, shard_rows):
    rows = d_two.shape[0]
    n_head = grads.shape[1]
    begin, shards = shards_of(n_head, shard_rows, 0, 4)
    keys = kept[6].shape[1]
    common_rows = (DQ + LAT + 4) * D // LANES
    return pl.pallas_call(
        functools.partial(ending_kernel, n_head, shard_rows, valid, rows),
        out_shape=[shape_of(grads.shape), shape_of(common_shape)],
        in_specs=[SMEM_SPEC, ANY_SPEC] + [VMEM_SPEC] * 18,
        out_specs=[ANY_SPEC, VMEM_SPEC],
        input_output_aliases={1: 0},
        scratch_shapes=[
            pltpu.VMEM((shards,) + grads.shape[1:], low),
            pltpu.VMEM((shards * shard_rows, LANES), jnp.float32),
            pltpu.VMEM((common_rows, LANES), jnp.float32),
            LINE,
            pltpu.VMEM((rows, D), low),
            pltpu.VMEM((keys, 2 * D), low),
            pltpu.SemaphoreType.DMA((2,)),
        ],
        compiler_params=pltpu.CompilerParams(vmem_limit_bytes=56 * MIB),
        name="ending",
    )(lengths, grads, *d_self, d_two, gains, gain_grads, query_grad, *kept)


def adam_step(weight, first, second, grad):
    first = beta_one * first + (1 - beta_one) * grad
    second = beta_two * second + (1 - beta_two) * grad * grad
    fixed_first = first / (1 - beta_one**STEP)
    fixed_second = second / (1 - beta_two**STEP)
    weight = weight - learn_rate * (
        fixed_first / (jnp.sqrt(fixed_second) + adam_eps) + weight_decay * weight
    )
    return (weight, first, second, weight.astype(low))


def per_device(
    inputs,
    out_queries,
    clip_lengths,
    labels,
    modality,
    labeled,
    head_params,
    head_first,
    head_second,
    common_params,
    common_first,
    common_second,
):
    n_head, n_blk = lax.axis_size("head"), lax.axis_size("blk")
    dims = grid_of(n_blk, n_head)
    rows = labels.shape[0] // n_head
    heads_here = HEADS // n_head
    n_h, n_c = head_params.shape[0], common_params.shape[0]
    shard_rows, common_rows = n_h // LANES, -(-n_c // LANES)
    head_rows = round_up(shard_rows + 1, TILE)
    piece_rows = round_up(-(-common_rows // n_head), TILE)
    marks = [x.reshape(-1, LANES) for x in (labels, modality, labeled)]
    head_wide = head_params.reshape(shard_rows, LANES)
    common_wide = jnp.pad(common_params, (0, common_rows * LANES - n_c)).reshape(common_rows, LANES)
    weights, common = gather_all(dims, marks, (head_wide, common_wide), (head_rows, piece_rows), 0)
    valid = common_rows
    if n_c % LANES:
        common = common.reshape(n_blk, -1)[:, :n_c].reshape(-1, LANES)
        valid = common.shape[0]
        common = jnp.pad(common, ((0, -valid % TILE), (0, 0)))[None, None]

    encoded = encode(clip_lengths, weights, common, inputs.T, valid, rows, n_head, shard_rows)
    gains, z_one, counts = encoded[4], encoded[11], encoded[15]
    o_self, lse_self, out_self_t, q_all, kv_all = attend(
        dims, clip_lengths, encoded[13], encoded[14], heads_here, 1
    )
    dout, d_two, tile, query_grad, gain_grads, grads = middle(
        counts, weights, common, z_one, o_self, out_queries.T, marks, gains, valid, n_head, shard_rows
    )
    d_self = attend_back(dims, clip_lengths, q_all, kv_all, dout, out_self_t, lse_self, heads_here, 2)
    kept = encoded[:4] + encoded[5:13]
    grads, common_grad = ending(
        clip_lengths,
        grads,
        d_self,
        d_two,
        gains,
        gain_grads,
        query_grad,
        kept,
        common.shape,
        valid,
        shard_rows,
    )
    if n_c % LANES:
        common_grad = common_grad[0, 0, :valid].reshape(n_blk, n_c)
        common_grad = jnp.pad(common_grad, ((0, 0), (0, n_head * piece_rows * LANES - n_c)))
        common_grad = common_grad.reshape(n_blk, n_head, piece_rows, LANES)
    head_share, common_share, totals = reduce_all(
        dims, (grads, common_grad), (shard_rows, common_rows), tile, 3
    )
    label_counts, loss_sums = counts[0, :MODES], totals[0, :MODES]
    clip_norm = jnp.sqrt(totals[0, MODES])
    factor = jnp.minimum(1.0, clip_limit / clip_norm)
    head_share, common_share = head_share.reshape(-1), common_share.reshape(-1)[:n_c]
    head_out = adam_step(head_params, head_first, head_second, head_share * factor)
    common_out = adam_step(common_params, common_first, common_second, common_share * factor)
    return head_out + common_out + (loss_sums, label_counts, clip_norm)


def solution(mesh):
    placed = (
        P("blk", None),
        P("blk", None),
        P(),
        P("blk"),
        P("blk"),
        P("blk"),
        P(("head", "blk")),
        P(("head", "blk")),
        P(("head", "blk")),
        P("blk"),
        P("blk"),
        P("blk"),
    )
    return jax.shard_map(
        per_device,
        mesh=mesh,
        in_specs=placed,
        out_specs=(
            P(("head", "blk")),
            P(("head", "blk")),
            P(("head", "blk")),
            P(("head", "blk")),
            P("blk"),
            P("blk"),
            P("blk"),
            P("blk"),
            P(),
            P(),
            P(),
        ),
        check_vma=False,
    )
```

profile of v0, /device:TPU:0, one launch (start us, length us, event | category | flops | bytes accessed | tf_op | source)
XLA Modules:
  0.0 324.5 jit_solution(3573456028269332528)
XLA Ops:
  0.6 53.6 %gather_weights.1 = (bf16[8,4,1168,128]{3,2,1,0:T(8,128)(2,1)}, bf16[8,4,240,128]{3,2,1,0:T(8,128)(2,1)}) custom-call(s32[8,128]{1,0:T(8,128)} %bitcast.30, s32[8,128]{1,0:T(8,128)} %bitcast.32, s32[8,128]{1,0:T(8,128)} %bitcast.34, f32[1160,128]{1,0:T(8,128)} %bitcast.26, f32[907,128]{1,0:T(8,128)} %bitcast.28), custom_call_target="tpu_custom_call" | custom-call | tf_op jit(solution)/shard_map/gather_weights/pallas_call | solution.py:284
  54.2 11.1 %encode.1 = (bf16[512,512]{1,0:T(8,128)(2,1)}, bf16[704,1024]{1,0:T(8,128)(2,1)}, bf16[512,512]{1,0:T(8,128)(2,1)}, bf16[512,1536]{1,0:T(8,128)(2,1)}, f32[4,512...) custom-call(s32[6]{0:T(128)} %lengths.7, ...), custom_call_target="tpu_custom_call" | custom-call | tf_op jit(solution)/shard_map/encode/pallas_call | solution.py:1263
  65.4 73.2 %attend.1 = (bf16[4,256,128]{2,1,0:T(8,128)(2,1)}, f32[2,1024]{1,0:T(2,128)}, f32[128,1024]{1,0:T(8,128)}, bf16[4,256,128]{2,1,0:T(8,128)(2,1)}, bf16[8,4,256,256]{3,2,1,0:T(8,128)(2,1)}) custom-call(s32[6]{0:T(128)} %lengths.7, bf16[4,256,128]{2,1,0:T(8,128)(2,1)} %get-tuple-element.51.q_in, bf16[4,256,256]{2,1,0:T(8,128)(2,1)} %get-tuple-element.52.kv_in), custom_call_target="tpu_custom_call" | custom-call | tf_op jit(solution)/shard_map/attend/pallas_call | solution.py:749
  138.6 18.1 %middle.1 = (bf16[4,256,128]{2,1,0:T(8,128)(2,1)}, f32[256,512]{1,0:T(8,128)}, f32[8,128]{1,0:T(8,128)}, f32[4104,128]{1,0:T(8,128)}, f32[2,512]{1,0:T(2,128)}, /*index=5*/bf16[8,4,1168,128]{3,2,1,0:T(8,128)(2,1)}) custom-call(f32[8,128]{1,0:T(8,128)} %get-tuple-element.49.counts, bf16[8,4,1168,128]{3,2,1,0:T(8,128)(2,1)} %get-tuple-element.47.weights, ...), custom_call_target="tpu_custom_call" | custom-call | tf_op jit(solution)/shard_map/middle/pallas_call | solution.py:1438
  156.8 76.3 %attend_back.1 = (bf16[4,256,128]{2,1,0:T(8,128)(2,1)}, bf16[4,256,256]{2,1,0:T(8,128)(2,1)}) custom-call(s32[6]{0:T(128)} %lengths.7, bf16[4,256,128]{2,1,0:T(8,128)(2,1)} %get-tuple-element.56.q_all, bf16[8,4,256,256]{3,2,1,0:T(8,128)(2,1)} %get-tuple-element.57.kv_all, bf16[4,256,128]{2,1,0:T(8,128)(2,1)} %get-tuple-element.58.do_in, ...), custom_call_target="tpu_custom_call" | custom-call | tf_op jit(solution)/shard_map/attend_back/pallas_call | solution.py:948
  233.1 17.7 %ending.1 = (bf16[8,4,1168,128]{3,2,1,0:T(8,128)(2,1)}, bf16[8,4,240,128]{3,2,1,0:T(8,128)(2,1)}) custom-call(s32[6]{0:T(128)} %lengths.7, bf16[8,4,1168,128]{3,2,1,0:T(8,128)(2,1)} %get-tuple-element.55.grads_in, bf16[4,256,128]{2,1,0:T(8,128)(2,1)} %get-tuple-element.61.d_q_self, ...), custom_call_target="tpu_custom_call", output_to_operand_aliasing={{0}: (1, {})} | custom-call | tf_op jit(solution)/shard_map/ending/pallas_call | solution.py:1601
  250.8 0.0 copy-start
  250.8 0.0 copy-start.2
  250.8 0.0 copy-start.3
  250.8 64.5 %reduce_gradients.1 = (f32[1160,128]{1,0:T(8,128)}, f32[907,128]{1,0:T(8,128)}, f32[8,128]{1,0:T(8,128)}) custom-call(bf16[8,4,1168,128]{3,2,1,0:T(8,128)(2,1)} %get-tuple-element.77.refs_0_, bf16[8,4,240,128]{3,2,1,0:T(8,128)(2,1)} %get-tuple-element.78.refs_1_, f32[8,128]{1,0:T(8,128)} %get-tuple-element.79.refs_2_), custom_call_target="tpu_custom_call" | custom-call | tf_op jit(solution)/shard_map/reduce_gradients/pallas_call | solution.py:469
  315.4 1.3 slice.9
  317.4 1.2 slice_bitcast_fusion
  318.6 0.0 copy-done
  318.6 0.0 copy-done.2
  318.6 0.0 copy-done.3
  318.6 0.0 copy-start.1
  318.6 0.0 copy-start.4
  318.6 0.0 copy-start.5
  318.6 0.0 copy-start.6
  318.7 2.8 fusion.7
  321.5 0.0 copy-done.1
  321.5 0.0 copy-done.4
  321.5 0.0 copy-done.5
  321.5 0.0 copy-done.6
  321.5 1.4 fusion.4
Async XLA Ops:
  250.8 67.8 %copy-start = (f32[148480]{0:T(1024)S(1)}, f32[148480]{0:T(1024)}, u32[]{:S(2)}) copy-start(f32[148480]{0:T(1024)} %param.18) | copy-start | bytes 1781764
  250.8 67.8 %copy-start.2 = (f32[148480]{0:T(1024)S(1)}, f32[148480]{0:T(1024)}, u32[]{:S(2)}) copy-start(f32[148480]{0:T(1024)} %param.19) | copy-start | bytes 1781764
  250.8 67.8 %copy-start.3 = (f32[148480]{0:T(1024)S(1)}, f32[148480]{0:T(1024)}, u32[]{:S(2)}) copy-start(f32[148480]{0:T(1024)} %param.20) | copy-start | bytes 1781764
  318.6 2.9 copy-start.1
  318.6 2.9 copy-start.4
  318.6 2.8 copy-start.5
  318.6 2.8 copy-start.6
where the time goes:
time: 330 us; the launch traced here: 324 us
  Pallas kernels  315 us (95%)
  other arithmetic  4.21 us (1%)
    pallas_call x1, Pallas kernels, attend_back(): pl.pallas_call(functools.partial(attend_back_kernel, dims, heads, 256), o...  76.3 us
    pallas_call x1, Pallas kernels, attend(): pl.pallas_call(functools.partial(attend_kernel, dims, heads, 256, 256), o...  73.2 us
    pallas_call x1, Pallas kernels, reduce_all(): pl.pallas_call(functools.partial(reduce_kernel, dims, parts), out_shape=[...  64.5 us
    pallas_call x1, Pallas kernels, gather_all(): pl.pallas_call(functools.partial(gather_kernel, dims, parts), out_shape=[...  53.6 us
    pallas_call x1, Pallas kernels, middle(): pl.pallas_call(functools.partial(middle_kernel, n_head, shard_rows, valid...  18.1 us
    pallas_call x1, Pallas kernels, ending(): pl.pallas_call(functools.partial(ending_kernel, n_head, shard_rows, valid...  17.7 us
    pallas_call x1, Pallas kernels, encode(): pl.pallas_call(functools.partial(encode_kernel, n_head, shard_rows, valid...  11.1 us

commit v1 on v0

--- a/solution.py
+++ b/solution.py
@@ -110,7 +110,7 @@
 RING = 0
 
 
-def in_order(first, follow, size_of, ahead, result):
+def in_order(first, follow, size_of, result):
     queues, busy, flight = {}, {}, {}
     now = 0.0
 
@@ -122,20 +122,20 @@
     while True:
         for axis in sorted(queues):
             queue, going = queues[axis], flight.setdefault(axis, [])
-            while queue and (not going or busy[axis] < now + ahead):
+            while queue and (not going or busy[axis] < now + AHEAD):
                 message = min(queue)
                 queue.remove(message)
                 busy[axis] = max(now, busy.get(axis, 0.0)) + size_of(message)
                 going.append((busy[axis] + 1.5, message))
-                result.append((True, message))
+                result.append((now, True, message))
         arrivals = [min(going) for going in flight.values() if going]
         if not arrivals:
-            return now
+            return
         arrival = min(arrivals)
         flight[arrival[1][1]].remove(arrival)
         now = max(now, arrival[0])
-        result.append((False, arrival[1]))
-        ready(follow(arrival[1]))
+        result.append((now, False, arrival[1]))
+        ready(follow(arrival[1], now))
 
 
 def time_of(rows, axis):
@@ -146,30 +146,150 @@
     return offset[:axis] + (d,) + offset[axis + 1 :]
 
 
-def gather_order(dims, parts):
-    def onward(p, offset, position):
-        order = parts[p][3]
-        result = []
-        for k in range(max(position, 0), 4):
-            axis = order[k]
-            n = dims[axis]
-            if k > position:
-                steps = [1] if axis == RING else range(1, n)
-                steps = [d for d in steps if d < n]
+def all_offsets(dims, axes):
+    offsets = [(0, 0, 0, 0)]
+    for a in axes:
+        offsets = [with_at(o, a, d) for o in offsets for d in range(dims[a])]
+    return offsets
+
+
+def cut(array, rows, planes, orders):
+    result = []
+    first = 0
+    for n, order in enumerate(orders):
+        end = rows * (n + 1) // len(orders) // TILE * TILE if n + 1 < len(orders) else rows
+        result.append((array, first, end - first, planes, order))
+        first = end
+    return tuple(result)
+
+
+class Copies:
+    def __init__(self, dims, me, send_sem, recv_sem):
+        self.dims, self.me, self.send_sem, self.recv_sem = dims, me, send_sem, recv_sem
+        self.made, self.always, self.maybe = 0, [], []
+
+    def make(self, src, dst, offset):
+        i = self.made
+        self.made += 1
+        place = shifted(self.dims, self.me, offset, 1)
+        return remote(src, dst, self.send_sem.at[i], self.recv_sem.at[i], place, self.dims)
+
+    def again(self, i, src, dst, offset):
+        place = shifted(self.dims, self.me, offset, 1)
+        return remote(src, dst, self.send_sem.at[i], self.recv_sem.at[i], place, self.dims)
+
+    def __call__(self, src, dst, offset):
+        copy = self.make(src, dst, offset)
+        copy.start()
+        self.always.append(copy)
+        return copy
+
+    def finish(self):
+        for copy in self.always:
+            copy.wait_send()
+        for condition, copy in self.maybe:
+            pl.when(condition)(copy.wait_send)
+
+
+class InSteps:
+    def __init__(self, events, stretch):
+        self.events, self.stretch, self.at = events, stretch, 0
+
+    def step(self, when):
+        while self.at < len(self.events) and self.events[self.at][0] * self.stretch <= when:
+            unused, kind, what = self.events[self.at]
+            self.at += 1
+            if kind is None:
+                self.add(*what)
+            elif kind:
+                self.send(what)
             else:
-                steps = [offset[axis] + 1] if axis == RING and offset[axis] + 1 < n else []
-            for d in steps:
-                result.append(((k, sum(offset), p), axis, p, with_at(offset, axis, d)))
-        return result
-
-    def follow(message):
-        rank, axis, p, offset = message
-        return onward(p, offset, rank[0])
-
-    first = [m for p in range(len(parts)) for m in onward(p, (0, 0, 0, 0), -1)]
-    result = []
-    now = in_order(first, follow, lambda m: time_of(parts[m[2]][2], m[1]), AHEAD, result)
-    return result, now
+                self.arrive(what)
+
+    def rest(self):
+        self.step(float("inf"))
+
+
+class Gather(InSteps):
+    def __init__(self, dims, parts, copies, outs, stretch=1.0):
+        self.dims, self.parts, self.copies, self.outs = dims, parts, copies, outs
+        self.flying = {}
+        events = []
+
+        def onward(p, plane, offset, position):
+            order = parts[p][4]
+            return [
+                ((k, -plane, p, offset), axis, p, plane, with_at(offset, axis, d))
+                for k, axis in enumerate(order)
+                if k > position
+                for d in range(1, dims[axis])
+            ]
+
+        def follow(message, now):
+            rank, axis, p, plane, offset = message
+            return onward(p, plane, offset, rank[0])
+
+        first = [
+            ((-1, -plane, p), 0, p, plane, (0, 0, 0, 0))
+            for p, part in enumerate(parts)
+            for plane in part[3]
+        ]
+        in_order(first, follow, lambda m: time_of(parts[m[2]][2], m[1]), events)
+        super().__init__(events, stretch)
+
+    def block(self, p, plane, offset):
+        array, first, rows, planes, order = self.parts[p]
+        place = (plane,) + shifted(self.dims, self.copies.me, offset, -1)[1:]
+        at = (blk_of(self.dims, place), head_of(self.dims, place), pl.ds(first, rows))
+        return self.outs[array].at[at]
+
+    def send(self, message):
+        rank, axis, p, plane, offset = message
+        z, planes = self.copies.me[0], self.dims[0]
+        if axis:
+            block = self.block(p, plane, with_at(offset, axis, 0))
+            self.flying[message[1:]] = self.copies(block, block, along(axis, offset[axis]))
+            return
+        block = self.block(p, plane, offset)
+        up = self.copies.make(block, block, along(0, 1))
+        down = self.copies.make(block, block, along(0, planes - 1))
+        self.flying[message[1:]] = (up, down)
+        for copy, there, here in ((up, z < planes - 1, z >= plane), (down, z > 0, z <= plane)):
+            self.copies.maybe.append((there & here, copy))
+            pl.when((z == plane) & there)(copy.start)
+
+    def arrive(self, message):
+        rank, axis, p, plane, offset = message
+        flying = self.flying[message[1:]]
+        if axis:
+            flying.wait_recv()
+            return
+        up, down = flying
+        z, planes = self.copies.me[0], self.dims[0]
+
+        @pl.when(z > plane)
+        def from_below():
+            up.wait_recv()
+            pl.when(z < planes - 1)(up.start)
+
+        @pl.when(z < plane)
+        def from_above():
+            down.wait_recv()
+            pl.when(z > 0)(down.start)
+
+
+def gather_copies(dims, parts):
+    z, y, x, cores = dims
+    return sum(len(part[3]) * (y * x * cores - 1 + 2) for part in parts)
+
+
+def lower_planes(dims, n_head, shard_rows):
+    first, shards = shards_of(n_head, shard_rows, 0, 4)
+    return -(-shards // dims[1])
+
+
+YXC, XYC = (1, 2, 3), (2, 1, 3)
+CXY, CYX = (3, 2, 1), (3, 1, 2)
 
 
 def gather_kernel(
@@ -190,68 +310,35 @@
     own_sem,
 ):
     me = my_place(dims)
-    my_head = head_of(dims, me)
-    n_head = dims[2] * dims[3]
+    my_blk, my_head = blk_of(dims, me), head_of(dims, me)
     shard_rows, common_rows = head_params.shape[0], common_params.shape[0]
-    per_head = labels.shape[0] // n_head
-    row = lax.broadcasted_iota(jnp.int32, labels.shape, 0)
-    mine = (row >= my_head * per_head) & (row < (my_head + 1) * per_head) & (labeled[...] == 1)
-    lane = lax.broadcasted_iota(jnp.int32, (1, LANES), 1)
-    counts = jnp.zeros((1, LANES), jnp.float32)
-    for m in range(MODES):
-        member = jnp.where(mine & (modality[...] == m), 1.0, 0.0)
-        counts = counts + jnp.where(lane == m, jnp.sum(member, (0, 1), keepdims=True), 0.0)
-    padding = head_low.shape[0] - shard_rows
     tail = shard_rows // TILE * TILE
     head_low[:tail] = head_params[:tail].astype(low)
-    last = [jnp.broadcast_to(counts, (padding, LANES))]
+    padding = jnp.zeros((head_low.shape[0] - shard_rows, LANES), jnp.float32)
     if shard_rows > tail:
-        last = [head_params[tail:]] + last
-    head_low[tail:] = jnp.concatenate(last, 0).astype(low)
+        padding = jnp.concatenate([head_params[tail:], padding], 0)
+    head_low[tail:] = padding.astype(low)
+    own_head = pltpu.make_async_copy(head_low, head_all.at[my_blk, my_head], own_sem.at[0])
+    own_head.start()
+    lane = lax.broadcasted_iota(jnp.int32, (1, LANES), 1)
+    counts = jnp.zeros(labels.shape, jnp.float32)
+    for m in range(MODES):
+        member = jnp.where((labeled[...] == 1) & (modality[...] == m), 1.0, 0.0)
+        counts = counts + jnp.where(lane == m, jnp.sum(member, 1, keepdims=True), 0.0)
     common_wide[...] = jnp.zeros(common_wide.shape, jnp.float32)
     common_wide[:common_rows] = common_params[...]
+    common_wide[common_rows : common_rows + labels.shape[0]] = counts
     piece = common_low.shape[0]
     common_low[...] = common_wide[pl.ds(pl.multiple_of(my_head * piece, TILE), piece)].astype(low)
-
+    own_common = pltpu.make_async_copy(common_low, common_all.at[my_blk, my_head], own_sem.at[1])
+    own_common.start()
+    copies = Copies(dims, me, send_sem, recv_sem)
     greet(dims, me, ring_and_others(dims))
-    srcs, outs = (head_low, common_low), (head_all, common_all)
-    copies = {}
-
-    def block(p, offset):
-        place = shifted(dims, me, offset, -1)
-        array, first, rows, order = parts[p]
-        return outs[array].at[blk_of(dims, place), head_of(dims, place), pl.ds(first, rows)]
-
-    own = []
-    for is_send, (rank, axis, p, offset) in gather_order(dims, parts)[0]:
-        if is_send:
-            step = 1 if axis == RING else offset[axis]
-            before = with_at(offset, axis, offset[axis] - step)
-            array, first, rows, order = parts[p]
-            source = block(p, before) if any(before) else srcs[array].at[pl.ds(first, rows)]
-            i = len(copies)
-            copies[(p, offset)] = remote(
-                source,
-                block(p, before),
-                send_sem.at[i],
-                recv_sem.at[i],
-                shifted(dims, me, along(axis, step), 1),
-                dims,
-            )
-            copies[(p, offset)].start()
-        else:
-            if not own:
-                for array in range(2):
-                    copy = pltpu.make_async_copy(
-                        srcs[array], outs[array].at[blk_of(dims, me), my_head], own_sem.at[array]
-                    )
-                    copy.start()
-                    own.append(copy)
-            copies[(p, offset)].wait_recv()
-    for copy in copies.values():
-        copy.wait_send()
-    for copy in own:
-        copy.wait()
+    own_head.wait()
+    own_common.wait()
+    gather = Gather(dims, parts, copies, (head_all, common_all))
+    gather.rest()
+    copies.finish()
 
 
 def ring_and_others(dims):
@@ -259,28 +346,11 @@
     return sorted(ring - {(0, 0, 0, 0)}) + axis_peers(dims, (1, 2, 3))
 
 
-def cut(array, rows, shares):
-    result = []
-    first, so_far = 0, 0
-    whole = sum(share for share, order in shares)
-    for share, order in shares:
-        so_far += share
-        end = rows * so_far // whole // TILE * TILE if so_far < whole else rows
-        if end > first:
-            result.append((array, first, end - first, order))
-        first = end
-    return tuple(result)
-
-
-ZYXC, ZXYC, YXZC, XYZC = (0, 1, 2, 3), (0, 2, 1, 3), (1, 2, 0, 3), (2, 1, 0, 3)
-GATHER_SHARES = ((8, ZYXC), (6, ZXYC), (2, YXZC), (2, XYZC))
-REDUCE_SHARES = ((7, ZYXC), (7, ZXYC), (2, YXZC), (2, XYZC))
-
-
-def gather_all(dims, marks, params, rows, collective_id):
+def gather_all(dims, marks, params, rows, lower, collective_id):
     z, y, x, cores = dims
-    parts = cut(0, rows[0], GATHER_SHARES) + cut(1, rows[1], ((1, ZXYC),))
-    count = len(parts) * (z * y * x * cores - 1)
+    parts = cut(0, rows[0], range(lower), (YXC, XYC, YXC, XYC))
+    parts = parts + cut(1, rows[1], range(z), (XYC,))
+    count = gather_copies(dims, parts)
     return pl.pallas_call(
         functools.partial(gather_kernel, dims, parts),
         out_shape=[shape_of((z * y, x * cores, n, LANES)) for n in rows],
@@ -293,136 +363,208 @@
             pltpu.SemaphoreType.DMA((count,)),
             pltpu.SemaphoreType.DMA((2,)),
         ],
-        compiler_params=pltpu.CompilerParams(collective_id=collective_id, has_side_effects=True),
+        compiler_params=pltpu.CompilerParams(
+            collective_id=collective_id, has_side_effects=True, vmem_limit_bytes=56 * MIB
+        ),
         name="gather_weights",
     )(*marks, *params)
 
 
-def reduce_order(dims, parts):
-    ready, arrived, order = set(), set(), []
-
-    def message(p, position, offset):
-        z = offset[RING]
-        rank = (dims[RING] - z if z else dims[RING], position, tuple(-o for o in offset), p)
-        return (rank, parts[p][3][position], p, position, offset)
-
-    def done(p, position, offset):
-        ready.add((p, position, offset))
-        if position == 4:
-            return []
-        axis = parts[p][3][position]
-        d = offset[axis]
-        first = d != 0 and (axis != RING or d == dims[axis] - 1)
-        return ([message(p, position, offset)] if first else []) + advance(p, position, offset)
-
-    def advance(p, position, offset):
-        axis = parts[p][3][position]
-        n = dims[axis]
-        start = with_at(offset, axis, 0)
-        if axis == RING:
-            here = (p, position, offset)
-            if here in ready and here in arrived:
-                order.append((None, here))
-                if offset[axis]:
-                    return [message(p, position, offset)]
-                return done(p, position + 1, offset)
-        elif (p, position, start) in ready and (p, position + 1, start) not in ready:
-            if all((p, position, with_at(start, axis, d)) in arrived for d in range(1, n)):
-                order.append((None, (p, position, start)))
-                return done(p, position + 1, start)
-        return []
-
-    def follow(sent):
-        rank, axis, p, position, offset = sent
-        here = with_at(offset, axis, offset[axis] - 1) if axis == RING else offset
-        arrived.add((p, position, here))
-        return advance(p, position, here)
-
-    first = []
-    for p in range(len(parts)):
-        for offset in all_offsets(dims, range(4)):
-            first += done(p, 0, offset)
-    now = in_order(first, follow, lambda m: time_of(parts[m[2]][2], m[1]), AHEAD, order)
-    return order, now
-
-
-def all_offsets(dims, axes):
-    offsets = [(0, 0, 0, 0)]
-    for a in axes:
-        offsets = [with_at(o, a, d) for o in offsets for d in range(dims[a])]
-    return offsets
+def row_chunk(rows):
+    for count in (4, 3, 2):
+        if rows % (count * TILE) == 0:
+            return rows // count
+    return rows
+
+
+class Reduce(InSteps):
+    def __init__(self, dims, parts, copies, srcs, buffers, outs, kept=None, stretch=1.0):
+        self.dims, self.parts, self.copies, self.srcs, self.outs, self.kept = dims, parts, copies, srcs, outs, kept
+        self.buffers, self.flying = {}, {}
+        buffers = list(buffers)
+        for p, part in enumerate(parts):
+            for position in range(len(part[4])):
+                self.buffers[(p, position)] = buffers.pop(0)
+            if outs is not None:
+                self.buffers[(p, 3)] = buffers.pop(0)
+        ready, arrived, events = set(), set(), []
+
+        def message(p, position, plane, offset):
+            return ((position, plane, tuple(-o for o in offset), p), parts[p][4][position], p, position, plane, offset)
+
+        def done(p, position, plane, offset, now):
+            ready.add((p, position, plane, offset))
+            order = parts[p][4]
+            if position == len(order):
+                return chain(p, plane, 1) if outs is not None else []
+            first = offset[order[position]] != 0
+            sent = [message(p, position, plane, offset)] if first else []
+            return sent + advance(p, position, plane, offset, now)
+
+        def chain(p, plane, k):
+            return [((3, k, plane, p), 0, p, 3, plane, k)]
+
+        def advance(p, position, plane, offset, now):
+            axis = parts[p][4][position]
+            start = with_at(offset, axis, 0)
+            if (p, position, plane, start) not in ready or (p, position + 1, plane, start) in ready:
+                return []
+            for d in range(1, dims[axis]):
+                if (p, position, plane, with_at(start, axis, d)) not in arrived:
+                    return []
+            events.append((now, None, (p, position, plane, start)))
+            return done(p, position + 1, plane, start, now)
+
+        def follow(sent, now):
+            rank, axis, p, position, plane, offset = sent
+            if position == 3:
+                if offset < dims[0] - 1:
+                    return chain(p, plane, offset + 1)
+                events.append((now, None, (p, 3, plane, None)))
+                return []
+            arrived.add((p, position, plane, offset))
+            return advance(p, position, plane, offset, now)
+
+        first = []
+        for p, part in enumerate(parts):
+            for plane in part[3]:
+                for offset in all_offsets(dims, part[4]):
+                    first += done(p, 0, plane, offset, 0.0)
+        in_order(first, follow, lambda m: time_of(parts[m[2]][2], m[1]), events)
+        super().__init__(events, stretch)
+
+    @staticmethod
+    def scratch(dims, parts, chained):
+        result = []
+        for array, first, rows, planes, order in parts:
+            for position, axis in enumerate(order):
+                rest = len(all_offsets(dims, order[position + 1 :]))
+                result.append(pltpu.VMEM((len(planes), rest, dims[axis] - 1, rows, LANES), low))
+            if chained:
+                result.append(pltpu.VMEM((len(planes), 2, rows, LANES), low))
+        return result
+
+    @staticmethod
+    def count(dims, parts, chained):
+        z, y, x, cores = dims
+        return sum(
+            len(planes) * ((y * x * cores - 1 if order else 0) + (2 if chained else 0))
+            for array, first, rows, planes, order in parts
+        )
+
+    def slot(self, p, position, plane, offset):
+        planes, order = self.parts[p][3:]
+        axis = order[position]
+        k = all_offsets(self.dims, order[position + 1 :]).index(with_at(offset, axis, 0))
+        return self.buffers[(p, position)].at[plane - planes[0], k, max(offset[axis] - 1, 0)]
+
+    def summed(self, p, position, plane, offset):
+        array, first, rows, planes, order = self.parts[p]
+        if position:
+            return self.slot(p, position - 1, plane, offset)
+        at = plane - planes[0]
+        if not order:
+            return self.srcs[array].at[at, pl.ds(first, rows)]
+        place = shifted(self.dims, self.copies.me, offset, 1)
+        place = (at,) + place[1:]
+        return self.srcs[array].at[blk_of(self.dims, place), head_of(self.dims, place), pl.ds(first, rows)]
+
+    def total(self, p, target, target_first, refs):
+        rows = self.parts[p][2]
+        step = row_chunk(rows)
+
+        @pl.loop(0, rows // step)
+        def some_rows(n):
+            at = pl.ds(pl.multiple_of(n * step, step), step)
+            total = refs[0][at].astype(jnp.float32)
+            for ref in refs[1:]:
+                total = total + ref[at].astype(jnp.float32)
+            there = pl.ds(pl.multiple_of(target_first + n * step, TILE), step)
+            target[there] = total.astype(target.dtype)
+
+    def add(self, p, position, plane, offset):
+        array, first, rows, planes, order = self.parts[p]
+        if position == 3:
+            self.last(p, plane)
+            return
+        axis = order[position]
+        arrivals = [self.slot(p, position, plane, with_at(offset, axis, d)) for d in range(1, self.dims[axis])]
+        refs = [self.summed(p, position, plane, offset)] + arrivals
+        if self.outs is None and position == len(order) - 1:
+            self.total(p, self.kept.at[plane - planes[0]], first, refs)
+        else:
+            self.total(p, arrivals[0], 0, refs)
+
+    def send(self, message):
+        rank, axis, p, position, plane, offset = message
+        if position < 3:
+            source = self.summed(p, position, plane, offset)
+            target = self.slot(p, position, plane, offset)
+            self.flying[message[1:]] = self.copies(source, target, along(axis, offset[axis]))
+            return
+        k, z, planes = offset, self.copies.me[0], self.dims[0]
+        mine = self.summed(p, len(self.parts[p][4]), plane, (0, 0, 0, 0))
+        if k == 1:
+            made = []
+            for side in range(2):
+                number = self.copies.made
+                away = along(0, 1 if side else planes - 1)
+                made.append((number, away, self.copies.make(mine, self.arrived(p, plane, side), away)))
+            self.flying[(p, plane)] = made
+        for side in range(2):
+            number, away, from_mine = self.flying[(p, plane)][side]
+            sender = k - 1 if side else planes - k
+            if not (sender < plane if side else sender > plane):
+                continue
+            arrived = self.arrived(p, plane, side)
+            copy = from_mine if k == 1 else self.copies.again(number, arrived, arrived, away)
+            self.copies.maybe.append((z == sender, copy))
+
+            @pl.when(z == sender)
+            def pass_on():
+                if k > 1:
+                    from_mine.wait_recv()
+                    self.total(p, arrived, 0, [arrived, mine])
+                copy.start()
+
+    def arrived(self, p, plane, side):
+        return self.buffers[(p, 3)].at[plane - self.parts[p][3][0], side]
+
+    def arrive(self, message):
+        if message[3] < 3:
+            self.flying[message[1:]].wait_recv()
+
+    def last(self, p, plane):
+        array, first, rows, planes, order = self.parts[p]
+
+        @pl.when(self.copies.me[0] == plane)
+        def here():
+            refs = [self.summed(p, len(order), plane, (0, 0, 0, 0))]
+            for side in range(2):
+                if plane > 0 if side else plane < self.dims[0] - 1:
+                    self.flying[(p, plane)][side][2].wait_recv()
+                    refs.append(self.arrived(p, plane, side))
+            self.total(p, self.outs[array], first, refs)
 
 
 def reduce_kernel(dims, parts, *refs):
-    srcs, tile = refs[:2], refs[2]
-    head_out, common_out, totals = refs[3:6]
-    places = len(parts) * 4
-    buffers = refs[6 : 6 + places]
-    head_sum, common_sum, shares, send_sem, recv_sem, near_tiles, far_tiles = refs[6 + places :]
-    sums = (head_sum, common_sum)
+    lower, upper, common, tile = refs[:4]
+    head_out, common_out, totals = refs[4:7]
+    places = len(Reduce.scratch(dims, parts, True))
+    buffers = refs[7 : 7 + places]
+    head_sum, common_sum, shares, send_sem, recv_sem, near_tiles, far_tiles = refs[7 + places :]
     me = my_place(dims)
     z, y, x, cores = dims
     across = peers_across(dims)
     others = [o for o in all_offsets(dims, (0, 1)) if any(o)]
     met = ring_and_others(dims)
     greet(dims, me, met + [o for o in across + others if o not in met])
-    push = Pushes(dims, me, send_sem, recv_sem)
-    copies = {}
-
-    def slot(p, position, offset):
-        order = parts[p][3]
-        axis = order[position]
-        rest = [o for o in all_offsets(dims, order[position + 1 :])]
-        k = rest.index(with_at(offset, axis, 0))
-        return buffers[p * 4 + position].at[k, max(offset[axis] - 1, 0)]
-
-    def summed(p, position, offset):
-        array, first, rows, order = parts[p]
-        if position == 0:
-            place = shifted(dims, me, offset, 1)
-            return srcs[array].at[blk_of(dims, place), head_of(dims, place), pl.ds(first, rows)]
-        return slot(p, position - 1, offset)
-
-    def ring_slot(p, position, offset):
-        axis = parts[p][3][position]
-        return slot(p, position, with_at(offset, axis, offset[axis] + 1))
-
-    def add(p, position, offset):
-        array, first, rows, order = parts[p]
-        axis = order[position]
-        if axis == RING:
-            arrivals = [ring_slot(p, position, offset)]
-        else:
-            arrivals = [slot(p, position, with_at(offset, axis, d)) for d in range(1, dims[axis])]
-        mine = summed(p, position, offset)
-        step = row_chunk(rows)
-
-        @pl.loop(0, rows // step)
-        def some_rows(n):
-            at = pl.ds(pl.multiple_of(n * step, step), step)
-            total = mine[at].astype(jnp.float32)
-            for arrival in arrivals:
-                total = total + arrival[at].astype(jnp.float32)
-            if position == 3 and not any(offset):
-                sums[array][pl.ds(pl.multiple_of(first + n * step, TILE), step)] = total
-            else:
-                arrivals[0][at] = total.astype(low)
-
-    for is_send, what in reduce_order(dims, parts)[0]:
-        if is_send is None:
-            add(*what)
-        elif is_send:
-            rank, axis, p, position, offset = what
-            d = offset[axis]
-            started = axis != RING or d == dims[axis] - 1
-            source = summed(p, position, offset) if started else ring_slot(p, position, offset)
-            step = along(axis, 1 if axis == RING else d)
-            copies[what] = push(source, slot(p, position, offset), step)
-        else:
-            copies[what].wait_recv()
+    copies = Copies(dims, me, send_sem, recv_sem)
+    reduction = Reduce(dims, parts, copies, (lower, upper, common), buffers, (head_sum, head_sum, common_sum))
+    reduction.rest()
     my_head, my_blk = head_of(dims, me), blk_of(dims, me)
     shares[my_head] = common_sum[...].astype(low)
-    share_copies = [push(shares.at[my_head], shares.at[my_head], o) for o in across]
+    share_copies = [copies(shares.at[my_head], shares.at[my_head], o) for o in across]
     amount = head_out.shape[0]
     head_out[...] = head_sum[:amount]
     squares = jnp.sum(head_sum[:amount] * head_sum[:amount], 0, keepdims=True)
@@ -431,11 +573,11 @@
     near_tiles[my_head] = tile[...] + jnp.where(
         lane == MODES, jnp.sum(squares, 1, keepdims=True), 0.0
     )
-    near = [push(near_tiles.at[my_head], near_tiles.at[my_head], o) for o in across]
+    near = [copies(near_tiles.at[my_head], near_tiles.at[my_head], o) for o in across]
     for copy in near:
         copy.wait_recv()
     far_tiles[my_blk] = jnp.sum(near_tiles[...], 0)
-    far = [push(far_tiles.at[my_blk], far_tiles.at[my_blk], o) for o in others]
+    far = [copies(far_tiles.at[my_blk], far_tiles.at[my_blk], o) for o in others]
     for copy in share_copies:
         copy.wait_recv()
     piece = shares.shape[1]
@@ -445,27 +587,17 @@
     for copy in far:
         copy.wait_recv()
     totals[...] = jnp.sum(far_tiles[...], 0)
-    push.finish()
-
-
-def row_chunk(rows):
-    for count in (4, 3, 2):
-        if rows % (count * TILE) == 0:
-            return rows // count
-    return rows
-
-
-def reduce_all(dims, arrays, valid, tile, collective_id):
+    copies.finish()
+
+
+def reduce_all(dims, lower_grads, upper_sums, common_grads, valid, tile, collective_id):
     z, y, x, cores = dims
-    rows = [array.shape[2] for array in arrays]
-    parts = cut(0, rows[0], [(share, order[::-1]) for share, order in REDUCE_SHARES])
-    parts = parts + cut(1, rows[1], ((1, ZXYC[::-1]),))
-    scratch = []
-    for array, first, amount, order in parts:
-        for position, axis in enumerate(order):
-            rest = len(all_offsets(dims, order[position + 1 :]))
-            scratch.append(pltpu.VMEM((rest, dims[axis] - 1, amount, LANES), low))
-    count = len(parts) * (z * y * x * cores - 1) + 2 * (x * cores - 1) + z * y - 1
+    lower = lower_grads.shape[0] // y
+    rows = [lower_grads.shape[2], common_grads.shape[2]]
+    parts = cut(1, rows[0], range(lower, z), ((), ()))
+    parts = parts + cut(0, rows[0], range(lower), (CXY, CYX, CXY, CYX))
+    parts = parts + cut(2, rows[1], range(z), (CXY,))
+    count = Reduce.count(dims, parts, True) + 2 * (x * cores - 1) + z * y - 1
     return pl.pallas_call(
         functools.partial(reduce_kernel, dims, parts),
         out_shape=[
@@ -473,9 +605,9 @@
             shape_of((valid[1], LANES), jnp.float32),
             shape_of((8, LANES), jnp.float32),
         ],
-        in_specs=[VMEM_SPEC] * 3,
+        in_specs=[VMEM_SPEC] * 4,
         out_specs=[VMEM_SPEC] * 3,
-        scratch_shapes=scratch
+        scratch_shapes=Reduce.scratch(dims, parts, True)
         + [pltpu.VMEM((n, LANES), jnp.float32) for n in rows]
         + [
             pltpu.VMEM((x * cores, rows[1], LANES), low),
@@ -488,7 +620,7 @@
             collective_id=collective_id, has_side_effects=True, vmem_limit_bytes=60 * MIB
         ),
         name="reduce_gradients",
-    )(*arrays, tile)
+    )(lower_grads, upper_sums, common_grads, tile)
 
 
 def contract_first(a, b):
@@ -611,14 +743,17 @@
     heads,
     key_step,
     query_step,
+    gather_parts,
     lengths,
     q_in,
     kv_in,
+    weights_in,
     o_out,
     lse,
     out_t,
     q_all,
     kv_all,
+    weights,
     keys,
     values_t,
     queries,
@@ -628,6 +763,8 @@
     send_sem,
     recv_sem,
     own_sem,
+    gather_send_sem,
+    gather_recv_sem,
 ):
     z, y, x, cores = dims
     me = my_place(dims)
@@ -644,12 +781,15 @@
     own_q = pltpu.make_async_copy(q_in.at[my_head], q_all.at[my_head], own_sem.at[1])
     own_kv.start()
     own_q.start()
+    gather_copy = Copies(dims, me, gather_send_sem, gather_recv_sem)
+    gather = Gather(dims, gather_parts, gather_copy, (weights,), 1.4)
 
     def to_head(src, dst, o):
         return push(src.at[head_of(dims, shifted(dims, me, o, 1))], dst, o)
 
     kv_copies = {o: to_head(kv_in, kv_all.at[my_blk, my_head], o) for o in across}
     q_copies = [to_head(q_in, q_all.at[my_head], o) for o in across]
+    gather.step(1)
     ring, side = {}, {}
     pieces = [(0, 0, 0, 0)] + across[::-1]
 
@@ -715,17 +855,24 @@
             queries[a, :, h * rows : (h + 1) * rows] = with_query_tail(
                 bounds, a, my_blk * amount + h * rows, q_t[a * HD : (a + 1) * HD], None
             )
+    gather.step(10)
     compute((0, 0, 0, 0))
+    now = 17
     for s in range(1, z + 1):
+        gather.step(now)
         if s < z:
             for n in range(n_head):
                 ring[(s, n)].wait_recv()
                 send_on(s, n)
             compute(along(0, s))
+            now += 7
+            gather.step(now)
         for o in sides:
             for n in range(n_head):
                 side[(s - 1, n, o)].wait_recv()
             compute((s - 1, o[1], 0, 0))
+            now += 7
+    gather.rest()
     for a in range(heads):
         total = accum[a, HD : HD + 1, :]
         out_t[a * HD : (a + 1) * HD, :] = accum[a, :HD, :] / total
@@ -739,24 +886,29 @@
     for copy in o_copies:
         copy.wait_recv()
     push.finish()
-
-
-def attend(dims, lengths, q, kv, heads, collective_id):
+    gather_copy.finish()
+
+
+def attend(dims, lengths, q, kv, weights, lower, heads, collective_id):
     z, y, x, cores = dims
     n_head, rows, width = q.shape
     amount = n_head * rows
     count = 3 * (n_head - 1) + n_head * (z - 1 + z * (y - 1))
+    parts = cut(0, weights.shape[2], range(lower, z), (YXC, YXC))
+    gather_count = gather_copies(dims, parts)
     return pl.pallas_call(
-        functools.partial(attend_kernel, dims, heads, 256, 256),
+        functools.partial(attend_kernel, dims, heads, 256, 256, parts),
         out_shape=(
             jax.ShapeDtypeStruct(q.shape, low),
             jax.ShapeDtypeStruct((heads, amount), jnp.float32),
             jax.ShapeDtypeStruct((width, amount), jnp.float32),
             jax.ShapeDtypeStruct(q.shape, low),
             jax.ShapeDtypeStruct((z * y,) + kv.shape, low),
+            jax.ShapeDtypeStruct(weights.shape, low),
         ),
-        in_specs=[SMEM_SPEC, VMEM_SPEC, VMEM_SPEC],
-        out_specs=[VMEM_SPEC] * 5,
+        in_specs=[SMEM_SPEC, VMEM_SPEC, VMEM_SPEC, ANY_SPEC],
+        out_specs=[VMEM_SPEC] * 5 + [ANY_SPEC],
+        input_output_aliases={3: 5},
         scratch_shapes=[
             pltpu.VMEM((heads, amount, LANES), low),
             pltpu.VMEM((heads, HD + TILE, amount), low),
@@ -767,26 +919,31 @@
             pltpu.SemaphoreType.DMA((count,)),
             pltpu.SemaphoreType.DMA((count,)),
             pltpu.SemaphoreType.DMA((3,)),
+            pltpu.SemaphoreType.DMA((gather_count,)),
+            pltpu.SemaphoreType.DMA((gather_count,)),
         ],
         compiler_params=pltpu.CompilerParams(
             collective_id=collective_id, has_side_effects=True, vmem_limit_bytes=56 * MIB
         ),
         name="attend",
-    )(lengths, q, kv)
+    )(lengths, q, kv, weights)
 
 
 def attend_back_kernel(
     dims,
     heads,
     key_step,
+    reduce_parts,
     lengths,
     q_all,
     kv_all,
     do_in,
     out_t,
     lse,
+    grads,
     d_q_out,
     d_kv_out,
+    grad_sums,
     do_all,
     keys,
     keys_t,
@@ -806,6 +963,9 @@
     send_sem,
     recv_sem,
     own_sem,
+    reduce_send_sem,
+    reduce_recv_sem,
+    *buffers,
 ):
     z, y, x, cores = dims
     me = my_place(dims)
@@ -824,6 +984,9 @@
     do_copies = [to_head(do_in, do_all.at[my_head], o) for o in across]
     own_do = pltpu.make_async_copy(do_in.at[my_head], do_all.at[my_head], own_sem.at[0])
     own_do.start()
+    reduce_copy = Copies(dims, me, reduce_send_sem, reduce_recv_sem)
+    reduction = Reduce(dims, reduce_parts, reduce_copy, (grads,), buffers, None, grad_sums, 1.5)
+    reduction.step(1)
     place = lax.broadcasted_iota(jnp.int32, (HD, 1), 0)
 
     def at_head(h):
@@ -916,11 +1079,17 @@
         if s < z:
             ring[s] = push(ring_out.at[s - 1], ring_in.at[s - 1], along(0, 1))
 
+    now = 7
     for s in range(1, z + 1):
         send_sides(s)
+        now += 7 * len(sides)
+        reduction.step(now)
         if s > 1:
             combine(s - 1)
         compute((z - s if s < z else 0, 0, 0, 0), mine.at[(s - 1) % 2])
+        now += 7
+        reduction.step(now)
+    reduction.rest()
     for h in range(n_head):
         block = jnp.concatenate([d_q_t[a, :, at_head(h)] for a in range(heads)], 0) * HD ** (-0.5)
         d_q_mine[h] = block.T.astype(low)
@@ -936,23 +1105,27 @@
     for copy in copies:
         copy.wait_recv()
     push.finish()
-
-
-def attend_back(dims, lengths, q, kv, dout, out_t, lse, heads, collective_id):
+    reduce_copy.finish()
+
+
+def attend_back(dims, lengths, q, kv, dout, out_t, lse, grads, lower, heads, collective_id):
     z, y, x, cores = dims
     n_head, rows, width = q.shape
     amount = n_head * rows
     count = 3 * (n_head - 1) + z * (y - 1) + z - 1
     block = (amount, 2 * width)
     others = max(y - 1, 1)
+    parts = cut(0, grads.shape[2], range(lower, z), (CXY, CXY))
+    reduce_count = Reduce.count(dims, parts, False)
     return pl.pallas_call(
-        functools.partial(attend_back_kernel, dims, heads, 256),
+        functools.partial(attend_back_kernel, dims, heads, 256, parts),
         out_shape=(
             jax.ShapeDtypeStruct(q.shape, low),
             jax.ShapeDtypeStruct((n_head, rows, 2 * width), low),
+            jax.ShapeDtypeStruct((z - lower,) + grads.shape[2:], low),
         ),
-        in_specs=[SMEM_SPEC] + [VMEM_SPEC] * 5,
-        out_specs=[VMEM_SPEC] * 2,
+        in_specs=[SMEM_SPEC] + [VMEM_SPEC] * 6,
+        out_specs=[VMEM_SPEC] * 3,
         scratch_shapes=[
             pltpu.VMEM(q.shape, low),
             pltpu.VMEM((heads, amount, LANES), low),
@@ -973,12 +1146,15 @@
             pltpu.SemaphoreType.DMA((count,)),
             pltpu.SemaphoreType.DMA((count,)),
             pltpu.SemaphoreType.DMA((3,)),
-        ],
+            pltpu.SemaphoreType.DMA((reduce_count,)),
+            pltpu.SemaphoreType.DMA((reduce_count,)),
+        ]
+        + Reduce.scratch(dims, parts, False),
         compiler_params=pltpu.CompilerParams(
             collective_id=collective_id, has_side_effects=True, vmem_limit_bytes=60 * MIB
         ),
         name="attend_back",
-    )(lengths, q, kv, dout, out_t, lse)
+    )(lengths, q, kv, dout, out_t, lse, grads)
 
 
 def part_shapes(n_head):
@@ -1159,9 +1335,11 @@
     shard_rows,
     valid,
     rows,
+    counts_at,
     lengths,
     weights,
     common,
+    counted,
     inputs_t,
     enc_query,
     enc_keyval,
@@ -1194,11 +1372,14 @@
     bounds = clip_bounds(lengths)
     first = DQ * D // LANES
     block, blocks = common_blocks(first, first + (LAT + 4) * D // LANES, valid)
-    tail = shard_rows // TILE * TILE
+    piece, count_row, count_rows = counts_at
+    count_tile = count_row // TILE * TILE
     copies = [
         pltpu.make_async_copy(common.at[pl.ds(block, blocks)], held_common, sems.at[0]),
         pltpu.make_async_copy(weights.at[pl.ds(0, shards)], held, sems.at[1]),
-        pltpu.make_async_copy(weights.at[:, :, pl.ds(tail, TILE)], held_counts, sems.at[2]),
+        pltpu.make_async_copy(
+            counted.at[:, piece, pl.ds(count_tile, held_counts.shape[1])], held_counts, sems.at[2]
+        ),
     ]
     for copy in copies:
         copy.start()
@@ -1217,8 +1398,9 @@
     z_zero[...] = product(picked, latent_table[...])
     h_zero[...] = layer_norm(z_zero[...], gains[0:1, :]).astype(low)
     copies[2].wait()
-    counted = held_counts[...].astype(jnp.float32)[:, :, shard_rows - tail : shard_rows - tail + 1]
-    counts[...] = jnp.broadcast_to(jnp.sum(counted, (0, 1)), counts.shape)
+    begin = count_row - count_tile
+    all_counts = jnp.sum(held_counts[...].astype(jnp.float32), 0)[begin : begin + count_rows]
+    counts[...] = jnp.broadcast_to(jnp.sum(all_counts, 0, keepdims=True), counts.shape)
     copies[1].wait()
     for g in range(n_head):
         load_stage(stage, held, 0, shard_rows, g)
@@ -1254,14 +1436,14 @@
     return begin, -(-starts[last] // shard_rows) - begin
 
 
-def encode(lengths, weights, common, inputs_t, valid, rows, n_head, shard_rows):
+def encode(lengths, weights, common, counted, counts_at, inputs_t, valid, rows, n_head, shard_rows):
     width = HEADS // n_head * HD
     begin, shards = shards_of(n_head, shard_rows, 0, 4)
     query_rows = DQ * D // LANES
     block, blocks = common_blocks(query_rows, query_rows + (LAT + 4) * D // LANES, valid)
     keys = inputs_t.shape[1]
     return pl.pallas_call(
-        functools.partial(encode_kernel, n_head, shard_rows, valid, rows),
+        functools.partial(encode_kernel, n_head, shard_rows, valid, rows, counts_at),
         out_shape=[
             shape_of((D, D)),
             shape_of((DI, 2 * D)),
@@ -1280,12 +1462,12 @@
             shape_of((n_head, rows, 2 * width)),
             shape_of((8, LANES), jnp.float32),
         ],
-        in_specs=[SMEM_SPEC, ANY_SPEC, ANY_SPEC, VMEM_SPEC],
+        in_specs=[SMEM_SPEC] + [ANY_SPEC] * 3 + [VMEM_SPEC],
         out_specs=[VMEM_SPEC] * 16,
         scratch_shapes=[
             pltpu.VMEM((shards,) + weights.shape[1:], low),
             pltpu.VMEM((blocks,) + common.shape[1:], low),
-            pltpu.VMEM(weights.shape[:2] + (TILE, LANES), low),
+            pltpu.VMEM((counted.shape[0], round_up(counts_at[1] % TILE + counts_at[2], TILE), LANES), low),
             pltpu.VMEM((shards * shard_rows, LANES), jnp.float32),
             pltpu.VMEM((blocks * valid, LANES), jnp.float32),
             LINE,
@@ -1294,7 +1476,7 @@
         ],
         compiler_params=pltpu.CompilerParams(vmem_limit_bytes=56 * MIB),
         name="encode",
-    )(lengths, weights, common, inputs_t)
+    )(lengths, weights, common, counted, inputs_t)
 
 
 def gelu_and_slope(x):
@@ -1338,7 +1520,8 @@
     tile,
     query_grad,
     gain_grads,
-    grads,
+    lower_grads,
+    upper_grads,
     held,
     held_common,
     stage,
@@ -1425,12 +1608,20 @@
             matrix_into(stage, starts[m] - first_row, result, line)
         for b in range(shards):
             held[b, g, :shard_rows, :] = stage[pl.ds(b * shard_rows, shard_rows), :].astype(low)
-    back = pltpu.make_async_copy(held, grads.at[pl.ds(first_shard, shards)], sems.at[2])
-    back.start()
-    back.wait()
-
-
-def middle(counts, weights, common, z_one, o_self, out_queries_t, marks, gains, valid, n_head, shard_rows):
+    split = lower_grads.shape[0] - first_shard
+    copies = [
+        pltpu.make_async_copy(held.at[pl.ds(split, shards - split)], upper_grads, sems.at[2]),
+        pltpu.make_async_copy(
+            held.at[pl.ds(0, split)], lower_grads.at[pl.ds(first_shard, split)], sems.at[3]
+        ),
+    ]
+    for copy in copies:
+        copy.start()
+    for copy in copies:
+        copy.wait()
+
+
+def middle(counts, weights, common, z_one, o_self, out_queries_t, marks, gains, valid, split, n_head, shard_rows):
     rows = z_one.shape[0]
     begin, shards = shards_of(n_head, shard_rows, 4, 8)
     query_rows = DQ * D // LANES
@@ -1444,7 +1635,8 @@
             shape_of((8, LANES), jnp.float32),
             shape_of((query_rows, LANES), jnp.float32),
             shape_of((2, D), jnp.float32),
-            shape_of(weights.shape),
+            shape_of((split,) + weights.shape[1:]),
+            shape_of((weights.shape[0] - split,) + weights.shape[1:]),
         ],
         in_specs=[
             VMEM_SPEC,
@@ -1458,7 +1650,7 @@
             VMEM_SPEC,
             VMEM_SPEC,
         ],
-        out_specs=[VMEM_SPEC] * 5 + [ANY_SPEC],
+        out_specs=[VMEM_SPEC] * 5 + [ANY_SPEC] * 2,
         scratch_shapes=[
             pltpu.VMEM((shards,) + weights.shape[1:], low),
             pltpu.VMEM((blocks,) + common.shape[1:], low),
@@ -1472,7 +1664,7 @@
             pltpu.VMEM((DQ, D), low),
             pltpu.VMEM((rows, FF), jnp.float32),
             pltpu.VMEM((rows, FF), low),
-            pltpu.SemaphoreType.DMA((3,)),
+            pltpu.SemaphoreType.DMA((4,)),
         ],
         compiler_params=pltpu.CompilerParams(vmem_limit_bytes=56 * MIB),
         name="middle",
@@ -1649,32 +1841,62 @@
     heads_here = HEADS // n_head
     n_h, n_c = head_params.shape[0], common_params.shape[0]
     shard_rows, common_rows = n_h // LANES, -(-n_c // LANES)
-    head_rows = round_up(shard_rows + 1, TILE)
-    piece_rows = round_up(-(-common_rows // n_head), TILE)
     marks = [x.reshape(-1, LANES) for x in (labels, modality, labeled)]
+    count_rows = marks[0].shape[0]
+    head_rows = round_up(shard_rows, TILE)
+    piece_rows = round_up(-(-(common_rows + count_rows) // n_head), TILE)
+    counts_at = (*divmod(common_rows, piece_rows), count_rows)
+    lower = lower_planes(dims, n_head, shard_rows)
     head_wide = head_params.reshape(shard_rows, LANES)
     common_wide = jnp.pad(common_params, (0, common_rows * LANES - n_c)).reshape(common_rows, LANES)
-    weights, common = gather_all(dims, marks, (head_wide, common_wide), (head_rows, piece_rows), 0)
-    valid = common_rows
+    weights, counted = gather_all(
+        dims, marks, (head_wide, common_wide), (head_rows, piece_rows), lower, 0
+    )
+    common, valid = counted, common_rows
     if n_c % LANES:
         common = common.reshape(n_blk, -1)[:, :n_c].reshape(-1, LANES)
         valid = common.shape[0]
         common = jnp.pad(common, ((0, -valid % TILE), (0, 0)))[None, None]
 
-    encoded = encode(clip_lengths, weights, common, inputs.T, valid, rows, n_head, shard_rows)
+    encoded = encode(
+        clip_lengths, weights, common, counted, counts_at, inputs.T, valid, rows, n_head, shard_rows
+    )
     gains, z_one, counts = encoded[4], encoded[11], encoded[15]
-    o_self, lse_self, out_self_t, q_all, kv_all = attend(
-        dims, clip_lengths, encoded[13], encoded[14], heads_here, 1
+    o_self, lse_self, out_self_t, q_all, kv_all, weights = attend(
+        dims, clip_lengths, encoded[13], encoded[14], weights, lower, heads_here, 1
     )
-    dout, d_two, tile, query_grad, gain_grads, grads = middle(
-        counts, weights, common, z_one, o_self, out_queries.T, marks, gains, valid, n_head, shard_rows
+    dout, d_two, tile, query_grad, gain_grads, lower_grads, upper_grads = middle(
+        counts,
+        weights,
+        common,
+        z_one,
+        o_self,
+        out_queries.T,
+        marks,
+        gains,
+        valid,
+        lower * dims[1],
+        n_head,
+        shard_rows,
     )
-    d_self = attend_back(dims, clip_lengths, q_all, kv_all, dout, out_self_t, lse_self, heads_here, 2)
+    d_q, d_kv, upper_sums = attend_back(
+        dims,
+        clip_lengths,
+        q_all,
+        kv_all,
+        dout,
+        out_self_t,
+        lse_self,
+        upper_grads,
+        lower,
+        heads_here,
+        2,
+    )
     kept = encoded[:4] + encoded[5:13]
-    grads, common_grad = ending(
+    lower_grads, common_grad = ending(
         clip_lengths,
-        grads,
-        d_self,
+        lower_grads,
+        (d_q, d_kv),
         d_two,
         gains,
         gain_grads,
@@ -1689,7 +1911,7 @@
         common_grad = jnp.pad(common_grad, ((0, 0), (0, n_head * piece_rows * LANES - n_c)))
         common_grad = common_grad.reshape(n_blk, n_head, piece_rows, LANES)
     head_share, common_share, totals = reduce_all(
-        dims, (grads, common_grad), (shard_rows, common_rows), tile, 3
+        dims, lower_grads, upper_sums, common_grad, (shard_rows, common_rows), tile, 3
     )
     label_counts, loss_sums = counts[0, :MODES], totals[0, :MODES]
     clip_norm = jnp.sqrt(totals[0, MODES])

time: 330 us -> 405 us (1.23)
  Pallas kernels: 315 us -> 390 us
    pallas_call x2, Pallas kernels: 150 us -> 228 us  [the longest x1 131 us: attend(): pl.pallas_call(functools.partial(attend_kernel, dims, heads, 256, 256, pa...]
where the time goes in v1:
time: 405 us; the launch traced here: 399 us
  Pallas kernels  390 us (96%)
  other arithmetic  4.06 us (1%)
    pallas_call x1, Pallas kernels, attend(): pl.pallas_call(functools.partial(attend_kernel, dims, heads, 256, 256, pa...  131 us
    pallas_call x1, Pallas kernels, attend_back(): pl.pallas_call(functools.partial(attend_back_kernel, dims, heads, 256, pa...  96.7 us
    pallas_call x1, Pallas kernels, reduce_all(): pl.pallas_call(functools.partial(reduce_kernel, dims, parts), out_shape=[...  63.5 us
    pallas_call x1, Pallas kernels, gather_all(): pl.pallas_call(functools.partial(gather_kernel, dims, parts), out_shape=[...  52.1 us
    pallas_call x1, Pallas kernels, middle(): pl.pallas_call(functools.partial(middle_kernel, n_head, shard_rows, valid...  18.2 us
    pallas_call x1, Pallas kernels, ending(): pl.pallas_call(functools.partial(ending_kernel, n_head, shard_rows, valid...  17.7 us
    pallas_call x1, Pallas kernels, encode(): pl.pallas_call(functools.partial(encode_kernel, n_head, shard_rows, valid...  10.6 us

profile of v1, /device:TPU:0, one launch (start us, length us, event | category | flops | bytes accessed | tf_op | source)
XLA Modules:
  0.0 399.4 jit_solution(10172895031692485985)
XLA Ops:
  0.6 52.1 %gather_weights.1 = (bf16[8,4,1168,128]{3,2,1,0:T(8,128)(2,1)}, bf16[8,4,240,128]{3,2,1,0:T(8,128)(2,1)}) custom-call(s32[8,128]{1,0:T(8,128)} %bitcast.30, s32[8,128]{1,0:T(8,128)} %bitcast.32, s32[8,128]{1,0:T(8,128)} %bitcast.34, f32[1160,128]{1,0:T(8,128)} %bitcast.26, f32[907,128]{1,0:T(8,128)} %bitcast.28), custom_call_target="tpu_custom_call" | custom-call | tf_op jit(solution)/shard_map/gather_weights/pallas_call | solution.py:354
  52.8 10.6 %encode.1 = (bf16[512,512]{1,0:T(8,128)(2,1)}, bf16[704,1024]{1,0:T(8,128)(2,1)}, bf16[512,512]{1,0:T(8,128)(2,1)}, bf16[512,1536]{1,0:T(8,128)(2,1)}, f32[4,512...) custom-call(s32[6]{0:T(128)} %lengths.7, ...), custom_call_target="tpu_custom_call" | custom-call | tf_op jit(solution)/shard_map/encode/pallas_call | solution.py:1445
  63.3 131.1 %attend.1 = (bf16[4,256,128]{2,1,0:T(8,128)(2,1)}, f32[2,1024]{1,0:T(2,128)}, f32[128,1024]{1,0:T(8,128)}, bf16[4,256,128]{2,1,0:T(8,128)(2,1)}, bf16[8,4,256,25...) custom-call(s32[6]{0:T(128)} %lengths.7, ...), custom_call_target="tpu_custom_call", output_to_operand_aliasing={{5}: (3, {})} | custom-call | tf_op jit(solution)/shard_map/attend/pallas_call | solution.py:899
  194.5 18.2 %middle.1 = (bf16[4,256,128]{2,1,0:T(8,128)(2,1)}, f32[256,512]{1,0:T(8,128)}, f32[8,128]{1,0:T(8,128)}, f32[4104,128]{1,0:T(8,128)}, f32[2,512]{1,0:T(2,128)}, ...) custom-call(f32[8,128]{1,0:T(8,128)} %get-tuple-element.52.counts, ...), custom_call_target="tpu_custom_call" | custom-call | tf_op jit(solution)/shard_map/middle/pallas_call | solution.py:1629
  212.7 96.7 %attend_back.1 = (bf16[4,256,128]{2,1,0:T(8,128)(2,1)}, bf16[4,256,256]{2,1,0:T(8,128)(2,1)}, bf16[2,1168,128]{2,1,0:T(8,128)(2,1)}) custom-call(s32[6]{0:T(128)} %lengths.7, bf16[4,256,128]{2,1,0:T(8,128)(2,1)} %get-tuple-element.60.q_all, bf16[8,4,256,256]{3,2,1,0:T(8,128)(2,1)} %get-tuple-element.61.kv_all, bf16[4,256,128]{2,1,0:T(8,128)(2,1)} %get-tuple-element.62.do_in, ...), custom_call_target="tpu_custom_call" | custom-call | tf_op jit(solution)/shard_map/attend_back/pallas_call | solution.py:1120
  309.4 17.7 %ending.1 = (bf16[4,4,1168,128]{3,2,1,0:T(8,128)(2,1)}, bf16[8,4,240,128]{3,2,1,0:T(8,128)(2,1)}) custom-call(s32[6]{0:T(128)} %lengths.7, bf16[4,4,1168,128]{3,2,1,0:T(8,128)(2,1)} %get-tuple-element.59.grads_in, bf16[4,256,128]{2,1,0:T(8,128)(2,1)} %get-tuple-element.66.d_q_self, ...), custom_call_target="tpu_custom_call", output_to_operand_aliasing={{0}: (1, {})} | custom-call | tf_op jit(solution)/shard_map/ending/pallas_call | solution.py:1793
  327.1 0.0 copy-start
  327.1 0.0 copy-start.2
  327.1 0.0 copy-start.3
  327.2 0.0 copy-start.1
  327.2 0.0 copy-start.4
  327.2 0.0 copy-start.5
  327.2 63.5 %reduce_gradients.1 = (f32[1160,128]{1,0:T(8,128)}, f32[907,128]{1,0:T(8,128)}, f32[8,128]{1,0:T(8,128)}) custom-call(bf16[4,4,1168,128]{3,2,1,0:T(8,128)(2,1)} %get-tuple-element.82.refs_0_, bf16[2,1168,128]{2,1,0:T(8,128)(2,1)} %get-tuple-element.83.refs_1_, bf16[8,4,240,128]{3,2,1,0:T(8,128)(2,1)} %get-tuple-element.84.refs_2_, ...), custom_call_target="tpu_custom_call" | custom-call | tf_op jit(solution)/shard_map/reduce_gradients/pallas_call | solution.py:601
  390.7 1.3 slice.9
  392.7 0.0 copy-start.6
  392.7 1.3 slice_bitcast_fusion
  394.0 0.0 copy-done
  394.0 0.0 copy-done.2
  394.0 0.0 copy-done.3
  394.0 2.7 fusion.7
  396.7 0.0 copy-done.1
  396.7 0.0 copy-done.4
  396.7 0.0 copy-done.5
  396.7 0.0 copy-done.6
  396.7 1.4 fusion.4
Async XLA Ops:
  327.1 66.9 %copy-start = (f32[148480]{0:T(1024)S(1)}, f32[148480]{0:T(1024)}, u32[]{:S(2)}) copy-start(f32[148480]{0:T(1024)} %param.18) | copy-start | bytes 1781764
  327.1 66.9 %copy-start.2 = (f32[148480]{0:T(1024)S(1)}, f32[148480]{0:T(1024)}, u32[]{:S(2)}) copy-start(f32[148480]{0:T(1024)} %param.19) | copy-start | bytes 1781764
  327.1 66.9 %copy-start.3 = (f32[148480]{0:T(1024)S(1)}, f32[148480]{0:T(1024)}, u32[]{:S(2)}) copy-start(f32[148480]{0:T(1024)} %param.20) | copy-start | bytes 1781764
  327.2 69.5 %copy-start.1 = (f32[116096]{0:T(1024)S(1)}, f32[116096]{0:T(1024)}, u32[]{:S(2)}) copy-start(f32[116096]{0:T(1024)} %param.21) | copy-start | bytes 1393156
  327.2 69.5 %copy-start.4 = (f32[116096]{0:T(1024)S(1)}, f32[116096]{0:T(1024)}, u32[]{:S(2)}) copy-start(f32[116096]{0:T(1024)} %param.22) | copy-start | bytes 1393156
  327.2 69.5 %copy-start.5 = (f32[116096]{0:T(1024)S(1)}, f32[116096]{0:T(1024)}, u32[]{:S(2)}) copy-start(f32[116096]{0:T(1024)} %param.23) | copy-start | bytes 1393156
  392.7 4.0 copy-start.6

commit v2 on v0

--- a/solution.py
+++ b/solution.py
@@ -106,7 +106,7 @@
     )
 
 
-AHEAD = 10
+AHEAD = 6.0
 RING = 0
 
 
@@ -609,7 +609,6 @@
 def attend_kernel(
     dims,
     heads,
-    key_step,
     query_step,
     lengths,
     q_in,
@@ -680,21 +679,12 @@
         def query_block(n):
             at = pl.ds(pl.multiple_of(n * query_step, query_step), query_step)
             for a in range(heads):
-                query = queries[a, :, at]
-                highest = jnp.full((8, query_step), -1e38, jnp.float32)
-                for k in range(0, amount, key_step):
-                    scores = product(keys[a, k : k + key_step, :], query)
-                    highest = jnp.maximum(
-                        highest, jnp.max(scores.reshape(key_step // 8, 8, query_step), 0)
-                    )
+                scores = product(keys[a], queries[a, :, at])
                 old = top[a, :, at]
-                new = jnp.maximum(old, jnp.max(highest, 0, keepdims=True))
+                new = jnp.maximum(old, jnp.max(scores, 0, keepdims=True))
                 top[a, :, at] = new
-                total = accum[a, :, at] * jnp.exp(old - new)
-                for k in range(0, amount, key_step):
-                    scores = product(keys[a, k : k + key_step, :], query)
-                    probs = jnp.exp(scores - new).astype(low)
-                    total = total + product(values_t[a, :, k : k + key_step], probs)
+                probs = jnp.exp(scores - new).astype(low)
+                total = accum[a, :, at] * jnp.exp(old - new) + product(values_t[a], probs)
                 accum[a, :, at] = total
 
     for a in range(heads):
@@ -747,7 +737,7 @@
     amount = n_head * rows
     count = 3 * (n_head - 1) + n_head * (z - 1 + z * (y - 1))
     return pl.pallas_call(
-        functools.partial(attend_kernel, dims, heads, 256, 256),
+        functools.partial(attend_kernel, dims, heads, 256),
         out_shape=(
             jax.ShapeDtypeStruct(q.shape, low),
             jax.ShapeDtypeStruct((heads, amount), jnp.float32),
@@ -840,7 +830,7 @@
                 q_t[a * HD : (a + 1) * HD],
                 lse[a : a + 1, at_head(h)],
             )
-            q_rows[a, at_head(h), :] = jnp.where(in_head(a, 1), block * HD ** (-0.5), 0.0).astype(low)
+            q_rows[a, :, at_head(h)] = (q_t[a * HD : (a + 1) * HD] * HD ** (-0.5)).astype(low)
     for a in range(heads):
         d_q_t[a] = jnp.zeros(d_q_t.shape[1:], jnp.float32)
     own_do.wait()
@@ -853,7 +843,7 @@
             part = do_t[a * HD : (a + 1) * HD]
             delta = jnp.sum(part * out_t[a * HD : (a + 1) * HD, at_head(h)], 0, keepdims=True)
             douts[a, :, at_head(h)] = with_tail(a, part, in_three(place, -delta)).astype(low)
-            do_rows[a, at_head(h), :] = jnp.where(in_head(a, 1), block, 0.0).astype(low)
+            do_rows[a, :, at_head(h)] = part.astype(low)
 
     def compute(offset, target):
         blk = blk_of(dims, shifted(dims, me, offset, 1))
@@ -877,18 +867,15 @@
         @pl.loop(0, amount // key_step)
         def key_block(k):
             at = pl.ds(pl.multiple_of(k * key_step, key_step), key_step)
-            d_key = jnp.zeros((key_step, LANES), jnp.float32)
-            d_value = jnp.zeros((key_step, LANES), jnp.float32)
+            d_keys, d_values = [], []
             for a in range(heads):
                 probs = jnp.exp(product(keys[a, at, :], queries[a]))
                 d_probs = product(values[a, at, :], douts[a])
                 d_scores = (probs * d_probs).astype(low)
-                d_value = d_value + product(probs.astype(low), do_rows[a])
-                d_key = d_key + product(d_scores, q_rows[a])
+                d_values.append(against(do_rows[a], probs.astype(low)))
+                d_keys.append(against(q_rows[a], d_scores))
                 d_q_t[a] = d_q_t[a] + product(keys_t[a, :, at], d_scores)
-            target[at, :] = jnp.concatenate([d_key[:, :width], d_value[:, :width]], 1).astype(
-                target.dtype
-            )
+            target[at, :] = jnp.concatenate(d_keys + d_values, 0).T.astype(target.dtype)
 
     side, ring = {}, {}
 
@@ -961,8 +948,8 @@
             pltpu.VMEM((heads, LANES, amount), low),
             pltpu.VMEM((heads, LANES, amount), low),
             pltpu.VMEM((heads, HD, amount), jnp.float32),
-            pltpu.VMEM((heads, amount, LANES), low),
-            pltpu.VMEM((heads, amount, LANES), low),
+            pltpu.VMEM((heads, HD, amount), low),
+            pltpu.VMEM((heads, HD, amount), low),
             pltpu.VMEM((z, others) + block, low),
             pltpu.VMEM((z, others) + block, low),
             pltpu.VMEM((max(z - 1, 1),) + block, low),

time: 330 us -> 329 us (level)
    pallas_call x1, Pallas kernels: 76.3 us -> 73 us  [attend_back(): pl.pallas_call(functools.partial(attend_back_kernel, dims, heads, 256), o...]
where the time goes in v2:
time: 329 us; the launch traced here: 324 us
  Pallas kernels  314 us (95%)
  other arithmetic  4.21 us (1%)
    pallas_call x1, Pallas kernels, attend(): pl.pallas_call(functools.partial(attend_kernel, dims, heads, 256), out_sh...  74.5 us
    pallas_call x1, Pallas kernels, attend_back(): pl.pallas_call(functools.partial(attend_back_kernel, dims, heads, 256), o...  73 us
    pallas_call x1, Pallas kernels, reduce_all(): pl.pallas_call(functools.partial(reduce_kernel, dims, parts), out_shape=[...  65.7 us
    pallas_call x1, Pallas kernels, gather_all(): pl.pallas_call(functools.partial(gather_kernel, dims, parts), out_shape=[...  53.6 us
    pallas_call x1, Pallas kernels, middle(): pl.pallas_call(functools.partial(middle_kernel, n_head, shard_rows, valid...  18.2 us
    pallas_call x1, Pallas kernels, ending(): pl.pallas_call(functools.partial(ending_kernel, n_head, shard_rows, valid...  17.7 us
    pallas_call x1, Pallas kernels, encode(): pl.pallas_call(functools.partial(encode_kernel, n_head, shard_rows, valid...  11.1 us

profile of v2, /device:TPU:0, one launch (start us, length us, event | category | flops | bytes accessed | tf_op | source)
XLA Modules:
  0.0 323.6 jit_solution(15891679127859142338)
XLA Ops:
  0.6 53.6 %gather_weights.1 = (bf16[8,4,1168,128]{3,2,1,0:T(8,128)(2,1)}, bf16[8,4,240,128]{3,2,1,0:T(8,128)(2,1)}) custom-call(s32[8,128]{1,0:T(8,128)} %bitcast.30, s32[8,128]{1,0:T(8,128)} %bitcast.32, s32[8,128]{1,0:T(8,128)} %bitcast.34, f32[1160,128]{1,0:T(8,128)} %bitcast.26, f32[907,128]{1,0:T(8,128)} %bitcast.28), custom_call_target="tpu_custom_call" | custom-call | tf_op jit(solution)/shard_map/gather_weights/pallas_call | solution.py:284
  54.2 11.1 %encode.1 = (bf16[512,512]{1,0:T(8,128)(2,1)}, bf16[704,1024]{1,0:T(8,128)(2,1)}, bf16[512,512]{1,0:T(8,128)(2,1)}, bf16[512,1536]{1,0:T(8,128)(2,1)}, f32[4,512...) custom-call(s32[6]{0:T(128)} %lengths.7, ...), custom_call_target="tpu_custom_call" | custom-call | tf_op jit(solution)/shard_map/encode/pallas_call | solution.py:1250
  65.4 74.5 %attend.1 = (bf16[4,256,128]{2,1,0:T(8,128)(2,1)}, f32[2,1024]{1,0:T(2,128)}, f32[128,1024]{1,0:T(8,128)}, bf16[4,256,128]{2,1,0:T(8,128)(2,1)}, bf16[8,4,256,256]{3,2,1,0:T(8,128)(2,1)}) custom-call(s32[6]{0:T(128)} %lengths.7, bf16[4,256,128]{2,1,0:T(8,128)(2,1)} %get-tuple-element.51.q_in, bf16[4,256,256]{2,1,0:T(8,128)(2,1)} %get-tuple-element.52.kv_in), custom_call_target="tpu_custom_call" | custom-call | tf_op jit(solution)/shard_map/attend/pallas_call | solution.py:739
  139.9 18.2 %middle.1 = (bf16[4,256,128]{2,1,0:T(8,128)(2,1)}, f32[256,512]{1,0:T(8,128)}, f32[8,128]{1,0:T(8,128)}, f32[4104,128]{1,0:T(8,128)}, f32[2,512]{1,0:T(2,128)}, /*index=5*/bf16[8,4,1168,128]{3,2,1,0:T(8,128)(2,1)}) custom-call(f32[8,128]{1,0:T(8,128)} %get-tuple-element.49.counts, bf16[8,4,1168,128]{3,2,1,0:T(8,128)(2,1)} %get-tuple-element.47.weights, ...), custom_call_target="tpu_custom_call" | custom-call | tf_op jit(solution)/shard_map/middle/pallas_call | solution.py:1425
  158.1 73.0 %attend_back.1 = (bf16[4,256,128]{2,1,0:T(8,128)(2,1)}, bf16[4,256,256]{2,1,0:T(8,128)(2,1)}) custom-call(s32[6]{0:T(128)} %lengths.7, bf16[4,256,128]{2,1,0:T(8,128)(2,1)} %get-tuple-element.56.q_all, bf16[8,4,256,256]{3,2,1,0:T(8,128)(2,1)} %get-tuple-element.57.kv_all, bf16[4,256,128]{2,1,0:T(8,128)(2,1)} %get-tuple-element.58.do_in, ...), custom_call_target="tpu_custom_call" | custom-call | tf_op jit(solution)/shard_map/attend_back/pallas_call | solution.py:935
  231.0 17.7 %ending.1 = (bf16[8,4,1168,128]{3,2,1,0:T(8,128)(2,1)}, bf16[8,4,240,128]{3,2,1,0:T(8,128)(2,1)}) custom-call(s32[6]{0:T(128)} %lengths.7, bf16[8,4,1168,128]{3,2,1,0:T(8,128)(2,1)} %get-tuple-element.55.grads_in, bf16[4,256,128]{2,1,0:T(8,128)(2,1)} %get-tuple-element.61.d_q_self, ...), custom_call_target="tpu_custom_call", output_to_operand_aliasing={{0}: (1, {})} | custom-call | tf_op jit(solution)/shard_map/ending/pallas_call | solution.py:1588
  248.8 0.0 copy-start
  248.8 0.0 copy-start.2
  248.8 0.0 copy-start.3
  248.8 65.7 %reduce_gradients.1 = (f32[1160,128]{1,0:T(8,128)}, f32[907,128]{1,0:T(8,128)}, f32[8,128]{1,0:T(8,128)}) custom-call(bf16[8,4,1168,128]{3,2,1,0:T(8,128)(2,1)} %get-tuple-element.77.refs_0_, bf16[8,4,240,128]{3,2,1,0:T(8,128)(2,1)} %get-tuple-element.78.refs_1_, f32[8,128]{1,0:T(8,128)} %get-tuple-element.79.refs_2_), custom_call_target="tpu_custom_call" | custom-call | tf_op jit(solution)/shard_map/reduce_gradients/pallas_call | solution.py:469
  314.5 1.3 slice.9
  316.5 1.2 slice_bitcast_fusion
  317.7 0.0 copy-done
  317.7 0.0 copy-done.2
  317.7 0.0 copy-done.3
  317.7 0.0 copy-start.1
  317.8 0.0 copy-start.4
  317.8 0.0 copy-start.5
  317.8 0.0 copy-start.6
  317.8 2.8 fusion.7
  320.6 0.0 copy-done.1
  320.6 0.0 copy-done.4
  320.6 0.0 copy-done.5
  320.6 0.0 copy-done.6
  320.6 1.4 fusion.4
Async XLA Ops:
  248.8 69.0 %copy-start = (f32[148480]{0:T(1024)S(1)}, f32[148480]{0:T(1024)}, u32[]{:S(2)}) copy-start(f32[148480]{0:T(1024)} %param.18) | copy-start | bytes 1781764
  248.8 68.9 %copy-start.2 = (f32[148480]{0:T(1024)S(1)}, f32[148480]{0:T(1024)}, u32[]{:S(2)}) copy-start(f32[148480]{0:T(1024)} %param.19) | copy-start | bytes 1781764
  248.8 68.9 %copy-start.3 = (f32[148480]{0:T(1024)S(1)}, f32[148480]{0:T(1024)}, u32[]{:S(2)}) copy-start(f32[148480]{0:T(1024)} %param.20) | copy-start | bytes 1781764
  317.7 2.9 copy-start.1
  317.8 2.9 copy-start.4
  317.8 2.8 copy-start.5
  317.8 2.8 copy-start.6

commit v3 on v2

--- a/solution.py
+++ b/solution.py
@@ -522,31 +522,24 @@
     return opening, ending
 
 
-def lane_of_tail(a):
-    return HD if a % 2 == 0 else 0
-
-
-def in_head(a, axis):
-    shape = (1, LANES) if axis else (LANES, 1)
-    lane = lax.broadcasted_iota(jnp.int32, shape, axis)
-    return (lane >= a * HD) & (lane < (a + 1) * HD)
-
-
-def all_lanes(block, first, width):
-    piece = block[:, first : first + width]
-    if width < LANES:
-        piece = jnp.concatenate([piece, jnp.zeros((piece.shape[0], LANES - width), piece.dtype)], 1)
-    return piece
-
-
-def with_key_tail(bounds, a, first_row, columns):
+def low_half(axis):
+    return lax.broadcasted_iota(jnp.int32, (1, LANES) if axis else (LANES, 1), axis) < HD
+
+
+def with_key_tail(bounds, first_row, kv):
     clips = len(bounds)
-    place = lax.broadcasted_iota(jnp.int32, (1, LANES), 1) - lane_of_tail(a)
+    place = lax.broadcasted_iota(jnp.int32, (1, LANES), 1) - HD
     opening, ending = clip_borders(bounds, place)
     ones = jnp.where((place >= clips) & (place < clips + 3), 1.0, 0.0)
-    row = first_row + lax.broadcasted_iota(jnp.int32, columns.shape, 0)
+    row = first_row + lax.broadcasted_iota(jnp.int32, kv.shape, 0)
     tail = jnp.where((row >= opening) & (row < ending), ones, big_negative)
-    return jnp.where(in_head(a, 1), columns.astype(jnp.float32), tail).astype(low)
+    return jnp.where(low_half(1), kv.astype(jnp.float32), tail).astype(low)
+
+
+def with_value_tail(kv):
+    place = lax.broadcasted_iota(jnp.int32, (1, LANES), 1)
+    ones = jnp.where(place < 3, 1.0, 0.0)
+    return jnp.where(low_half(1), ones, kv.astype(jnp.float32)).astype(low)
 
 
 def in_three(place, value):
@@ -560,11 +553,7 @@
     )
 
 
-def with_tail(a, rows, tail):
-    return jnp.concatenate([rows, tail] if lane_of_tail(a) else [tail, rows], 0)
-
-
-def with_query_tail(bounds, a, first_row, rows, extra):
+def with_query_tail(bounds, first_row, rows, extra):
     clips = len(bounds)
     place = lax.broadcasted_iota(jnp.int32, (HD, 1), 0)
     opening, ending = clip_borders(bounds, place)
@@ -573,7 +562,50 @@
     tail = jnp.where(inside, 1.0, 0.0)
     if extra is not None:
         tail = tail + in_three(place - clips, -extra)
-    return with_tail(a, rows * HD ** (-0.5), tail).astype(low)
+    return jnp.concatenate([rows * HD ** (-0.5), tail], 0).astype(low)
+
+
+def pack(rows):
+    half = rows.shape[0] // 2
+    return jnp.concatenate([rows[:half], rows[half:]], 1)
+
+
+def unpack(packed):
+    return jnp.concatenate([packed[:, :HD], packed[:, HD:]], 0)
+
+
+def unpack_t(packed):
+    turned = packed.astype(jnp.float32).T
+    return jnp.concatenate([turned[:HD], turned[HD:]], 1)
+
+
+def pack_t(columns):
+    half = columns.shape[1] // 2
+    return jnp.concatenate([columns[:, :half], columns[:, half:]], 0).T
+
+
+class Team:
+    def __init__(self, dims):
+        z, y, x, cores = dims
+        self.dims = dims
+        self.wide = HEADS // (x * cores) == y
+        self.size = x * cores * (y if self.wide else 1)
+        self.groups = z if self.wide else z * y
+        axes = (1, 2, 3) if self.wide else (2, 3)
+        offsets = [o for o in all_offsets(dims, axes) if any(o)]
+        self.others = sorted(offsets, key=lambda o: (o[1] + o[2], o))
+        self.sides = [] if self.wide else axis_peers(dims, (1,))
+
+    def slot(self, place):
+        head = head_of(self.dims, place)
+        return place[1] * self.dims[2] * self.dims[3] + head if self.wide else head
+
+    def group(self, place):
+        return place[0] if self.wide else blk_of(self.dims, place)
+
+
+def heads_of(n_head, slots):
+    return [(s % n_head, s // n_head) for s in range(slots)]
 
 
 class Pushes:
@@ -600,16 +632,10 @@
     return sorted(across, key=lambda o: (o[2] == 0, o[3]))
 
 
-def ring_and_sides(dims):
-    z = dims[0]
-    ring = sorted({along(0, 1 % z), along(0, (z - 1) % z)} - {(0, 0, 0, 0)})
-    return ring + axis_peers(dims, (1,))
-
-
 def attend_kernel(
-    dims,
-    heads,
+    team,
     query_step,
+    key_step,
     lengths,
     q_in,
     kv_in,
@@ -628,102 +654,101 @@
     recv_sem,
     own_sem,
 ):
-    z, y, x, cores = dims
+    dims = team.dims
+    z = dims[0]
     me = my_place(dims)
     bounds = clip_bounds(lengths)
-    n_head = x * cores
-    rows, width = q_in.shape[1], heads * HD
-    amount = n_head * rows
-    my_blk, my_head = blk_of(dims, me), head_of(dims, me)
-    across = peers_across(dims)
-    sides = axis_peers(dims, (1,))
-    greet(dims, me, across + ring_and_sides(dims))
+    rows = kv_in.shape[1]
+    amount = team.size * rows
+    my_group, my_slot = team.group(me), team.slot(me)
+    ring_ends = sorted({along(0, 1 % z), along(0, (z - 1) % z)} - {(0, 0, 0, 0)})
+    greet(dims, me, team.others + ring_ends + team.sides)
     push = Pushes(dims, me, send_sem, recv_sem)
-    own_kv = pltpu.make_async_copy(kv_in.at[my_head], kv_all.at[my_blk, my_head], own_sem.at[0])
-    own_q = pltpu.make_async_copy(q_in.at[my_head], q_all.at[my_head], own_sem.at[1])
+    own_kv = pltpu.make_async_copy(kv_in.at[my_slot], kv_all.at[my_group, my_slot], own_sem.at[0])
+    own_q = pltpu.make_async_copy(q_in.at[my_slot], q_all.at[my_slot], own_sem.at[1])
     own_kv.start()
     own_q.start()
 
-    def to_head(src, dst, o):
-        return push(src.at[head_of(dims, shifted(dims, me, o, 1))], dst, o)
-
-    kv_copies = {o: to_head(kv_in, kv_all.at[my_blk, my_head], o) for o in across}
-    q_copies = [to_head(q_in, q_all.at[my_head], o) for o in across]
+    def to_team(src, dst, o):
+        return push(src.at[team.slot(shifted(dims, me, o, 1))], dst, o)
+
+    kv_copies = {o: to_team(kv_in, kv_all.at[my_group, my_slot], o) for o in team.others}
+    q_copies = [to_team(q_in, q_all.at[my_slot], o) for o in team.others]
     ring, side = {}, {}
-    pieces = [(0, 0, 0, 0)] + across[::-1]
-
-    def send_on(s, n):
-        block = kv_all.at[
-            blk_of(dims, shifted(dims, me, along(0, s), -1)),
-            head_of(dims, shifted(dims, me, pieces[n], -1)),
-        ]
-        if s < z - 1:
-            ring[(s + 1, n)] = push(block, block, along(0, 1))
-        for o in sides:
-            side[(s, n, o)] = push(block, block, o)
+
+    def group_at(offset):
+        return team.group(shifted(dims, me, offset, -1))
+
+    def send_piece(o):
+        block = kv_all.at[my_group, team.slot(shifted(dims, me, o, -1))]
+        if z > 1:
+            ring.setdefault(1, []).append(push(block, block, along(0, 1)))
+
+    def send_on(s):
+        block = kv_all.at[group_at(along(0, s))]
+        if 0 < s < z - 1:
+            ring[s + 1] = [push(block, block, along(0, 1))]
+        for o in team.sides:
+            side[(s, o)] = push(block, block, o)
 
     def compute(offset):
-        blk = blk_of(dims, shifted(dims, me, offset, -1))
-
-        @pl.loop(0, n_head)
-        def build(h):
-            at = pl.ds(pl.multiple_of(h * rows, rows), rows)
-            block = kv_all[blk, h]
-            k_block, v_block = all_lanes(block, 0, width), all_lanes(block, width, width)
-            v_t = v_block.astype(jnp.float32).T
-            for a in range(heads):
-                keys[a, at, :] = with_key_tail(bounds, a, blk * amount + h * rows, k_block)
-                values_t[a, :HD, at] = v_t[a * HD : (a + 1) * HD].astype(low)
-
-        @pl.loop(0, amount // query_step)
-        def query_block(n):
-            at = pl.ds(pl.multiple_of(n * query_step, query_step), query_step)
-            for a in range(heads):
-                scores = product(keys[a], queries[a, :, at])
-                old = top[a, :, at]
-                new = jnp.maximum(old, jnp.max(scores, 0, keepdims=True))
-                top[a, :, at] = new
-                probs = jnp.exp(scores - new).astype(low)
-                total = accum[a, :, at] * jnp.exp(old - new) + product(values_t[a], probs)
-                accum[a, :, at] = total
-
-    for a in range(heads):
-        values_t[a, HD:, :] = jnp.ones((values_t.shape[1] - HD, amount), low)
-        top[a] = jnp.full((1, amount), -1e38, jnp.float32)
-        accum[a] = jnp.zeros(accum.shape[1:], jnp.float32)
+        group = group_at(offset)
+
+        @pl.loop(0, team.size)
+        def build(n):
+            at = pl.ds(pl.multiple_of(n * rows, rows), rows)
+            block = kv_all[group, n]
+            keys[at, :] = with_key_tail(bounds, group * amount + n * rows, block)
+            values_t[:HD, at] = block.astype(jnp.float32).T[HD:].astype(low)
+
+        @pl.loop(0, amount // (2 * query_step))
+        def query_blocks(n):
+            for half in range(2):
+                at = pl.ds(pl.multiple_of((2 * n + half) * query_step, query_step), query_step)
+                query = queries[:, at]
+                old, total = top[:, at], accum[:, at]
+                for k in range(0, amount, key_step):
+                    scores = product(keys[k : k + key_step, :], query)
+                    new = jnp.maximum(old, jnp.max(scores, 0, keepdims=True))
+                    probs = jnp.exp(scores - new).astype(low)
+                    total = total * jnp.exp(old - new) + product(values_t[:, k : k + key_step], probs)
+                    old = new
+                top[:, at] = old
+                accum[:, at] = total
+
+    values_t[HD:, :] = jnp.ones((TILE, amount), low)
+    top[...] = jnp.full(top.shape, -1e38, jnp.float32)
+    accum[...] = jnp.zeros(accum.shape, jnp.float32)
     own_kv.wait()
-    send_on(0, 0)
-    for n in range(1, n_head):
-        kv_copies[pieces[n]].wait_recv()
-        send_on(0, n)
+    send_piece((0, 0, 0, 0))
+    for o in team.others:
+        kv_copies[o].wait_recv()
+        send_piece(o)
+    send_on(0)
     own_q.wait()
     for copy in q_copies:
         copy.wait_recv()
-    for a in range(heads):
-        for h in range(n_head):
-            q_t = all_lanes(q_all[h], 0, width).astype(jnp.float32).T
-            queries[a, :, h * rows : (h + 1) * rows] = with_query_tail(
-                bounds, a, my_blk * amount + h * rows, q_t[a * HD : (a + 1) * HD], None
-            )
+    for n in range(team.size):
+        queries[:, n * rows : (n + 1) * rows] = with_query_tail(
+            bounds, my_group * amount + n * rows, unpack_t(q_all[n]), None
+        )
     compute((0, 0, 0, 0))
     for s in range(1, z + 1):
         if s < z:
-            for n in range(n_head):
-                ring[(s, n)].wait_recv()
-                send_on(s, n)
+            for copy in ring[s]:
+                copy.wait_recv()
+            send_on(s)
             compute(along(0, s))
-        for o in sides:
-            for n in range(n_head):
-                side[(s - 1, n, o)].wait_recv()
+        for o in team.sides:
+            side[(s - 1, o)].wait_recv()
             compute((s - 1, o[1], 0, 0))
-    for a in range(heads):
-        total = accum[a, HD : HD + 1, :]
-        out_t[a * HD : (a + 1) * HD, :] = accum[a, :HD, :] / total
-        lse[a : a + 1, :] = top[a] + jnp.log(total)
-    for h in range(n_head):
-        o_mine[h] = out_t[:, h * rows : (h + 1) * rows].T.astype(low)
-    o_copies = [to_head(o_mine, o_out.at[my_head], o) for o in across]
-    own_o = pltpu.make_async_copy(o_mine.at[my_head], o_out.at[my_head], own_sem.at[2])
+    total = accum[HD : HD + 1, :]
+    out_t[...] = accum[:HD, :] / total
+    lse[...] = top[...] + jnp.log(total)
+    for n in range(team.size):
+        o_mine[n] = pack_t(out_t[:, n * rows : (n + 1) * rows]).astype(low)
+    o_copies = [to_team(o_mine, o_out.at[my_slot], o) for o in team.others]
+    own_o = pltpu.make_async_copy(o_mine.at[my_slot], o_out.at[my_slot], own_sem.at[2])
     own_o.start()
     own_o.wait()
     for copy in o_copies:
@@ -731,28 +756,28 @@
     push.finish()
 
 
-def attend(dims, lengths, q, kv, heads, collective_id):
-    z, y, x, cores = dims
-    n_head, rows, width = q.shape
-    amount = n_head * rows
-    count = 3 * (n_head - 1) + n_head * (z - 1 + z * (y - 1))
+def attend(dims, lengths, q, kv, collective_id):
+    team = Team(dims)
+    z = dims[0]
+    amount = team.size * kv.shape[1]
+    count = 3 * (team.size - 1) + team.size + z + z * len(team.sides)
     return pl.pallas_call(
-        functools.partial(attend_kernel, dims, heads, 256),
+        functools.partial(attend_kernel, team, 256, 1024),
         out_shape=(
             jax.ShapeDtypeStruct(q.shape, low),
-            jax.ShapeDtypeStruct((heads, amount), jnp.float32),
-            jax.ShapeDtypeStruct((width, amount), jnp.float32),
+            jax.ShapeDtypeStruct((1, amount), jnp.float32),
+            jax.ShapeDtypeStruct((HD, amount), jnp.float32),
             jax.ShapeDtypeStruct(q.shape, low),
-            jax.ShapeDtypeStruct((z * y,) + kv.shape, low),
+            jax.ShapeDtypeStruct((team.groups,) + kv.shape, low),
         ),
         in_specs=[SMEM_SPEC, VMEM_SPEC, VMEM_SPEC],
         out_specs=[VMEM_SPEC] * 5,
         scratch_shapes=[
-            pltpu.VMEM((heads, amount, LANES), low),
-            pltpu.VMEM((heads, HD + TILE, amount), low),
-            pltpu.VMEM((heads, LANES, amount), low),
-            pltpu.VMEM((heads, 1, amount), jnp.float32),
-            pltpu.VMEM((heads, HD + TILE, amount), jnp.float32),
+            pltpu.VMEM((amount, LANES), low),
+            pltpu.VMEM((HD + TILE, amount), low),
+            pltpu.VMEM((LANES, amount), low),
+            pltpu.VMEM((1, amount), jnp.float32),
+            pltpu.VMEM((HD + TILE, amount), jnp.float32),
             pltpu.VMEM(q.shape, low),
             pltpu.SemaphoreType.DMA((count,)),
             pltpu.SemaphoreType.DMA((count,)),
@@ -766,9 +791,9 @@
 
 
 def attend_back_kernel(
-    dims,
-    heads,
+    team,
     key_step,
+    pieces,
     lengths,
     q_all,
     kv_all,
@@ -797,126 +822,112 @@
     recv_sem,
     own_sem,
 ):
-    z, y, x, cores = dims
+    dims = team.dims
+    z = dims[0]
     me = my_place(dims)
     bounds = clip_bounds(lengths)
-    n_head, rows, width = q_all.shape
-    amount = n_head * rows
-    my_blk, my_head = blk_of(dims, me), head_of(dims, me)
-    across = peers_across(dims)
-    sides = axis_peers(dims, (1,))
-    greet(dims, me, across + ring_and_sides(dims))
+    rows = kv_all.shape[2]
+    amount = team.size * rows
+    slots = team.size // pieces
+    piece_rows = slots * rows
+    my_group, my_slot = team.group(me), team.slot(me)
+    ring_ends = sorted({along(0, 1 % z), along(0, (z - 1) % z)} - {(0, 0, 0, 0)})
+    greet(dims, me, team.others + ring_ends + team.sides)
     push = Pushes(dims, me, send_sem, recv_sem)
 
-    def to_head(src, dst, o):
-        return push(src.at[head_of(dims, shifted(dims, me, o, 1))], dst, o)
-
-    do_copies = [to_head(do_in, do_all.at[my_head], o) for o in across]
-    own_do = pltpu.make_async_copy(do_in.at[my_head], do_all.at[my_head], own_sem.at[0])
+    def to_team(src, dst, o):
+        return push(src.at[team.slot(shifted(dims, me, o, 1))], dst, o)
+
+    do_copies = [to_team(do_in, do_all.at[my_slot], o) for o in team.others]
+    own_do = pltpu.make_async_copy(do_in.at[my_slot], do_all.at[my_slot], own_sem.at[0])
     own_do.start()
     place = lax.broadcasted_iota(jnp.int32, (HD, 1), 0)
-
-    def at_head(h):
-        return slice(h * rows, (h + 1) * rows)
-
-    for h in range(n_head):
-        block = all_lanes(q_all[h], 0, width).astype(jnp.float32)
-        q_t = block.T
-        for a in range(heads):
-            queries[a, :, at_head(h)] = with_query_tail(
-                bounds,
-                a,
-                my_blk * amount + h * rows,
-                q_t[a * HD : (a + 1) * HD],
-                lse[a : a + 1, at_head(h)],
-            )
-            q_rows[a, :, at_head(h)] = (q_t[a * HD : (a + 1) * HD] * HD ** (-0.5)).astype(low)
-    for a in range(heads):
-        d_q_t[a] = jnp.zeros(d_q_t.shape[1:], jnp.float32)
+    for n in range(team.size):
+        at = slice(n * rows, (n + 1) * rows)
+        q_t = unpack_t(q_all[n])
+        queries[:, at] = with_query_tail(bounds, my_group * amount + n * rows, q_t, lse[:, at])
+        q_rows[:, at] = (q_t * HD ** (-0.5)).astype(low)
+    d_q_t[...] = jnp.zeros(d_q_t.shape, jnp.float32)
     own_do.wait()
     for copy in do_copies:
         copy.wait_recv()
-    for h in range(n_head):
-        block = all_lanes(do_all[h], 0, width).astype(jnp.float32)
-        do_t = block.T
-        for a in range(heads):
-            part = do_t[a * HD : (a + 1) * HD]
-            delta = jnp.sum(part * out_t[a * HD : (a + 1) * HD, at_head(h)], 0, keepdims=True)
-            douts[a, :, at_head(h)] = with_tail(a, part, in_three(place, -delta)).astype(low)
-            do_rows[a, :, at_head(h)] = part.astype(low)
-
-    def compute(offset, target):
-        blk = blk_of(dims, shifted(dims, me, offset, 1))
-
-        @pl.loop(0, n_head)
-        def build(h):
-            at = pl.ds(pl.multiple_of(h * rows, rows), rows)
-            block = kv_all[blk, h]
-            k_block, v_block = all_lanes(block, 0, width), all_lanes(block, width, width)
-            k_t = k_block.astype(jnp.float32).T
-            lane = lax.broadcasted_iota(jnp.int32, (1, LANES), 1)
-            for a in range(heads):
-                keys[a, at, :] = with_key_tail(bounds, a, blk * amount + h * rows, k_block)
-                keys_t[a, :, at] = k_t[a * HD : (a + 1) * HD].astype(low)
-                tail = lane - lane_of_tail(a)
-                ones = jnp.where((tail >= 0) & (tail < 3), 1.0, 0.0)
-                values[a, at, :] = jnp.where(
-                    in_head(a, 1), v_block.astype(jnp.float32), ones
-                ).astype(low)
-
-        @pl.loop(0, amount // key_step)
+    for n in range(team.size):
+        at = slice(n * rows, (n + 1) * rows)
+        do_t = unpack_t(do_all[n])
+        delta = jnp.sum(do_t * out_t[:, at], 0, keepdims=True)
+        douts[:, at] = jnp.concatenate([in_three(place, -delta), do_t], 0).astype(low)
+        do_rows[:, at] = do_t.astype(low)
+
+    def compute(offset, piece, target):
+        group = team.group(shifted(dims, me, offset, 1))
+
+        @pl.loop(0, slots)
+        def build(n):
+            at = pl.ds(pl.multiple_of(n * rows, rows), rows)
+            slot = piece * slots + n
+            block = kv_all[group, slot]
+            keys[at, :] = with_key_tail(bounds, group * amount + slot * rows, block)
+            keys_t[:, at] = block.astype(jnp.float32).T[:HD].astype(low)
+            values[at, :] = with_value_tail(block)
+
+        @pl.loop(0, piece_rows // key_step)
         def key_block(k):
             at = pl.ds(pl.multiple_of(k * key_step, key_step), key_step)
-            d_keys, d_values = [], []
-            for a in range(heads):
-                probs = jnp.exp(product(keys[a, at, :], queries[a]))
-                d_probs = product(values[a, at, :], douts[a])
+            d_key = jnp.zeros((HD, key_step), jnp.float32)
+            d_value = jnp.zeros((HD, key_step), jnp.float32)
+            for half in (slice(0, amount // 2), slice(amount // 2, amount)):
+                probs = jnp.exp(product(keys[at, :], queries[:, half]))
+                d_probs = product(values[at, :], douts[:, half])
                 d_scores = (probs * d_probs).astype(low)
-                d_values.append(against(do_rows[a], probs.astype(low)))
-                d_keys.append(against(q_rows[a], d_scores))
-                d_q_t[a] = d_q_t[a] + product(keys_t[a, :, at], d_scores)
-            target[at, :] = jnp.concatenate(d_keys + d_values, 0).T.astype(target.dtype)
+                d_value = d_value + against(do_rows[:, half], probs.astype(low))
+                d_key = d_key + against(q_rows[:, half], d_scores)
+                d_q_t[:, half] = d_q_t[:, half] + product(keys_t[:, at], d_scores)
+            target[at, :] = jnp.concatenate([d_key, d_value], 0).T.astype(target.dtype)
 
     side, ring = {}, {}
 
-    def send_sides(s):
-        for o in sides:
-            compute((z - s, o[1], 0, 0), side_out.at[s - 1, o[1] - 1])
-            side[(s, o)] = push(side_out.at[s - 1, o[1] - 1], side_in.at[s - 1, o[1] - 1], o)
-
-    def combine(s):
-        for o in sides:
-            side[(s, o)].wait_recv()
+    def send_sides(s, piece):
+        for o in team.sides:
+            target = side_out.at[s - 1, o[1] - 1, piece]
+            compute((z - s, o[1], 0, 0), piece, target)
+            side[(s, o, piece)] = push(target, side_in.at[s - 1, o[1] - 1, piece], o)
+
+    def combine(s, piece):
+        for o in team.sides:
+            side[(s, o, piece)].wait_recv()
         if s > 1:
-            ring[s - 1].wait_recv()
-
-        for h in range(n_head):
-            total = mine[(s - 1) % 2, at_head(h), :]
-            for o in sides:
-                total = total + side_in[s - 1, o[1] - 1, at_head(h), :].astype(jnp.float32)
+            ring[(s - 1, piece)].wait_recv()
+        for n in range(slots):
+            at = slice(n * rows, (n + 1) * rows)
+            total = mine[piece, at, :]
+            for o in team.sides:
+                total = total + side_in[s - 1, o[1] - 1, piece, at, :].astype(jnp.float32)
             if s > 1:
-                total = total + ring_in[s - 2, at_head(h), :].astype(jnp.float32)
+                total = total + ring_in[s - 2, piece, at, :].astype(jnp.float32)
             if s < z:
-                ring_out[s - 1, at_head(h), :] = total.astype(low)
+                ring_out[s - 1, piece, at, :] = total.astype(low)
             else:
-                d_kv_mine[h] = total.astype(low)
+                d_kv_mine[piece * slots + n] = total.astype(low)
         if s < z:
-            ring[s] = push(ring_out.at[s - 1], ring_in.at[s - 1], along(0, 1))
+            ring[(s, piece)] = push(ring_out.at[s - 1, piece], ring_in.at[s - 1, piece], along(0, 1))
 
     for s in range(1, z + 1):
-        send_sides(s)
-        if s > 1:
-            combine(s - 1)
-        compute((z - s if s < z else 0, 0, 0, 0), mine.at[(s - 1) % 2])
-    for h in range(n_head):
-        block = jnp.concatenate([d_q_t[a, :, at_head(h)] for a in range(heads)], 0) * HD ** (-0.5)
-        d_q_mine[h] = block.T.astype(low)
-    copies = [to_head(d_q_mine, d_q_out.at[my_head], o) for o in across]
-    own_q = pltpu.make_async_copy(d_q_mine.at[my_head], d_q_out.at[my_head], own_sem.at[1])
+        for piece in range(pieces):
+            send_sides(s, piece)
+            compute((z - s if s < z else 0, 0, 0, 0), piece, mine.at[piece])
+            if team.sides or s < z:
+                combine(s, piece)
+    for n in range(team.size):
+        at = slice(n * rows, (n + 1) * rows)
+        d_q_mine[n] = pack_t(d_q_t[:, at] * HD ** (-0.5)).astype(low)
+    copies = [to_team(d_q_mine, d_q_out.at[my_slot], o) for o in team.others]
+    own_q = pltpu.make_async_copy(d_q_mine.at[my_slot], d_q_out.at[my_slot], own_sem.at[1])
     own_q.start()
-    combine(z)
-    copies += [to_head(d_kv_mine, d_kv_out.at[my_head], o) for o in across]
-    own_kv = pltpu.make_async_copy(d_kv_mine.at[my_head], d_kv_out.at[my_head], own_sem.at[2])
+    if not team.sides:
+        for piece in range(pieces):
+            combine(z, piece)
+    copies += [to_team(d_kv_mine, d_kv_out.at[my_slot], o) for o in team.others]
+    own_kv = pltpu.make_async_copy(d_kv_mine.at[my_slot], d_kv_out.at[my_slot], own_sem.at[2])
     own_kv.start()
     own_q.wait()
     own_kv.wait()
@@ -925,38 +936,41 @@
     push.finish()
 
 
-def attend_back(dims, lengths, q, kv, dout, out_t, lse, heads, collective_id):
-    z, y, x, cores = dims
-    n_head, rows, width = q.shape
-    amount = n_head * rows
-    count = 3 * (n_head - 1) + z * (y - 1) + z - 1
-    block = (amount, 2 * width)
-    others = max(y - 1, 1)
+def attend_back(dims, lengths, q, kv, dout, out_t, lse, collective_id):
+    team = Team(dims)
+    z = dims[0]
+    rows = kv.shape[2]
+    amount = team.size * rows
+    pieces = 2
+    piece = (pieces, amount // pieces, LANES)
+    count = 3 * (team.size - 1) + pieces * (z + z * len(team.sides))
+    others = max(len(team.sides), 1)
+    ring_steps, side_steps = max(z - 1, 1), z if team.sides else 1
     return pl.pallas_call(
-        functools.partial(attend_back_kernel, dims, heads, 256),
+        functools.partial(attend_back_kernel, team, 256, pieces),
         out_shape=(
             jax.ShapeDtypeStruct(q.shape, low),
-            jax.ShapeDtypeStruct((n_head, rows, 2 * width), low),
+            jax.ShapeDtypeStruct(kv.shape[1:], low),
         ),
         in_specs=[SMEM_SPEC] + [VMEM_SPEC] * 5,
         out_specs=[VMEM_SPEC] * 2,
         scratch_shapes=[
             pltpu.VMEM(q.shape, low),
-            pltpu.VMEM((heads, amount, LANES), low),
-            pltpu.VMEM((heads, HD, amount), low),
-            pltpu.VMEM((heads, amount, LANES), low),
-            pltpu.VMEM((heads, LANES, amount), low),
-            pltpu.VMEM((heads, LANES, amount), low),
-            pltpu.VMEM((heads, HD, amount), jnp.float32),
-            pltpu.VMEM((heads, HD, amount), low),
-            pltpu.VMEM((heads, HD, amount), low),
-            pltpu.VMEM((z, others) + block, low),
-            pltpu.VMEM((z, others) + block, low),
-            pltpu.VMEM((max(z - 1, 1),) + block, low),
-            pltpu.VMEM((max(z - 1, 1),) + block, low),
-            pltpu.VMEM((2,) + block, jnp.float32),
+            pltpu.VMEM((amount // pieces, LANES), low),
+            pltpu.VMEM((HD, amount // pieces), low),
+            pltpu.VMEM((amount // pieces, LANES), low),
+            pltpu.VMEM((LANES, amount), low),
+            pltpu.VMEM((LANES, amount), low),
+            pltpu.VMEM((HD, amount), jnp.float32),
+            pltpu.VMEM((HD, amount), low),
+            pltpu.VMEM((HD, amount), low),
+            pltpu.VMEM((side_steps, others) + piece, low),
+            pltpu.VMEM((side_steps, others) + piece, low),
+            pltpu.VMEM((ring_steps,) + piece, low),
+            pltpu.VMEM((ring_steps,) + piece, low),
+            pltpu.VMEM(piece, jnp.float32),
             pltpu.VMEM(q.shape, low),
-            pltpu.VMEM((n_head, rows, 2 * width), low),
+            pltpu.VMEM(kv.shape[1:], low),
             pltpu.SemaphoreType.DMA((count,)),
             pltpu.SemaphoreType.DMA((count,)),
             pltpu.SemaphoreType.DMA((3,)),
@@ -1227,9 +1241,13 @@
     z_one[...] = z_zero[...] + product(o_enc[...], enc_output[...])
     h_one[...] = layer_norm(z_one[...], gains[1:2, :]).astype(low)
     projected = product(h_one[...], self_project[...]).astype(low)
-    for g in range(n_head):
-        q_self[g] = projected[:, 3 * g * width : (3 * g + 1) * width]
-        kv_self[g] = projected[:, (3 * g + 1) * width : (3 * g + 3) * width]
+    for slot, (g, a) in enumerate(heads_of(n_head, q_self.shape[0])):
+        query, key, value = (
+            projected[:, (3 * g + i) * width + a * HD : (3 * g + i) * width + (a + 1) * HD]
+            for i in range(3)
+        )
+        q_self[slot] = pack(query)
+        kv_self[slot] = jnp.concatenate([key, value], 1)
 
 
 LINE = pltpu.VMEM((4, round_up(max(D, DI), 8), LANES), jnp.float32)
@@ -1241,8 +1259,7 @@
     return begin, -(-starts[last] // shard_rows) - begin
 
 
-def encode(lengths, weights, common, inputs_t, valid, rows, n_head, shard_rows):
-    width = HEADS // n_head * HD
+def encode(lengths, weights, common, inputs_t, valid, rows, slots, n_head, shard_rows):
     begin, shards = shards_of(n_head, shard_rows, 0, 4)
     query_rows = DQ * D // LANES
     block, blocks = common_blocks(query_rows, query_rows + (LAT + 4) * D // LANES, valid)
@@ -1263,8 +1280,8 @@
             shape_of((rows, D)),
             shape_of((rows, D), jnp.float32),
             shape_of((rows, D)),
-            shape_of((n_head, rows, width)),
-            shape_of((n_head, rows, 2 * width)),
+            shape_of((slots, rows // 2, LANES)),
+            shape_of((slots, rows, LANES)),
             shape_of((8, LANES), jnp.float32),
         ],
         in_specs=[SMEM_SPEC, ANY_SPEC, ANY_SPEC, VMEM_SPEC],
@@ -1362,7 +1379,9 @@
             stage, first_row, n_head, g, (4, 5, 6, 7), (self_output, hidden_in, hidden_out, class_table), line
         )
     gain_two, gain_three = gains[2:3, :], gains[3:4, :]
-    o_low = jnp.concatenate([o_self[g] for g in range(n_head)], 1)
+    o_heads = {head: unpack(o_self[s]) for s, head in enumerate(heads_of(n_head, o_self.shape[0]))}
+    o_groups = [joined_lanes([o_heads[(g, a)] for a in range(heads)]) for g in range(n_head)]
+    o_low = jnp.concatenate(o_groups, 1)
     z_two = z_one[...] + product(o_low, self_output[...])
     h_two = layer_norm(z_two, gain_two).astype(low)
     value, bend = gelu_and_slope(product(h_two, hidden_in[...]))
@@ -1399,11 +1418,11 @@
     gain_grads[...] = jnp.concatenate([gain_two_grad, gain_three_grad], 0)
     d_two_low = d_two.astype(low)
     d_o = against(d_two_low, self_output[...]).astype(low)
-    for g in range(n_head):
-        dout[g] = d_o[:, g * width : (g + 1) * width]
+    for slot, (g, a) in enumerate(heads_of(n_head, o_self.shape[0])):
+        dout[slot] = pack(d_o[:, g * width + a * HD : g * width + (a + 1) * HD])
     for g in range(n_head):
         results = (
-            contract_first(o_self[g], d_two_low),
+            contract_first(o_groups[g], d_two_low),
             contract_first(h_two, d_pre[:, g * hidden : (g + 1) * hidden]),
             contract_first(activ[:, g * hidden : (g + 1) * hidden], d_branch),
             contract_first(decoded, dlogits[:, g * classes : (g + 1) * classes]),
@@ -1507,7 +1526,14 @@
     starts = borders(n_head)
     shared = pltpu.make_async_copy(grads_in.at[pl.ds(shards - 1, 1)], held.at[pl.ds(shards - 1, 1)], sems.at[0])
     shared.start()
-    d_projected = [jnp.concatenate([d_q_self[g], d_kv_self[g]], 1) for g in range(n_head)]
+    d_heads = {}
+    for slot, head in enumerate(heads_of(n_head, d_kv_self.shape[0])):
+        d_kv_head = d_kv_self[slot]
+        d_heads[head] = (unpack(d_q_self[slot]), d_kv_head[:, :HD], d_kv_head[:, HD:])
+    d_projected = [
+        jnp.concatenate([d_heads[(g, a)][i] for i in range(3) for a in range(heads)], 1)
+        for g in range(n_head)
+    ]
     whole = jnp.concatenate(d_projected, 1)
     d_middle, gain_one_grad = norm_pullback(
         z_one[...], gains[1:2, :], against(whole, self_project[...])
@@ -1633,7 +1659,6 @@
     n_head, n_blk = lax.axis_size("head"), lax.axis_size("blk")
     dims = grid_of(n_blk, n_head)
     rows = labels.shape[0] // n_head
-    heads_here = HEADS // n_head
     n_h, n_c = head_params.shape[0], common_params.shape[0]
     shard_rows, common_rows = n_h // LANES, -(-n_c // LANES)
     head_rows = round_up(shard_rows + 1, TILE)
@@ -1648,15 +1673,17 @@
         valid = common.shape[0]
         common = jnp.pad(common, ((0, -valid % TILE), (0, 0)))[None, None]
 
-    encoded = encode(clip_lengths, weights, common, inputs.T, valid, rows, n_head, shard_rows)
+    encoded = encode(
+        clip_lengths, weights, common, inputs.T, valid, rows, Team(dims).size, n_head, shard_rows
+    )
     gains, z_one, counts = encoded[4], encoded[11], encoded[15]
     o_self, lse_self, out_self_t, q_all, kv_all = attend(
-        dims, clip_lengths, encoded[13], encoded[14], heads_here, 1
+        dims, clip_lengths, encoded[13], encoded[14], 1
     )
     dout, d_two, tile, query_grad, gain_grads, grads = middle(
         counts, weights, common, z_one, o_self, out_queries.T, marks, gains, valid, n_head, shard_rows
     )
-    d_self = attend_back(dims, clip_lengths, q_all, kv_all, dout, out_self_t, lse_self, heads_here, 2)
+    d_self = attend_back(dims, clip_lengths, q_all, kv_all, dout, out_self_t, lse_self, 2)
     kept = encoded[:4] + encoded[5:13]
     grads, common_grad = ending(
         clip_lengths,

time: 329 us -> 327 us (level)
  no operation moved by 1% of the time
where the time goes in v3:
time: 327 us; the launch traced here: 322 us
  Pallas kernels  312 us (95%)
  other arithmetic  4.21 us (1%)
    pallas_call x1, Pallas kernels, attend(): pl.pallas_call(functools.partial(attend_kernel, team, 256, 1024), out_sha...  73.1 us
    pallas_call x1, Pallas kernels, attend_back(): pl.pallas_call(functools.partial(attend_back_kernel, team, 256, pieces),...  72.9 us
    pallas_call x1, Pallas kernels, reduce_all(): pl.pallas_call(functools.partial(reduce_kernel, dims, parts), out_shape=[...  65.3 us
    pallas_call x1, Pallas kernels, gather_all(): pl.pallas_call(functools.partial(gather_kernel, dims, parts), out_shape=[...  53.6 us
    pallas_call x1, Pallas kernels, middle(): pl.pallas_call(functools.partial(middle_kernel, n_head, shard_rows, valid...  18.1 us
    pallas_call x1, Pallas kernels, ending(): pl.pallas_call(functools.partial(ending_kernel, n_head, shard_rows, valid...  18.1 us
    pallas_call x1, Pallas kernels, encode(): pl.pallas_call(functools.partial(encode_kernel, n_head, shard_rows, valid...  10.7 us

profile of v3, /device:TPU:0, one launch (start us, length us, event | category | flops | bytes accessed | tf_op | source)
XLA Modules:
  0.0 321.5 jit_solution(16675916082531375704)
XLA Ops:
  0.6 53.6 %gather_weights.1 = (bf16[8,4,1168,128]{3,2,1,0:T(8,128)(2,1)}, bf16[8,4,240,128]{3,2,1,0:T(8,128)(2,1)}) custom-call(s32[8,128]{1,0:T(8,128)} %bitcast.30, s32[8,128]{1,0:T(8,128)} %bitcast.32, s32[8,128]{1,0:T(8,128)} %bitcast.34, f32[1160,128]{1,0:T(8,128)} %bitcast.26, f32[907,128]{1,0:T(8,128)} %bitcast.28), custom_call_target="tpu_custom_call" | custom-call | tf_op jit(solution)/shard_map/gather_weights/pallas_call | solution.py:284
  54.2 10.7 %encode.1 = (bf16[512,512]{1,0:T(8,128)(2,1)}, bf16[704,1024]{1,0:T(8,128)(2,1)}, bf16[512,512]{1,0:T(8,128)(2,1)}, bf16[512,1536]{1,0:T(8,128)(2,1)}, f32[4,512...) custom-call(s32[6]{0:T(128)} %lengths.7, ...), custom_call_target="tpu_custom_call" | custom-call | tf_op jit(solution)/shard_map/encode/pallas_call | solution.py:1267
  65.0 73.1 %attend.1 = (bf16[8,128,128]{2,1,0:T(8,128)(2,1)}, f32[1,2048]{1,0:T(1,128)}, f32[64,2048]{1,0:T(8,128)}, bf16[8,128,128]{2,1,0:T(8,128)(2,1)}, bf16[4,8,256,128]{3,2,1,0:T(8,128)(2,1)}) custom-call(s32[6]{0:T(128)} %lengths.7, bf16[8,128,128]{2,1,0:T(8,128)(2,1)} %get-tuple-element.51.q_in, bf16[8,256,128]{2,1,0:T(8,128)(2,1)} %get-tuple-element.52.kv_in), custom_call_target="tpu_custom_call" | custom-call | tf_op jit(solution)/shard_map/attend/pallas_call | solution.py:764
  138.0 18.1 %middle.1 = (bf16[8,128,128]{2,1,0:T(8,128)(2,1)}, f32[256,512]{1,0:T(8,128)}, f32[8,128]{1,0:T(8,128)}, f32[4104,128]{1,0:T(8,128)}, f32[2,512]{1,0:T(2,128)}, /*index=5*/bf16[8,4,1168,128]{3,2,1,0:T(8,128)(2,1)}) custom-call(f32[8,128]{1,0:T(8,128)} %get-tuple-element.49.counts, bf16[8,4,1168,128]{3,2,1,0:T(8,128)(2,1)} %get-tuple-element.47.weights, ...), custom_call_target="tpu_custom_call" | custom-call | tf_op jit(solution)/shard_map/middle/pallas_call | solution.py:1444
  156.2 72.9 %attend_back.1 = (bf16[8,128,128]{2,1,0:T(8,128)(2,1)}, bf16[8,256,128]{2,1,0:T(8,128)(2,1)}) custom-call(s32[6]{0:T(128)} %lengths.7, bf16[8,128,128]{2,1,0:T(8,128)(2,1)} %get-tuple-element.56.q_all, bf16[4,8,256,128]{3,2,1,0:T(8,128)(2,1)} %get-tuple-element.57.kv_all, bf16[8,128,128]{2,1,0:T(8,128)(2,1)} %get-tuple-element.58.do_in, ...), custom_call_target="tpu_custom_call" | custom-call | tf_op jit(solution)/shard_map/attend_back/pallas_call | solution.py:949
  229.1 18.1 %ending.1 = (bf16[8,4,1168,128]{3,2,1,0:T(8,128)(2,1)}, bf16[8,4,240,128]{3,2,1,0:T(8,128)(2,1)}) custom-call(s32[6]{0:T(128)} %lengths.7, bf16[8,4,1168,128]{3,2,1,0:T(8,128)(2,1)} %get-tuple-element.55.grads_in, bf16[8,128,128]{2,1,0:T(8,128)(2,1)} %get-tuple-element.61.d_q_self, ...), custom_call_target="tpu_custom_call", output_to_operand_aliasing={{0}: (1, {})} | custom-call | tf_op jit(solution)/shard_map/ending/pallas_call | solution.py:1614
  247.1 0.0 copy-start
  247.1 0.0 copy-start.2
  247.2 0.0 copy-start.3
  247.2 65.3 %reduce_gradients.1 = (f32[1160,128]{1,0:T(8,128)}, f32[907,128]{1,0:T(8,128)}, f32[8,128]{1,0:T(8,128)}) custom-call(bf16[8,4,1168,128]{3,2,1,0:T(8,128)(2,1)} %get-tuple-element.77.refs_0_, bf16[8,4,240,128]{3,2,1,0:T(8,128)(2,1)} %get-tuple-element.78.refs_1_, f32[8,128]{1,0:T(8,128)} %get-tuple-element.79.refs_2_), custom_call_target="tpu_custom_call" | custom-call | tf_op jit(solution)/shard_map/reduce_gradients/pallas_call | solution.py:469
  312.5 1.3 slice.9
  314.4 1.2 slice_bitcast_fusion
  315.7 0.0 copy-done
  315.7 0.0 copy-done.2
  315.7 0.0 copy-done.3
  315.7 0.0 copy-start.1
  315.7 0.0 copy-start.4
  315.7 0.0 copy-start.5
  315.7 0.0 copy-start.6
  315.7 2.8 fusion.7
  318.5 0.0 copy-done.1
  318.5 0.0 copy-done.4
  318.5 0.0 copy-done.5
  318.5 0.0 copy-done.6
  318.5 1.4 fusion.4
Async XLA Ops:
  247.1 68.5 %copy-start = (f32[148480]{0:T(1024)S(1)}, f32[148480]{0:T(1024)}, u32[]{:S(2)}) copy-start(f32[148480]{0:T(1024)} %param.18) | copy-start | bytes 1781764
  247.1 68.5 %copy-start.2 = (f32[148480]{0:T(1024)S(1)}, f32[148480]{0:T(1024)}, u32[]{:S(2)}) copy-start(f32[148480]{0:T(1024)} %param.19) | copy-start | bytes 1781764
  247.2 68.5 %copy-start.3 = (f32[148480]{0:T(1024)S(1)}, f32[148480]{0:T(1024)}, u32[]{:S(2)}) copy-start(f32[148480]{0:T(1024)} %param.20) | copy-start | bytes 1781764
  315.7 2.9 copy-start.1
  315.7 2.9 copy-start.4
  315.7 2.8 copy-start.5
  315.7 2.8 copy-start.6

commit v4 on v3

--- a/solution.py
+++ b/solution.py
@@ -29,6 +29,8 @@
 clip_limit = 0.05
 big_negative = -1e30
 low = jnp.bfloat16
+LOG2E = 1.4426950408889634
+SCORE_SCALE = HD ** (-0.5)
 MESH = pl.DeviceIdType.MESH
 MIB = 1 << 20
 VMEM_SPEC = pl.BlockSpec(memory_space=pltpu.VMEM)
@@ -355,10 +357,10 @@
 
 def reduce_kernel(dims, parts, *refs):
     srcs, tile = refs[:2], refs[2]
-    head_out, common_out, totals = refs[3:6]
+    head_out, common_out, losses, norm, factor = refs[3:8]
     places = len(parts) * 4
-    buffers = refs[6 : 6 + places]
-    head_sum, common_sum, shares, send_sem, recv_sem, near_tiles, far_tiles = refs[6 + places :]
+    buffers = refs[8 : 8 + places]
+    head_sum, common_sum, shares, send_sem, recv_sem, near_tiles, far_tiles = refs[8 + places :]
     sums = (head_sum, common_sum)
     me = my_place(dims)
     z, y, x, cores = dims
@@ -444,7 +446,10 @@
         common_out[k * piece : k * piece + amount] = shares[k].astype(jnp.float32)[:amount]
     for copy in far:
         copy.wait_recv()
-    totals[...] = jnp.sum(far_tiles[...], 0)
+    totals = jnp.sum(far_tiles[...], 0)[:1]
+    losses[...] = totals[:, :MODES]
+    norm[...] = jnp.sqrt(totals[:, MODES : MODES + 1])
+    factor[...] = jnp.minimum(1.0, clip_limit / norm[...])
     push.finish()
 
 
@@ -471,10 +476,12 @@
         out_shape=[
             shape_of((valid[0], LANES), jnp.float32),
             shape_of((valid[1], LANES), jnp.float32),
-            shape_of((8, LANES), jnp.float32),
+            shape_of((1, MODES), jnp.float32),
+            shape_of((1, 1), jnp.float32),
+            shape_of((1, 1), jnp.float32),
         ],
         in_specs=[VMEM_SPEC] * 3,
-        out_specs=[VMEM_SPEC] * 3,
+        out_specs=[VMEM_SPEC] * 5,
         scratch_shapes=scratch
         + [pltpu.VMEM((n, LANES), jnp.float32) for n in rows]
         + [
@@ -562,7 +569,7 @@
     tail = jnp.where(inside, 1.0, 0.0)
     if extra is not None:
         tail = tail + in_three(place - clips, -extra)
-    return jnp.concatenate([rows * HD ** (-0.5), tail], 0).astype(low)
+    return jnp.concatenate([rows * (SCORE_SCALE * LOG2E), tail], 0).astype(low)
 
 
 def pack(rows):
@@ -710,8 +717,8 @@
                 for k in range(0, amount, key_step):
                     scores = product(keys[k : k + key_step, :], query)
                     new = jnp.maximum(old, jnp.max(scores, 0, keepdims=True))
-                    probs = jnp.exp(scores - new).astype(low)
-                    total = total * jnp.exp(old - new) + product(values_t[:, k : k + key_step], probs)
+                    probs = jnp.exp2(scores - new).astype(low)
+                    total = total * jnp.exp2(old - new) + product(values_t[:, k : k + key_step], probs)
                     old = new
                 top[:, at] = old
                 accum[:, at] = total
@@ -744,7 +751,7 @@
             compute((s - 1, o[1], 0, 0))
     total = accum[HD : HD + 1, :]
     out_t[...] = accum[:HD, :] / total
-    lse[...] = top[...] + jnp.log(total)
+    lse[...] = top[...] + jnp.log(total) * LOG2E
     for n in range(team.size):
         o_mine[n] = pack_t(out_t[:, n * rows : (n + 1) * rows]).astype(low)
     o_copies = [to_team(o_mine, o_out.at[my_slot], o) for o in team.others]
@@ -846,7 +853,7 @@
         at = slice(n * rows, (n + 1) * rows)
         q_t = unpack_t(q_all[n])
         queries[:, at] = with_query_tail(bounds, my_group * amount + n * rows, q_t, lse[:, at])
-        q_rows[:, at] = (q_t * HD ** (-0.5)).astype(low)
+        q_rows[:, at] = (q_t * SCORE_SCALE).astype(low)
     d_q_t[...] = jnp.zeros(d_q_t.shape, jnp.float32)
     own_do.wait()
     for copy in do_copies:
@@ -876,7 +883,7 @@
             d_key = jnp.zeros((HD, key_step), jnp.float32)
             d_value = jnp.zeros((HD, key_step), jnp.float32)
             for half in (slice(0, amount // 2), slice(amount // 2, amount)):
-                probs = jnp.exp(product(keys[at, :], queries[:, half]))
+                probs = jnp.exp2(product(keys[at, :], queries[:, half]))
                 d_probs = product(values[at, :], douts[:, half])
                 d_scores = (probs * d_probs).astype(low)
                 d_value = d_value + against(do_rows[:, half], probs.astype(low))
@@ -919,7 +926,7 @@
                 combine(s, piece)
     for n in range(team.size):
         at = slice(n * rows, (n + 1) * rows)
-        d_q_mine[n] = pack_t(d_q_t[:, at] * HD ** (-0.5)).astype(low)
+        d_q_mine[n] = pack_t(d_q_t[:, at] * SCORE_SCALE).astype(low)
     copies = [to_team(d_q_mine, d_q_out.at[my_slot], o) for o in team.others]
     own_q = pltpu.make_async_copy(d_q_mine.at[my_slot], d_q_out.at[my_slot], own_sem.at[1])
     own_q.start()
@@ -1152,7 +1159,7 @@
 
 
 def enc_scores(q_head, keys):
-    return against(q_head, keys) * HD ** (-0.5)
+    return against(q_head, keys) * (SCORE_SCALE * LOG2E)
 
 
 def encode_kernel(
@@ -1180,6 +1187,7 @@
     q_self,
     kv_self,
     counts,
+    label_counts,
     held,
     held_common,
     held_counts,
@@ -1220,6 +1228,7 @@
     copies[2].wait()
     counted = held_counts[...].astype(jnp.float32)[:, :, shard_rows - tail : shard_rows - tail + 1]
     counts[...] = jnp.broadcast_to(jnp.sum(counted, (0, 1)), counts.shape)
+    label_counts[...] = counts[:1, :MODES]
     copies[1].wait()
     for g in range(n_head):
         load_stage(stage, held, 0, shard_rows, g)
@@ -1234,7 +1243,7 @@
         outcome = jnp.zeros((rows, width), jnp.float32)
         for here, q_head in head_lanes(g, heads, q_enc[...]):
             scores = enc_scores(q_head, keys)
-            probs = jnp.exp(scores - jnp.max(scores, 1, keepdims=True))
+            probs = jnp.exp2(scores - jnp.max(scores, 1, keepdims=True))
             total = jnp.sum(probs, 1, keepdims=True)
             outcome = jnp.where(here, product(probs.astype(low), values) / total, outcome)
         o_enc[:, g * width : (g + 1) * width] = outcome.astype(low)
@@ -1283,9 +1292,10 @@
             shape_of((slots, rows // 2, LANES)),
             shape_of((slots, rows, LANES)),
             shape_of((8, LANES), jnp.float32),
+            shape_of((1, MODES), jnp.float32),
         ],
         in_specs=[SMEM_SPEC, ANY_SPEC, ANY_SPEC, VMEM_SPEC],
-        out_specs=[VMEM_SPEC] * 16,
+        out_specs=[VMEM_SPEC] * 17,
         scratch_shapes=[
             pltpu.VMEM((shards,) + weights.shape[1:], low),
             pltpu.VMEM((blocks,) + common.shape[1:], low),
@@ -1396,7 +1406,7 @@
     lane = lax.broadcasted_iota(jnp.int32, (rows, C), 1).astype(jnp.float32)
     is_target = jnp.where(lane == label, 1.0, 0.0)
     row_top = jnp.max(logits, 1, keepdims=True)
-    row_lse = row_top + jnp.log(jnp.sum(jnp.exp(logits - row_top), 1, keepdims=True))
+    row_lse = row_top + jnp.log(jnp.sum(jnp.exp2((logits - row_top) * LOG2E), 1, keepdims=True))
     loss = row_lse - jnp.sum(is_target * logits, 1, keepdims=True)
     weight = jnp.zeros((rows, 1), jnp.float32)
     place = lax.broadcasted_iota(jnp.int32, (1, LANES), 1)
@@ -1406,7 +1416,7 @@
         weight = weight + member / jnp.maximum(counts[0:1, m : m + 1], 1.0)
         losses = losses + jnp.where(place == m, jnp.sum(loss * member, 0, keepdims=True), 0.0)
     tile[...] = jnp.broadcast_to(losses, tile.shape)
-    dlogits = (weight * (jnp.exp(logits - row_lse) - is_target)).astype(low)
+    dlogits = (weight * (jnp.exp2((logits - row_lse) * LOG2E) - is_target)).astype(low)
     d_decoded = against(dlogits, class_table[...])
     matrix_into(query_grad, 0, product(queries_t, d_decoded.astype(low)), line)
     d_three, gain_three_grad = norm_pullback(z_three, gain_three, d_decoded)
@@ -1551,7 +1561,7 @@
             head_lanes(g, heads, q_enc[...]), head_lanes(g, heads, d_o)
         ):
             scores = enc_scores(keys, q_head)
-            probs = jnp.exp(scores - jnp.max(scores, 0, keepdims=True))
+            probs = jnp.exp2(scores - jnp.max(scores, 0, keepdims=True))
             probs = probs / jnp.sum(probs, 0, keepdims=True)
             d_probs = against(values, do_head)
             delta = jnp.sum(probs * d_probs, 0, keepdims=True)
@@ -1559,8 +1569,8 @@
             d_value = d_value + product(probs.astype(low), do_head)
             d_key = d_key + product(d_scores, q_head)
             d_query = jnp.where(here, contract_first(d_scores, keys), d_query)
-        d_q[:, g * width : (g + 1) * width] = (d_query * HD ** (-0.5)).astype(low)
-        d_kv[:, 2 * g * width : (2 * g + 1) * width] = (d_key * HD ** (-0.5)).astype(low)
+        d_q[:, g * width : (g + 1) * width] = (d_query * SCORE_SCALE).astype(low)
+        d_kv[:, 2 * g * width : (2 * g + 1) * width] = (d_key * SCORE_SCALE).astype(low)
         d_kv[:, (2 * g + 1) * width : (2 * g + 2) * width] = d_value.astype(low)
     d_middle, gain_zero_grad = norm_pullback(
         z_zero[...], gains[0:1, :], against(d_q[...], enc_query[...])
@@ -1702,12 +1712,11 @@
         common_grad = common_grad[0, 0, :valid].reshape(n_blk, n_c)
         common_grad = jnp.pad(common_grad, ((0, 0), (0, n_head * piece_rows * LANES - n_c)))
         common_grad = common_grad.reshape(n_blk, n_head, piece_rows, LANES)
-    head_share, common_share, totals = reduce_all(
+    head_share, common_share, loss_sums, clip_norm, factor = reduce_all(
         dims, (grads, common_grad), (shard_rows, common_rows), tile, 3
     )
-    label_counts, loss_sums = counts[0, :MODES], totals[0, :MODES]
-    clip_norm = jnp.sqrt(totals[0, MODES])
-    factor = jnp.minimum(1.0, clip_limit / clip_norm)
+    label_counts, loss_sums = encoded[16].reshape(MODES), loss_sums.reshape(MODES)
+    clip_norm, factor = clip_norm.reshape(()), factor.reshape(())
     head_share, common_share = head_share.reshape(-1), common_share.reshape(-1)[:n_c]
     head_out = adam_step(head_params, head_first, head_second, head_share * factor)
     common_out = adam_step(common_params, common_first, common_second, common_share * factor)

time: 327 us -> 326 us (level)
  no operation moved by 1% of the time
where the time goes in v4:
time: 326 us; the launch traced here: 320 us
  Pallas kernels  311 us (95%)
  other arithmetic  5.47 us (2%)
    pallas_call x1, Pallas kernels, attend(): pl.pallas_call(functools.partial(attend_kernel, team, 256, 1024), out_sha...  73 us
    pallas_call x1, Pallas kernels, attend_back(): pl.pallas_call(functools.partial(attend_back_kernel, team, 256, pieces),...  72.7 us
    pallas_call x1, Pallas kernels, reduce_all(): pl.pallas_call(functools.partial(reduce_kernel, dims, parts), out_shape=[...  65.4 us
    pallas_call x1, Pallas kernels, gather_all(): pl.pallas_call(functools.partial(gather_kernel, dims, parts), out_shape=[...  53.6 us
    pallas_call x1, Pallas kernels, middle(): pl.pallas_call(functools.partial(middle_kernel, n_head, shard_rows, valid...  18.1 us
    pallas_call x1, Pallas kernels, ending(): pl.pallas_call(functools.partial(ending_kernel, n_head, shard_rows, valid...  18 us
    pallas_call x1, Pallas kernels, encode(): pl.pallas_call(functools.partial(encode_kernel, n_head, shard_rows, valid...  10.6 us

profile of v4, /device:TPU:0, one launch (start us, length us, event | category | flops | bytes accessed | tf_op | source)
XLA Modules:
  0.0 320.4 jit_solution(12884874195586780103)
XLA Ops:
  0.6 53.6 %gather_weights.1 = (bf16[8,4,1168,128]{3,2,1,0:T(8,128)(2,1)}, bf16[8,4,240,128]{3,2,1,0:T(8,128)(2,1)}) custom-call(s32[8,128]{1,0:T(8,128)} %bitcast.29, s32[8,128]{1,0:T(8,128)} %bitcast.31, s32[8,128]{1,0:T(8,128)} %bitcast.33, f32[1160,128]{1,0:T(8,128)} %bitcast.25, f32[907,128]{1,0:T(8,128)} %bitcast.27), custom_call_target="tpu_custom_call" | custom-call | tf_op jit(solution)/shard_map/gather_weights/pallas_call | solution.py:286
  54.2 10.6 %encode.1 = (bf16[512,512]{1,0:T(8,128)(2,1)}, bf16[704,1024]{1,0:T(8,128)(2,1)}, bf16[512,512]{1,0:T(8,128)(2,1)}, bf16[512,1536]{1,0:T(8,128)(2,1)}, f32[4,512...) custom-call(s32[6]{0:T(128)} %lengths.7, ...), custom_call_target="tpu_custom_call" | custom-call | tf_op jit(solution)/shard_map/encode/pallas_call | solution.py:1276
  64.9 73.0 %attend.1 = (bf16[8,128,128]{2,1,0:T(8,128)(2,1)}, f32[1,2048]{1,0:T(1,128)}, f32[64,2048]{1,0:T(8,128)}, bf16[8,128,128]{2,1,0:T(8,128)(2,1)}, bf16[4,8,256,128]{3,2,1,0:T(8,128)(2,1)}) custom-call(s32[6]{0:T(128)} %lengths.7, bf16[8,128,128]{2,1,0:T(8,128)(2,1)} %get-tuple-element.54.q_in, bf16[8,256,128]{2,1,0:T(8,128)(2,1)} %get-tuple-element.55.kv_in), custom_call_target="tpu_custom_call" | custom-call | tf_op jit(solution)/shard_map/attend/pallas_call | solution.py:771
  137.9 18.1 %middle.1 = (bf16[8,128,128]{2,1,0:T(8,128)(2,1)}, f32[256,512]{1,0:T(8,128)}, f32[8,128]{1,0:T(8,128)}, f32[4104,128]{1,0:T(8,128)}, f32[2,512]{1,0:T(2,128)}, /*index=5*/bf16[8,4,1168,128]{3,2,1,0:T(8,128)(2,1)}) custom-call(f32[8,128]{1,0:T(8,128)} %get-tuple-element.52.counts, bf16[8,4,1168,128]{3,2,1,0:T(8,128)(2,1)} %get-tuple-element.50.weights, ...), custom_call_target="tpu_custom_call" | custom-call | tf_op jit(solution)/shard_map/middle/pallas_call | solution.py:1454
  156.0 72.7 %attend_back.1 = (bf16[8,128,128]{2,1,0:T(8,128)(2,1)}, bf16[8,256,128]{2,1,0:T(8,128)(2,1)}) custom-call(s32[6]{0:T(128)} %lengths.7, bf16[8,128,128]{2,1,0:T(8,128)(2,1)} %get-tuple-element.59.q_all, bf16[4,8,256,128]{3,2,1,0:T(8,128)(2,1)} %get-tuple-element.60.kv_all, bf16[8,128,128]{2,1,0:T(8,128)(2,1)} %get-tuple-element.61.do_in, ...), custom_call_target="tpu_custom_call" | custom-call | tf_op jit(solution)/shard_map/attend_back/pallas_call | solution.py:956
  228.7 18.0 %ending.1 = (bf16[8,4,1168,128]{3,2,1,0:T(8,128)(2,1)}, bf16[8,4,240,128]{3,2,1,0:T(8,128)(2,1)}) custom-call(s32[6]{0:T(128)} %lengths.7, bf16[8,4,1168,128]{3,2,1,0:T(8,128)(2,1)} %get-tuple-element.58.grads_in, bf16[8,128,128]{2,1,0:T(8,128)(2,1)} %get-tuple-element.64.d_q_self, ...), custom_call_target="tpu_custom_call", output_to_operand_aliasing={{0}: (1, {})} | custom-call | tf_op jit(solution)/shard_map/ending/pallas_call | solution.py:1624
  246.7 0.0 copy-start
  246.7 0.0 copy-start.2
  246.7 0.0 copy-start.3
  246.8 65.4 %reduce_gradients.1 = (f32[1160,128]{1,0:T(8,128)}, f32[907,128]{1,0:T(8,128)}, f32[1,3]{1,0:T(1,128)}, f32[1,1]{1,0:T(1,128)}, f32[1,1]{1,0:T(1,128)}) custom-call(bf16[8,4,1168,128]{3,2,1,0:T(8,128)(2,1)} %get-tuple-element.80.refs_0_, bf16[8,4,240,128]{3,2,1,0:T(8,128)(2,1)} %get-tuple-element.81.refs_1_, f32[8,128]{1,0:T(8,128)} %get-tuple-element.82.refs_2_), custom_call_target="tpu_custom_call" | custom-call | tf_op jit(solution)/shard_map/reduce_gradients/pallas_call | solution.py:474
  312.1 0.0 copy-done
  312.1 0.0 copy-done.2
  312.1 0.0 copy-done.3
  312.2 0.0 copy-start.1
  312.2 0.0 copy-start.4
  312.2 0.0 copy-start.5
  312.2 0.0 copy-start.6
  312.2 3.4 %fusion.7 = (bf16[148480]{0:T(1024)(128)(2,1)}, f32[148480]{0:T(1024)}, f32[148480]{0:T(1024)}, f32[148480]{0:T(1024)}) fusion(f32[148480]{0:T(1024)S(1)} %copy-done, f32[1160,128]{1,0:T(8,128)} %get-tuple-element.83, f32[]{:T(128)} %bitcast.7, f32[148480]{0:T(1024)S(1)} %copy-done.2, f32[148480]{0:T(1024)S(1)} %copy-done.3), kind=kLoop, calls=%fused_computation.11 | loop fusion | flops 2524160 | bytes 4454404 | tf_op jit(solution)/shard_map/convert_element_type | solution.py:1652
  315.6 0.0 copy-start.7
  315.6 0.0 copy-done.1
  315.7 0.0 copy-done.4
  315.7 0.0 copy-done.5
  315.7 0.0 copy-done.6
  315.7 2.0 fusion.4
  317.7 0.0 copy-done.7
  317.7 0.5 copy.27
Async XLA Ops:
  246.7 65.4 %copy-start = (f32[148480]{0:T(1024)S(1)}, f32[148480]{0:T(1024)}, u32[]{:S(2)}) copy-start(f32[148480]{0:T(1024)} %param.18) | copy-start | bytes 1781764
  246.7 65.4 %copy-start.2 = (f32[148480]{0:T(1024)S(1)}, f32[148480]{0:T(1024)}, u32[]{:S(2)}) copy-start(f32[148480]{0:T(1024)} %param.19) | copy-start | bytes 1781764
  246.7 65.4 %copy-start.3 = (f32[148480]{0:T(1024)S(1)}, f32[148480]{0:T(1024)}, u32[]{:S(2)}) copy-start(f32[148480]{0:T(1024)} %param.20) | copy-start | bytes 1781764
  312.2 3.5 %copy-start.1 = (f32[116096]{0:T(1024)S(1)}, f32[116096]{0:T(1024)}, u32[]{:S(2)}) copy-start(f32[116096]{0:T(1024)} %param.21) | copy-start | bytes 1393156
  312.2 3.5 %copy-start.4 = (f32[116096]{0:T(1024)S(1)}, f32[116096]{0:T(1024)}, u32[]{:S(2)}) copy-start(f32[116096]{0:T(1024)} %param.22) | copy-start | bytes 1393156
  312.2 3.5 %copy-start.5 = (f32[116096]{0:T(1024)S(1)}, f32[116096]{0:T(1024)}, u32[]{:S(2)}) copy-start(f32[116096]{0:T(1024)} %param.23) | copy-start | bytes 1393156
  312.2 3.5 %copy-start.6 = (f32[907,128]{1,0:T(8,128)S(1)}, f32[907,128]{1,0:T(8,128)}, u32[]{:S(2)}) copy-start(f32[907,128]{1,0:T(8,128)} %get-tuple-element.85) | copy-start | bytes 1393156
  315.6 2.1 copy-start.7

commit v5 on v4

--- a/solution.py
+++ b/solution.py
@@ -643,6 +643,7 @@
     team,
     query_step,
     key_step,
+    pieces,
     lengths,
     q_in,
     kv_in,
@@ -667,6 +668,7 @@
     bounds = clip_bounds(lengths)
     rows = kv_in.shape[1]
     amount = team.size * rows
+    slots = team.size // pieces
     my_group, my_slot = team.group(me), team.slot(me)
     ring_ends = sorted({along(0, 1 % z), along(0, (z - 1) % z)} - {(0, 0, 0, 0)})
     greet(dims, me, team.others + ring_ends + team.sides)
@@ -686,26 +688,22 @@
     def group_at(offset):
         return team.group(shifted(dims, me, offset, -1))
 
-    def send_piece(o):
-        block = kv_all.at[my_group, team.slot(shifted(dims, me, o, -1))]
-        if z > 1:
-            ring.setdefault(1, []).append(push(block, block, along(0, 1)))
-
-    def send_on(s):
-        block = kv_all.at[group_at(along(0, s))]
-        if 0 < s < z - 1:
-            ring[s + 1] = [push(block, block, along(0, 1))]
+    def send_on(s, piece):
+        block = kv_all.at[group_at(along(0, s)), pl.ds(piece * slots, slots)]
+        if s < z - 1:
+            ring[(s + 1, piece)] = push(block, block, along(0, 1))
         for o in team.sides:
-            side[(s, o)] = push(block, block, o)
-
-    def compute(offset):
+            side[(s, o, piece)] = push(block, block, o)
+
+    def compute(offset, piece):
         group = group_at(offset)
 
-        @pl.loop(0, team.size)
+        @pl.loop(0, slots)
         def build(n):
             at = pl.ds(pl.multiple_of(n * rows, rows), rows)
-            block = kv_all[group, n]
-            keys[at, :] = with_key_tail(bounds, group * amount + n * rows, block)
+            slot = piece * slots + n
+            block = kv_all[group, slot]
+            keys[at, :] = with_key_tail(bounds, group * amount + slot * rows, block)
             values_t[:HD, at] = block.astype(jnp.float32).T[HD:].astype(low)
 
         @pl.loop(0, amount // (2 * query_step))
@@ -714,24 +712,23 @@
                 at = pl.ds(pl.multiple_of((2 * n + half) * query_step, query_step), query_step)
                 query = queries[:, at]
                 old, total = top[:, at], accum[:, at]
-                for k in range(0, amount, key_step):
+                for k in range(0, slots * rows, key_step):
                     scores = product(keys[k : k + key_step, :], query)
                     new = jnp.maximum(old, jnp.max(scores, 0, keepdims=True))
-                    probs = jnp.exp2(scores - new).astype(low)
+                    probs = jnp.exp2((scores - new).astype(low))
                     total = total * jnp.exp2(old - new) + product(values_t[:, k : k + key_step], probs)
                     old = new
                 top[:, at] = old
                 accum[:, at] = total
 
-    values_t[HD:, :] = jnp.ones((TILE, amount), low)
+    values_t[HD:, :] = jnp.ones((TILE, slots * rows), low)
     top[...] = jnp.full(top.shape, -1e38, jnp.float32)
     accum[...] = jnp.zeros(accum.shape, jnp.float32)
     own_kv.wait()
-    send_piece((0, 0, 0, 0))
     for o in team.others:
         kv_copies[o].wait_recv()
-        send_piece(o)
-    send_on(0)
+    for piece in range(pieces):
+        send_on(0, piece)
     own_q.wait()
     for copy in q_copies:
         copy.wait_recv()
@@ -739,16 +736,15 @@
         queries[:, n * rows : (n + 1) * rows] = with_query_tail(
             bounds, my_group * amount + n * rows, unpack_t(q_all[n]), None
         )
-    compute((0, 0, 0, 0))
-    for s in range(1, z + 1):
-        if s < z:
-            for copy in ring[s]:
-                copy.wait_recv()
-            send_on(s)
-            compute(along(0, s))
-        for o in team.sides:
-            side[(s - 1, o)].wait_recv()
-            compute((s - 1, o[1], 0, 0))
+    for s in range(z):
+        for piece in range(pieces):
+            compute(along(0, s), piece)
+            if s < z - 1:
+                ring[(s + 1, piece)].wait_recv()
+                send_on(s + 1, piece)
+            for o in team.sides:
+                side[(s, o, piece)].wait_recv()
+                compute((s, o[1], 0, 0), piece)
     total = accum[HD : HD + 1, :]
     out_t[...] = accum[:HD, :] / total
     lse[...] = top[...] + jnp.log(total) * LOG2E
@@ -767,9 +763,10 @@
     team = Team(dims)
     z = dims[0]
     amount = team.size * kv.shape[1]
-    count = 3 * (team.size - 1) + team.size + z + z * len(team.sides)
+    pieces = 2
+    count = 3 * (team.size - 1) + pieces * (z + z * len(team.sides))
     return pl.pallas_call(
-        functools.partial(attend_kernel, team, 256, 1024),
+        functools.partial(attend_kernel, team, 256, min(1024, amount // pieces), pieces),
         out_shape=(
             jax.ShapeDtypeStruct(q.shape, low),
             jax.ShapeDtypeStruct((1, amount), jnp.float32),
@@ -780,8 +777,8 @@
         in_specs=[SMEM_SPEC, VMEM_SPEC, VMEM_SPEC],
         out_specs=[VMEM_SPEC] * 5,
         scratch_shapes=[
-            pltpu.VMEM((amount, LANES), low),
-            pltpu.VMEM((HD + TILE, amount), low),
+            pltpu.VMEM((amount // pieces, LANES), low),
+            pltpu.VMEM((HD + TILE, amount // pieces), low),
             pltpu.VMEM((LANES, amount), low),
             pltpu.VMEM((1, amount), jnp.float32),
             pltpu.VMEM((HD + TILE, amount), jnp.float32),
@@ -883,10 +880,10 @@
             d_key = jnp.zeros((HD, key_step), jnp.float32)
             d_value = jnp.zeros((HD, key_step), jnp.float32)
             for half in (slice(0, amount // 2), slice(amount // 2, amount)):
-                probs = jnp.exp2(product(keys[at, :], queries[:, half]))
+                probs = jnp.exp2(product(keys[at, :], queries[:, half]).astype(low))
                 d_probs = product(values[at, :], douts[:, half])
-                d_scores = (probs * d_probs).astype(low)
-                d_value = d_value + against(do_rows[:, half], probs.astype(low))
+                d_scores = (probs.astype(jnp.float32) * d_probs).astype(low)
+                d_value = d_value + against(do_rows[:, half], probs)
                 d_key = d_key + against(q_rows[:, half], d_scores)
                 d_q_t[:, half] = d_q_t[:, half] + product(keys_t[:, at], d_scores)
             target[at, :] = jnp.concatenate([d_key, d_value], 0).T.astype(target.dtype)
@@ -1243,9 +1240,9 @@
         outcome = jnp.zeros((rows, width), jnp.float32)
         for here, q_head in head_lanes(g, heads, q_enc[...]):
             scores = enc_scores(q_head, keys)
-            probs = jnp.exp2(scores - jnp.max(scores, 1, keepdims=True))
-            total = jnp.sum(probs, 1, keepdims=True)
-            outcome = jnp.where(here, product(probs.astype(low), values) / total, outcome)
+            probs = jnp.exp2((scores - jnp.max(scores, 1, keepdims=True)).astype(low))
+            total = jnp.sum(probs.astype(jnp.float32), 1, keepdims=True)
+            outcome = jnp.where(here, product(probs, values) / total, outcome)
         o_enc[:, g * width : (g + 1) * width] = outcome.astype(low)
     z_one[...] = z_zero[...] + product(o_enc[...], enc_output[...])
     h_one[...] = layer_norm(z_one[...], gains[1:2, :]).astype(low)
@@ -1561,7 +1558,8 @@
             head_lanes(g, heads, q_enc[...]), head_lanes(g, heads, d_o)
         ):
             scores = enc_scores(keys, q_head)
-            probs = jnp.exp2(scores - jnp.max(scores, 0, keepdims=True))
+            probs = jnp.exp2((scores - jnp.max(scores, 0, keepdims=True)).astype(low))
+            probs = probs.astype(jnp.float32)
             probs = probs / jnp.sum(probs, 0, keepdims=True)
             d_probs = against(values, do_head)
             delta = jnp.sum(probs * d_probs, 0, keepdims=True)

time: 326 us -> 325 us (level)
  no operation moved by 1% of the time
where the time goes in v5:
time: 325 us; the launch traced here: 319 us
  Pallas kernels  310 us (95%)
  other arithmetic  5.47 us (2%)
    pallas_call x1, Pallas kernels, attend_back(): pl.pallas_call(functools.partial(attend_back_kernel, team, 256, pieces),...  73.5 us
    pallas_call x1, Pallas kernels, attend(): pl.pallas_call(functools.partial(attend_kernel, team, 256, min(1024, amou...  70.5 us
    pallas_call x1, Pallas kernels, reduce_all(): pl.pallas_call(functools.partial(reduce_kernel, dims, parts), out_shape=[...  65.5 us
    pallas_call x1, Pallas kernels, gather_all(): pl.pallas_call(functools.partial(gather_kernel, dims, parts), out_shape=[...  53.6 us
    pallas_call x1, Pallas kernels, ending(): pl.pallas_call(functools.partial(ending_kernel, n_head, shard_rows, valid...  18.2 us
    pallas_call x1, Pallas kernels, middle(): pl.pallas_call(functools.partial(middle_kernel, n_head, shard_rows, valid...  18.1 us
    pallas_call x1, Pallas kernels, encode(): pl.pallas_call(functools.partial(encode_kernel, n_head, shard_rows, valid...  10.7 us

profile of v5, /device:TPU:0, one launch (start us, length us, event | category | flops | bytes accessed | tf_op | source)
XLA Modules:
  0.0 319.1 jit_solution(2804597636814462218)
XLA Ops:
  0.6 53.6 %gather_weights.1 = (bf16[8,4,1168,128]{3,2,1,0:T(8,128)(2,1)}, bf16[8,4,240,128]{3,2,1,0:T(8,128)(2,1)}) custom-call(s32[8,128]{1,0:T(8,128)} %bitcast.29, s32[8,128]{1,0:T(8,128)} %bitcast.31, s32[8,128]{1,0:T(8,128)} %bitcast.33, f32[1160,128]{1,0:T(8,128)} %bitcast.25, f32[907,128]{1,0:T(8,128)} %bitcast.27), custom_call_target="tpu_custom_call" | custom-call | tf_op jit(solution)/shard_map/gather_weights/pallas_call | solution.py:286
  54.2 10.7 %encode.1 = (bf16[512,512]{1,0:T(8,128)(2,1)}, bf16[704,1024]{1,0:T(8,128)(2,1)}, bf16[512,512]{1,0:T(8,128)(2,1)}, bf16[512,1536]{1,0:T(8,128)(2,1)}, f32[4,512...) custom-call(s32[6]{0:T(128)} %lengths.7, ...), custom_call_target="tpu_custom_call" | custom-call | tf_op jit(solution)/shard_map/encode/pallas_call | solution.py:1273
  64.9 70.5 %attend.1 = (bf16[8,128,128]{2,1,0:T(8,128)(2,1)}, f32[1,2048]{1,0:T(1,128)}, f32[64,2048]{1,0:T(8,128)}, bf16[8,128,128]{2,1,0:T(8,128)(2,1)}, bf16[4,8,256,128]{3,2,1,0:T(8,128)(2,1)}) custom-call(s32[6]{0:T(128)} %lengths.7, bf16[8,128,128]{2,1,0:T(8,128)(2,1)} %get-tuple-element.54.q_in, bf16[8,256,128]{2,1,0:T(8,128)(2,1)} %get-tuple-element.55.kv_in), custom_call_target="tpu_custom_call" | custom-call | tf_op jit(solution)/shard_map/attend/pallas_call | solution.py:768
  135.4 18.1 %middle.1 = (bf16[8,128,128]{2,1,0:T(8,128)(2,1)}, f32[256,512]{1,0:T(8,128)}, f32[8,128]{1,0:T(8,128)}, f32[4104,128]{1,0:T(8,128)}, f32[2,512]{1,0:T(2,128)}, /*index=5*/bf16[8,4,1168,128]{3,2,1,0:T(8,128)(2,1)}) custom-call(f32[8,128]{1,0:T(8,128)} %get-tuple-element.52.counts, bf16[8,4,1168,128]{3,2,1,0:T(8,128)(2,1)} %get-tuple-element.50.weights, ...), custom_call_target="tpu_custom_call" | custom-call | tf_op jit(solution)/shard_map/middle/pallas_call | solution.py:1451
  153.5 73.5 %attend_back.1 = (bf16[8,128,128]{2,1,0:T(8,128)(2,1)}, bf16[8,256,128]{2,1,0:T(8,128)(2,1)}) custom-call(s32[6]{0:T(128)} %lengths.7, bf16[8,128,128]{2,1,0:T(8,128)(2,1)} %get-tuple-element.59.q_all, bf16[4,8,256,128]{3,2,1,0:T(8,128)(2,1)} %get-tuple-element.60.kv_all, bf16[8,128,128]{2,1,0:T(8,128)(2,1)} %get-tuple-element.61.do_in, ...), custom_call_target="tpu_custom_call" | custom-call | tf_op jit(solution)/shard_map/attend_back/pallas_call | solution.py:953
  227.1 18.2 %ending.1 = (bf16[8,4,1168,128]{3,2,1,0:T(8,128)(2,1)}, bf16[8,4,240,128]{3,2,1,0:T(8,128)(2,1)}) custom-call(s32[6]{0:T(128)} %lengths.7, bf16[8,4,1168,128]{3,2,1,0:T(8,128)(2,1)} %get-tuple-element.58.grads_in, bf16[8,128,128]{2,1,0:T(8,128)(2,1)} %get-tuple-element.64.d_q_self, ...), custom_call_target="tpu_custom_call", output_to_operand_aliasing={{0}: (1, {})} | custom-call | tf_op jit(solution)/shard_map/ending/pallas_call | solution.py:1622
  245.3 0.0 copy-start
  245.3 0.0 copy-start.2
  245.3 0.0 copy-start.3
  245.3 65.5 %reduce_gradients.1 = (f32[1160,128]{1,0:T(8,128)}, f32[907,128]{1,0:T(8,128)}, f32[1,3]{1,0:T(1,128)}, f32[1,1]{1,0:T(1,128)}, f32[1,1]{1,0:T(1,128)}) custom-call(bf16[8,4,1168,128]{3,2,1,0:T(8,128)(2,1)} %get-tuple-element.80.refs_0_, bf16[8,4,240,128]{3,2,1,0:T(8,128)(2,1)} %get-tuple-element.81.refs_1_, f32[8,128]{1,0:T(8,128)} %get-tuple-element.82.refs_2_), custom_call_target="tpu_custom_call" | custom-call | tf_op jit(solution)/shard_map/reduce_gradients/pallas_call | solution.py:474
  310.8 0.0 copy-done
  310.8 0.0 copy-done.2
  310.9 0.0 copy-done.3
  310.9 0.0 copy-start.1
  310.9 0.0 copy-start.4
  310.9 0.0 copy-start.5
  310.9 0.0 copy-start.6
  310.9 3.4 %fusion.7 = (bf16[148480]{0:T(1024)(128)(2,1)}, f32[148480]{0:T(1024)}, f32[148480]{0:T(1024)}, f32[148480]{0:T(1024)}) fusion(f32[148480]{0:T(1024)S(1)} %copy-done, f32[1160,128]{1,0:T(8,128)} %get-tuple-element.83, f32[]{:T(128)} %bitcast.7, f32[148480]{0:T(1024)S(1)} %copy-done.2, f32[148480]{0:T(1024)S(1)} %copy-done.3), kind=kLoop, calls=%fused_computation.11 | loop fusion | flops 2524160 | bytes 4454404 | tf_op jit(solution)/shard_map/convert_element_type | solution.py:1650
  314.4 0.0 copy-start.7
  314.4 0.0 copy-done.1
  314.4 0.0 copy-done.4
  314.4 0.0 copy-done.5
  314.4 0.0 copy-done.6
  314.4 2.0 fusion.4
  316.4 0.0 copy-done.7
  316.4 0.5 copy.27
Async XLA Ops:
  245.3 65.6 %copy-start = (f32[148480]{0:T(1024)S(1)}, f32[148480]{0:T(1024)}, u32[]{:S(2)}) copy-start(f32[148480]{0:T(1024)} %param.18) | copy-start | bytes 1781764
  245.3 65.6 %copy-start.2 = (f32[148480]{0:T(1024)S(1)}, f32[148480]{0:T(1024)}, u32[]{:S(2)}) copy-start(f32[148480]{0:T(1024)} %param.19) | copy-start | bytes 1781764
  245.3 65.6 %copy-start.3 = (f32[148480]{0:T(1024)S(1)}, f32[148480]{0:T(1024)}, u32[]{:S(2)}) copy-start(f32[148480]{0:T(1024)} %param.20) | copy-start | bytes 1781764
  310.9 3.5 %copy-start.1 = (f32[116096]{0:T(1024)S(1)}, f32[116096]{0:T(1024)}, u32[]{:S(2)}) copy-start(f32[116096]{0:T(1024)} %param.21) | copy-start | bytes 1393156
  310.9 3.5 %copy-start.4 = (f32[116096]{0:T(1024)S(1)}, f32[116096]{0:T(1024)}, u32[]{:S(2)}) copy-start(f32[116096]{0:T(1024)} %param.22) | copy-start | bytes 1393156
  310.9 3.5 %copy-start.5 = (f32[116096]{0:T(1024)S(1)}, f32[116096]{0:T(1024)}, u32[]{:S(2)}) copy-start(f32[116096]{0:T(1024)} %param.23) | copy-start | bytes 1393156
  310.9 3.5 %copy-start.6 = (f32[907,128]{1,0:T(8,128)S(1)}, f32[907,128]{1,0:T(8,128)}, u32[]{:S(2)}) copy-start(f32[907,128]{1,0:T(8,128)} %get-tuple-element.85) | copy-start | bytes 1393156
  314.4 2.1 copy-start.7

commit v6 on v5

--- a/solution.py
+++ b/solution.py
@@ -657,6 +657,10 @@
     queries,
     top,
     accum,
+    even_scores,
+    odd_scores,
+    even_top,
+    odd_top,
     o_mine,
     send_sem,
     recv_sem,
@@ -706,20 +710,39 @@
             keys[at, :] = with_key_tail(bounds, group * amount + slot * rows, block)
             values_t[:HD, at] = block.astype(jnp.float32).T[HD:].astype(low)
 
-        @pl.loop(0, amount // (2 * query_step))
+        def both(now, now_scores, now_top, later, later_scores, later_top):
+            if now is not None:
+                at = tile(now)
+                old = top[:, at]
+                new = jnp.maximum(old, jnp.max(now_top[...], 0, keepdims=True))
+                top[:, at] = new
+                total = accum[:, at] * jnp.exp2(old - new)
+            query = queries[:, tile(later)]
+            highest = jnp.full(later_top.shape, -1e38, jnp.float32)
+            for k in range(0, slots * rows, key_step):
+                scores = product(keys[k : k + key_step, :], query)
+                later_scores[k : k + key_step, :] = scores
+                highest = jnp.maximum(
+                    highest, jnp.max(scores.reshape(key_step // 8, 8, query_step), 0)
+                )
+                if now is not None:
+                    probs = jnp.exp2((now_scores[k : k + key_step, :] - new).astype(low))
+                    total = total + product(values_t[:, k : k + key_step], probs)
+            later_top[...] = highest
+            if now is not None:
+                accum[:, at] = total
+
+        def tile(n):
+            return pl.ds(pl.multiple_of(n * query_step, query_step), query_step)
+
+        tiles = amount // query_step
+        both(None, None, None, 0, even_scores, even_top)
+
+        @pl.loop(0, tiles // 2)
         def query_blocks(n):
-            for half in range(2):
-                at = pl.ds(pl.multiple_of((2 * n + half) * query_step, query_step), query_step)
-                query = queries[:, at]
-                old, total = top[:, at], accum[:, at]
-                for k in range(0, slots * rows, key_step):
-                    scores = product(keys[k : k + key_step, :], query)
-                    new = jnp.maximum(old, jnp.max(scores, 0, keepdims=True))
-                    probs = jnp.exp2((scores - new).astype(low))
-                    total = total * jnp.exp2(old - new) + product(values_t[:, k : k + key_step], probs)
-                    old = new
-                top[:, at] = old
-                accum[:, at] = total
+            last = jnp.minimum(2 * n + 2, tiles - 1)
+            both(2 * n, even_scores, even_top, 2 * n + 1, odd_scores, odd_top)
+            both(2 * n + 1, odd_scores, odd_top, last, even_scores, even_top)
 
     values_t[HD:, :] = jnp.ones((TILE, slots * rows), low)
     top[...] = jnp.full(top.shape, -1e38, jnp.float32)
@@ -763,10 +786,10 @@
     team = Team(dims)
     z = dims[0]
     amount = team.size * kv.shape[1]
-    pieces = 2
+    pieces, query_step = 2, 256
     count = 3 * (team.size - 1) + pieces * (z + z * len(team.sides))
     return pl.pallas_call(
-        functools.partial(attend_kernel, team, 256, min(1024, amount // pieces), pieces),
+        functools.partial(attend_kernel, team, query_step, 256, pieces),
         out_shape=(
             jax.ShapeDtypeStruct(q.shape, low),
             jax.ShapeDtypeStruct((1, amount), jnp.float32),
@@ -782,6 +805,10 @@
             pltpu.VMEM((LANES, amount), low),
             pltpu.VMEM((1, amount), jnp.float32),
             pltpu.VMEM((HD + TILE, amount), jnp.float32),
+            pltpu.VMEM((amount // pieces, query_step), jnp.float32),
+            pltpu.VMEM((amount // pieces, query_step), jnp.float32),
+            pltpu.VMEM((8, query_step), jnp.float32),
+            pltpu.VMEM((8, query_step), jnp.float32),
             pltpu.VMEM(q.shape, low),
             pltpu.SemaphoreType.DMA((count,)),
             pltpu.SemaphoreType.DMA((count,)),
@@ -797,6 +824,7 @@
 def attend_back_kernel(
     team,
     key_step,
+    query_step,
     pieces,
     lengths,
     q_all,
@@ -815,6 +843,10 @@
     d_q_t,
     q_rows,
     do_rows,
+    even_probs,
+    odd_probs,
+    even_scores,
+    odd_scores,
     side_out,
     side_in,
     ring_out,
@@ -850,7 +882,7 @@
         at = slice(n * rows, (n + 1) * rows)
         q_t = unpack_t(q_all[n])
         queries[:, at] = with_query_tail(bounds, my_group * amount + n * rows, q_t, lse[:, at])
-        q_rows[:, at] = (q_t * SCORE_SCALE).astype(low)
+        q_rows[at, :] = jnp.concatenate([q_t * SCORE_SCALE, jnp.zeros_like(q_t)], 0).T.astype(low)
     d_q_t[...] = jnp.zeros(d_q_t.shape, jnp.float32)
     own_do.wait()
     for copy in do_copies:
@@ -860,7 +892,7 @@
         do_t = unpack_t(do_all[n])
         delta = jnp.sum(do_t * out_t[:, at], 0, keepdims=True)
         douts[:, at] = jnp.concatenate([in_three(place, -delta), do_t], 0).astype(low)
-        do_rows[:, at] = do_t.astype(low)
+        do_rows[at, :] = jnp.concatenate([jnp.zeros_like(do_t), do_t], 0).T.astype(low)
 
     def compute(offset, piece, target):
         group = team.group(shifted(dims, me, offset, 1))
@@ -874,19 +906,36 @@
             keys_t[:, at] = block.astype(jnp.float32).T[:HD].astype(low)
             values[at, :] = with_value_tail(block)
 
-        @pl.loop(0, piece_rows // key_step)
-        def key_block(k):
-            at = pl.ds(pl.multiple_of(k * key_step, key_step), key_step)
-            d_key = jnp.zeros((HD, key_step), jnp.float32)
-            d_value = jnp.zeros((HD, key_step), jnp.float32)
-            for half in (slice(0, amount // 2), slice(amount // 2, amount)):
-                probs = jnp.exp2(product(keys[at, :], queries[:, half]).astype(low))
-                d_probs = product(values[at, :], douts[:, half])
-                d_scores = (probs.astype(jnp.float32) * d_probs).astype(low)
-                d_value = d_value + against(do_rows[:, half], probs)
-                d_key = d_key + against(q_rows[:, half], d_scores)
-                d_q_t[:, half] = d_q_t[:, half] + product(keys_t[:, at], d_scores)
-            target[at, :] = jnp.concatenate([d_key, d_value], 0).T.astype(target.dtype)
+        def both(now, now_probs, now_scores, later, later_probs, later_scores):
+            at = rows_of(later)
+            if now is not None:
+                now_at = rows_of(now)
+                total = jnp.zeros((key_step, LANES), jnp.float32)
+            for first in range(0, amount, query_step):
+                part = slice(first, first + query_step)
+                probs = jnp.exp2(product(keys[at, :], queries[:, part]).astype(low))
+                d_probs = product(values[at, :], douts[:, part])
+                later_probs[:, part] = probs
+                later_scores[:, part] = (probs.astype(jnp.float32) * d_probs).astype(low)
+                if now is not None:
+                    d_scores = now_scores[:, part]
+                    total = total + product(now_probs[:, part], do_rows[part, :])
+                    total = total + product(d_scores, q_rows[part, :])
+                    d_q_t[:, part] = d_q_t[:, part] + product(keys_t[:, now_at], d_scores)
+            if now is not None:
+                target[now_at, :] = total.astype(target.dtype)
+
+        def rows_of(k):
+            return pl.ds(pl.multiple_of(k * key_step, key_step), key_step)
+
+        steps = piece_rows // key_step
+        both(None, None, None, 0, even_probs, even_scores)
+
+        @pl.loop(0, steps // 2)
+        def key_blocks(k):
+            last = jnp.minimum(2 * k + 2, steps - 1)
+            both(2 * k, even_probs, even_scores, 2 * k + 1, odd_probs, odd_scores)
+            both(2 * k + 1, odd_probs, odd_scores, last, even_probs, even_scores)
 
     side, ring = {}, {}
 
@@ -945,13 +994,13 @@
     z = dims[0]
     rows = kv.shape[2]
     amount = team.size * rows
-    pieces = 2
+    pieces, key_step = 2, 256
     piece = (pieces, amount // pieces, LANES)
     count = 3 * (team.size - 1) + pieces * (z + z * len(team.sides))
     others = max(len(team.sides), 1)
     ring_steps, side_steps = max(z - 1, 1), z if team.sides else 1
     return pl.pallas_call(
-        functools.partial(attend_back_kernel, team, 256, pieces),
+        functools.partial(attend_back_kernel, team, key_step, 512, pieces),
         out_shape=(
             jax.ShapeDtypeStruct(q.shape, low),
             jax.ShapeDtypeStruct(kv.shape[1:], low),
@@ -966,8 +1015,12 @@
             pltpu.VMEM((LANES, amount), low),
             pltpu.VMEM((LANES, amount), low),
             pltpu.VMEM((HD, amount), jnp.float32),
-            pltpu.VMEM((HD, amount), low),
-            pltpu.VMEM((HD, amount), low),
+            pltpu.VMEM((amount, LANES), low),
+            pltpu.VMEM((amount, LANES), low),
+            pltpu.VMEM((key_step, amount), low),
+            pltpu.VMEM((key_step, amount), low),
+            pltpu.VMEM((key_step, amount), low),
+            pltpu.VMEM((key_step, amount), low),
             pltpu.VMEM((side_steps, others) + piece, low),
             pltpu.VMEM((side_steps, others) + piece, low),
             pltpu.VMEM((ring_steps,) + piece, low),

time: 325 us -> 313 us (0.963)
  Pallas kernels: 310 us -> 299 us
    pallas_call x2, Pallas kernels: 144 us -> 133 us  [the longest x1 69.9 us: attend_back(): pl.pallas_call(functools.partial(attend_back_kernel, team, key_step, 512,...]
where the time goes in v6:
time: 313 us; the launch traced here: 307 us
  Pallas kernels  299 us (96%)
  other arithmetic  5.47 us (2%)
    pallas_call x1, Pallas kernels, attend_back(): pl.pallas_call(functools.partial(attend_back_kernel, team, key_step, 512,...  69.9 us
    pallas_call x1, Pallas kernels, reduce_all(): pl.pallas_call(functools.partial(reduce_kernel, dims, parts), out_shape=[...  65.4 us
    pallas_call x1, Pallas kernels, attend(): pl.pallas_call(functools.partial(attend_kernel, team, query_step, 256, pi...  62.8 us
    pallas_call x1, Pallas kernels, gather_all(): pl.pallas_call(functools.partial(gather_kernel, dims, parts), out_shape=[...  53.6 us
    pallas_call x1, Pallas kernels, ending(): pl.pallas_call(functools.partial(ending_kernel, n_head, shard_rows, valid...  18.2 us
    pallas_call x1, Pallas kernels, middle(): pl.pallas_call(functools.partial(middle_kernel, n_head, shard_rows, valid...  18.1 us
    pallas_call x1, Pallas kernels, encode(): pl.pallas_call(functools.partial(encode_kernel, n_head, shard_rows, valid...  10.7 us

profile of v6, /device:TPU:0, one launch (start us, length us, event | category | flops | bytes accessed | tf_op | source)
XLA Modules:
  0.0 307.4 jit_solution(5644575832352513605)
XLA Ops:
  0.6 53.6 %gather_weights.1 = (bf16[8,4,1168,128]{3,2,1,0:T(8,128)(2,1)}, bf16[8,4,240,128]{3,2,1,0:T(8,128)(2,1)}) custom-call(s32[8,128]{1,0:T(8,128)} %bitcast.29, s32[8,128]{1,0:T(8,128)} %bitcast.31, s32[8,128]{1,0:T(8,128)} %bitcast.33, f32[1160,128]{1,0:T(8,128)} %bitcast.25, f32[907,128]{1,0:T(8,128)} %bitcast.27), custom_call_target="tpu_custom_call" | custom-call | tf_op jit(solution)/shard_map/gather_weights/pallas_call | solution.py:286
  54.2 10.7 %encode.1 = (bf16[512,512]{1,0:T(8,128)(2,1)}, bf16[704,1024]{1,0:T(8,128)(2,1)}, bf16[512,512]{1,0:T(8,128)(2,1)}, bf16[512,1536]{1,0:T(8,128)(2,1)}, f32[4,512...) custom-call(s32[6]{0:T(128)} %lengths.7, ...), custom_call_target="tpu_custom_call" | custom-call | tf_op jit(solution)/shard_map/encode/pallas_call | solution.py:1326
  64.9 62.8 %attend.1 = (bf16[8,128,128]{2,1,0:T(8,128)(2,1)}, f32[1,2048]{1,0:T(1,128)}, f32[64,2048]{1,0:T(8,128)}, bf16[8,128,128]{2,1,0:T(8,128)(2,1)}, bf16[4,8,256,128]{3,2,1,0:T(8,128)(2,1)}) custom-call(s32[6]{0:T(128)} %lengths.7, bf16[8,128,128]{2,1,0:T(8,128)(2,1)} %get-tuple-element.54.q_in, bf16[8,256,128]{2,1,0:T(8,128)(2,1)} %get-tuple-element.55.kv_in), custom_call_target="tpu_custom_call" | custom-call | tf_op jit(solution)/shard_map/attend/pallas_call | solution.py:791
  127.7 18.1 %middle.1 = (bf16[8,128,128]{2,1,0:T(8,128)(2,1)}, f32[256,512]{1,0:T(8,128)}, f32[8,128]{1,0:T(8,128)}, f32[4104,128]{1,0:T(8,128)}, f32[2,512]{1,0:T(2,128)}, /*index=5*/bf16[8,4,1168,128]{3,2,1,0:T(8,128)(2,1)}) custom-call(f32[8,128]{1,0:T(8,128)} %get-tuple-element.52.counts, bf16[8,4,1168,128]{3,2,1,0:T(8,128)(2,1)} %get-tuple-element.50.weights, ...), custom_call_target="tpu_custom_call" | custom-call | tf_op jit(solution)/shard_map/middle/pallas_call | solution.py:1504
  145.9 69.9 %attend_back.1 = (bf16[8,128,128]{2,1,0:T(8,128)(2,1)}, bf16[8,256,128]{2,1,0:T(8,128)(2,1)}) custom-call(s32[6]{0:T(128)} %lengths.7, bf16[8,128,128]{2,1,0:T(8,128)(2,1)} %get-tuple-element.59.q_all, bf16[4,8,256,128]{3,2,1,0:T(8,128)(2,1)} %get-tuple-element.60.kv_all, bf16[8,128,128]{2,1,0:T(8,128)(2,1)} %get-tuple-element.61.do_in, ...), custom_call_target="tpu_custom_call" | custom-call | tf_op jit(solution)/shard_map/attend_back/pallas_call | solution.py:1002
  215.7 18.2 %ending.1 = (bf16[8,4,1168,128]{3,2,1,0:T(8,128)(2,1)}, bf16[8,4,240,128]{3,2,1,0:T(8,128)(2,1)}) custom-call(s32[6]{0:T(128)} %lengths.7, bf16[8,4,1168,128]{3,2,1,0:T(8,128)(2,1)} %get-tuple-element.58.grads_in, bf16[8,128,128]{2,1,0:T(8,128)(2,1)} %get-tuple-element.64.d_q_self, ...), custom_call_target="tpu_custom_call", output_to_operand_aliasing={{0}: (1, {})} | custom-call | tf_op jit(solution)/shard_map/ending/pallas_call | solution.py:1675
  233.9 0.0 copy-start
  233.9 0.0 copy-start.2
  233.9 0.0 copy-start.3
  234.0 65.4 %reduce_gradients.1 = (f32[1160,128]{1,0:T(8,128)}, f32[907,128]{1,0:T(8,128)}, f32[1,3]{1,0:T(1,128)}, f32[1,1]{1,0:T(1,128)}, f32[1,1]{1,0:T(1,128)}) custom-call(bf16[8,4,1168,128]{3,2,1,0:T(8,128)(2,1)} %get-tuple-element.80.refs_0_, bf16[8,4,240,128]{3,2,1,0:T(8,128)(2,1)} %get-tuple-element.81.refs_1_, f32[8,128]{1,0:T(8,128)} %get-tuple-element.82.refs_2_), custom_call_target="tpu_custom_call" | custom-call | tf_op jit(solution)/shard_map/reduce_gradients/pallas_call | solution.py:474
  299.3 0.0 copy-done
  299.3 0.0 copy-done.2
  299.4 0.0 copy-done.3
  299.4 0.0 copy-start.1
  299.4 0.0 copy-start.4
  299.4 0.0 copy-start.5
  299.4 0.0 copy-start.6
  299.4 3.4 %fusion.7 = (bf16[148480]{0:T(1024)(128)(2,1)}, f32[148480]{0:T(1024)}, f32[148480]{0:T(1024)}, f32[148480]{0:T(1024)}) fusion(f32[148480]{0:T(1024)S(1)} %copy-done, f32[1160,128]{1,0:T(8,128)} %get-tuple-element.83, f32[]{:T(128)} %bitcast.7, f32[148480]{0:T(1024)S(1)} %copy-done.2, f32[148480]{0:T(1024)S(1)} %copy-done.3), kind=kLoop, calls=%fused_computation.11 | loop fusion | flops 2524160 | bytes 4454404 | tf_op jit(solution)/shard_map/convert_element_type | solution.py:1703
  302.9 0.0 copy-start.7
  302.9 0.0 copy-done.1
  302.9 0.0 copy-done.4
  302.9 0.0 copy-done.5
  302.9 0.0 copy-done.6
  302.9 2.0 fusion.4
  304.9 0.0 copy-done.7
  304.9 0.5 copy.27
Async XLA Ops:
  233.9 65.4 %copy-start = (f32[148480]{0:T(1024)S(1)}, f32[148480]{0:T(1024)}, u32[]{:S(2)}) copy-start(f32[148480]{0:T(1024)} %param.18) | copy-start | bytes 1781764
  233.9 65.4 %copy-start.2 = (f32[148480]{0:T(1024)S(1)}, f32[148480]{0:T(1024)}, u32[]{:S(2)}) copy-start(f32[148480]{0:T(1024)} %param.19) | copy-start | bytes 1781764
  233.9 65.4 %copy-start.3 = (f32[148480]{0:T(1024)S(1)}, f32[148480]{0:T(1024)}, u32[]{:S(2)}) copy-start(f32[148480]{0:T(1024)} %param.20) | copy-start | bytes 1781764
  299.4 3.5 %copy-start.1 = (f32[116096]{0:T(1024)S(1)}, f32[116096]{0:T(1024)}, u32[]{:S(2)}) copy-start(f32[116096]{0:T(1024)} %param.21) | copy-start | bytes 1393156
  299.4 3.5 %copy-start.4 = (f32[116096]{0:T(1024)S(1)}, f32[116096]{0:T(1024)}, u32[]{:S(2)}) copy-start(f32[116096]{0:T(1024)} %param.22) | copy-start | bytes 1393156
  299.4 3.5 %copy-start.5 = (f32[116096]{0:T(1024)S(1)}, f32[116096]{0:T(1024)}, u32[]{:S(2)}) copy-start(f32[116096]{0:T(1024)} %param.23) | copy-start | bytes 1393156
  299.4 3.5 %copy-start.6 = (f32[907,128]{1,0:T(8,128)S(1)}, f32[907,128]{1,0:T(8,128)}, u32[]{:S(2)}) copy-start(f32[907,128]{1,0:T(8,128)} %get-tuple-element.85) | copy-start | bytes 1393156
  302.9 2.1 copy-start.7

commit v7 on v5

--- a/solution.py
+++ b/solution.py
@@ -652,11 +652,17 @@
     out_t,
     q_all,
     kv_all,
-    keys,
-    values_t,
+    even_keys,
+    even_values_t,
+    odd_keys,
+    odd_values_t,
     queries,
     top,
     accum,
+    even_scores,
+    odd_scores,
+    even_top,
+    odd_top,
     o_mine,
     send_sem,
     recv_sem,
@@ -695,8 +701,42 @@
         for o in team.sides:
             side[(s, o, piece)] = push(block, block, o)
 
+    def both(now, later):
+        if now is not None:
+            n, unused, now_values, now_scores, now_top = now
+            at = tile(n)
+            old = top[:, at]
+            new = jnp.maximum(old, jnp.max(now_top[...], 0, keepdims=True))
+            top[:, at] = new
+            total = accum[:, at] * jnp.exp2(old - new)
+        if later is not None:
+            n, later_keys, unused, later_scores, later_top = later
+            query = queries[:, tile(n)]
+            highest = jnp.full(later_top.shape, -1e38, jnp.float32)
+        for k in range(0, slots * rows, key_step):
+            if later is not None:
+                scores = product(later_keys[k : k + key_step, :], query)
+                later_scores[k : k + key_step, :] = scores
+                highest = jnp.maximum(
+                    highest, jnp.max(scores.reshape(key_step // 8, 8, query_step), 0)
+                )
+            if now is not None:
+                probs = jnp.exp2((now_scores[k : k + key_step, :] - new).astype(low))
+                total = total + product(now_values[:, k : k + key_step], probs)
+        if later is not None:
+            later_top[...] = highest
+        if now is not None:
+            accum[:, at] = total
+
+    def tile(n):
+        return pl.ds(pl.multiple_of(n * query_step, query_step), query_step)
+
+    computed, pending = [], [None]
+
     def compute(offset, piece):
         group = group_at(offset)
+        keys, values_t = sides_of_keys[len(computed) % 2]
+        computed.append(offset)
 
         @pl.loop(0, slots)
         def build(n):
@@ -706,22 +746,26 @@
             keys[at, :] = with_key_tail(bounds, group * amount + slot * rows, block)
             values_t[:HD, at] = block.astype(jnp.float32).T[HD:].astype(low)
 
-        @pl.loop(0, amount // (2 * query_step))
+        def even(n):
+            return (n, keys, values_t, even_scores, even_top)
+
+        def odd(n):
+            return (n, keys, values_t, odd_scores, odd_top)
+
+        tiles = amount // query_step
+        both(pending[0], even(0))
+
+        @pl.loop(0, tiles // 2 - 1)
         def query_blocks(n):
-            for half in range(2):
-                at = pl.ds(pl.multiple_of((2 * n + half) * query_step, query_step), query_step)
-                query = queries[:, at]
-                old, total = top[:, at], accum[:, at]
-                for k in range(0, slots * rows, key_step):
-                    scores = product(keys[k : k + key_step, :], query)
-                    new = jnp.maximum(old, jnp.max(scores, 0, keepdims=True))
-                    probs = jnp.exp2((scores - new).astype(low))
-                    total = total * jnp.exp2(old - new) + product(values_t[:, k : k + key_step], probs)
-                    old = new
-                top[:, at] = old
-                accum[:, at] = total
-
-    values_t[HD:, :] = jnp.ones((TILE, slots * rows), low)
+            both(even(2 * n), odd(2 * n + 1))
+            both(odd(2 * n + 1), even(2 * n + 2))
+
+        both(even(tiles - 2), odd(tiles - 1))
+        pending[0] = odd(tiles - 1)
+
+    sides_of_keys = ((even_keys, even_values_t), (odd_keys, odd_values_t))
+    for unused, values_t in sides_of_keys:
+        values_t[HD:, :] = jnp.ones((TILE, slots * rows), low)
     top[...] = jnp.full(top.shape, -1e38, jnp.float32)
     accum[...] = jnp.zeros(accum.shape, jnp.float32)
     own_kv.wait()
@@ -745,6 +789,7 @@
             for o in team.sides:
                 side[(s, o, piece)].wait_recv()
                 compute((s, o[1], 0, 0), piece)
+    both(pending[0], None)
     total = accum[HD : HD + 1, :]
     out_t[...] = accum[:HD, :] / total
     lse[...] = top[...] + jnp.log(total) * LOG2E
@@ -763,10 +808,10 @@
     team = Team(dims)
     z = dims[0]
     amount = team.size * kv.shape[1]
-    pieces = 2
+    pieces, query_step = 2, 256
     count = 3 * (team.size - 1) + pieces * (z + z * len(team.sides))
     return pl.pallas_call(
-        functools.partial(attend_kernel, team, 256, min(1024, amount // pieces), pieces),
+        functools.partial(attend_kernel, team, query_step, 256, pieces),
         out_shape=(
             jax.ShapeDtypeStruct(q.shape, low),
             jax.ShapeDtypeStruct((1, amount), jnp.float32),
@@ -779,9 +824,15 @@
         scratch_shapes=[
             pltpu.VMEM((amount // pieces, LANES), low),
             pltpu.VMEM((HD + TILE, amount // pieces), low),
+            pltpu.VMEM((amount // pieces, LANES), low),
+            pltpu.VMEM((HD + TILE, amount // pieces), low),
             pltpu.VMEM((LANES, amount), low),
             pltpu.VMEM((1, amount), jnp.float32),
             pltpu.VMEM((HD + TILE, amount), jnp.float32),
+            pltpu.VMEM((amount // pieces, query_step), jnp.float32),
+            pltpu.VMEM((amount // pieces, query_step), jnp.float32),
+            pltpu.VMEM((8, query_step), jnp.float32),
+            pltpu.VMEM((8, query_step), jnp.float32),
             pltpu.VMEM(q.shape, low),
             pltpu.SemaphoreType.DMA((count,)),
             pltpu.SemaphoreType.DMA((count,)),
@@ -797,6 +848,7 @@
 def attend_back_kernel(
     team,
     key_step,
+    query_step,
     pieces,
     lengths,
     q_all,
@@ -807,14 +859,21 @@
     d_q_out,
     d_kv_out,
     do_all,
-    keys,
-    keys_t,
-    values,
+    even_keys_t,
+    even_values_t,
+    even_rows,
+    odd_keys_t,
+    odd_values_t,
+    odd_rows,
     queries,
     douts,
-    d_q_t,
+    d_q_sum,
     q_rows,
     do_rows,
+    even_probs,
+    odd_probs,
+    even_scores,
+    odd_scores,
     side_out,
     side_in,
     ring_out,
@@ -849,9 +908,10 @@
     for n in range(team.size):
         at = slice(n * rows, (n + 1) * rows)
         q_t = unpack_t(q_all[n])
-        queries[:, at] = with_query_tail(bounds, my_group * amount + n * rows, q_t, lse[:, at])
+        extended = with_query_tail(bounds, my_group * amount + n * rows, q_t, lse[:, at])
+        queries[at, :] = extended.astype(jnp.float32).T.astype(low)
         q_rows[:, at] = (q_t * SCORE_SCALE).astype(low)
-    d_q_t[...] = jnp.zeros(d_q_t.shape, jnp.float32)
+    d_q_sum[...] = jnp.zeros(d_q_sum.shape, jnp.float32)
     own_do.wait()
     for copy in do_copies:
         copy.wait_recv()
@@ -859,42 +919,84 @@
         at = slice(n * rows, (n + 1) * rows)
         do_t = unpack_t(do_all[n])
         delta = jnp.sum(do_t * out_t[:, at], 0, keepdims=True)
-        douts[:, at] = jnp.concatenate([in_three(place, -delta), do_t], 0).astype(low)
+        extended = jnp.concatenate([in_three(place, -delta), do_t], 0).astype(low)
+        douts[at, :] = extended.astype(jnp.float32).T.astype(low)
         do_rows[:, at] = do_t.astype(low)
 
-    def compute(offset, piece, target):
+    def both(now, later):
+        if now is not None:
+            n, (unused, unused, now_rows), now_probs, now_scores, target = now
+            now_at = rows_of(n)
+        if later is not None:
+            n, (keys_t, values_t, unused), later_probs, later_scores, unused = later
+            at = rows_of(n)
+        for first in range(0, amount, query_step):
+            part = slice(first, first + query_step)
+            if later is not None:
+                probs = jnp.exp2(product(queries[part, :], keys_t[:, at]).astype(low))
+                d_probs = product(douts[part, :], values_t[:, at])
+                later_probs[part, :] = probs
+                later_scores[part, :] = (probs.astype(jnp.float32) * d_probs).astype(low)
+            if now is not None:
+                if first == 0:
+                    d_value = product(do_rows[...], now_probs[...])
+                if first == amount // 2:
+                    d_key = product(q_rows[...], now_scores[...])
+                d_q_sum[part, :] = d_q_sum[part, :] + product(now_scores[part, :], now_rows[now_at, :])
+        if now is not None:
+            target[now_at, :] = jnp.concatenate([d_key, d_value], 0).T.astype(target.dtype)
+
+    def rows_of(k):
+        return slice(k * key_step, (k + 1) * key_step)
+
+    computed, pending = [], []
+
+    def flush(later=None):
+        if pending:
+            now, after = pending.pop()
+            both(now, later)
+            after()
+        elif later is not None:
+            both(None, later)
+
+    def compute(offset, piece, target, after):
         group = team.group(shifted(dims, me, offset, 1))
+        keys = sides_of_keys[len(computed) % 2]
+        computed.append(offset)
 
         @pl.loop(0, slots)
         def build(n):
             at = pl.ds(pl.multiple_of(n * rows, rows), rows)
             slot = piece * slots + n
             block = kv_all[group, slot]
-            keys[at, :] = with_key_tail(bounds, group * amount + slot * rows, block)
-            keys_t[:, at] = block.astype(jnp.float32).T[:HD].astype(low)
-            values[at, :] = with_value_tail(block)
-
-        @pl.loop(0, piece_rows // key_step)
-        def key_block(k):
-            at = pl.ds(pl.multiple_of(k * key_step, key_step), key_step)
-            d_key = jnp.zeros((HD, key_step), jnp.float32)
-            d_value = jnp.zeros((HD, key_step), jnp.float32)
-            for half in (slice(0, amount // 2), slice(amount // 2, amount)):
-                probs = jnp.exp2(product(keys[at, :], queries[:, half]).astype(low))
-                d_probs = product(values[at, :], douts[:, half])
-                d_scores = (probs.astype(jnp.float32) * d_probs).astype(low)
-                d_value = d_value + against(do_rows[:, half], probs)
-                d_key = d_key + against(q_rows[:, half], d_scores)
-                d_q_t[:, half] = d_q_t[:, half] + product(keys_t[:, at], d_scores)
-            target[at, :] = jnp.concatenate([d_key, d_value], 0).T.astype(target.dtype)
-
+            extended = with_key_tail(bounds, group * amount + slot * rows, block)
+            keys[0][:, at] = extended.astype(jnp.float32).T.astype(low)
+            keys[1][:, at] = with_value_tail(block).astype(jnp.float32).T.astype(low)
+            keys[2][at, :] = block
+
+        steps = [
+            (k, keys) + ((odd_probs, odd_scores) if k % 2 else (even_probs, even_scores)) + (target,)
+            for k in range(piece_rows // key_step)
+        ]
+        flush(steps[0])
+        for now, later in zip(steps[:-1], steps[1:]):
+            both(now, later)
+        pending.append((steps[-1], after))
+
+    sides_of_keys = (
+        (even_keys_t, even_values_t, even_rows),
+        (odd_keys_t, odd_values_t, odd_rows),
+    )
     side, ring = {}, {}
 
     def send_sides(s, piece):
         for o in team.sides:
             target = side_out.at[s - 1, o[1] - 1, piece]
-            compute((z - s, o[1], 0, 0), piece, target)
-            side[(s, o, piece)] = push(target, side_in.at[s - 1, o[1] - 1, piece], o)
+
+            def send(o=o, target=target):
+                side[(s, o, piece)] = push(target, side_in.at[s - 1, o[1] - 1, piece], o)
+
+            compute((z - s, o[1], 0, 0), piece, target, send)
 
     def combine(s, piece):
         for o in team.sides:
@@ -918,18 +1020,17 @@
     for s in range(1, z + 1):
         for piece in range(pieces):
             send_sides(s, piece)
-            compute((z - s if s < z else 0, 0, 0, 0), piece, mine.at[piece])
-            if team.sides or s < z:
-                combine(s, piece)
+            after = functools.partial(combine, s, piece) if s < z else lambda: None
+            compute((z - s if s < z else 0, 0, 0, 0), piece, mine.at[piece], after)
+    flush()
     for n in range(team.size):
         at = slice(n * rows, (n + 1) * rows)
-        d_q_mine[n] = pack_t(d_q_t[:, at] * SCORE_SCALE).astype(low)
+        d_q_mine[n] = pack(d_q_sum[at, :HD] * SCORE_SCALE).astype(low)
     copies = [to_team(d_q_mine, d_q_out.at[my_slot], o) for o in team.others]
     own_q = pltpu.make_async_copy(d_q_mine.at[my_slot], d_q_out.at[my_slot], own_sem.at[1])
     own_q.start()
-    if not team.sides:
-        for piece in range(pieces):
-            combine(z, piece)
+    for piece in range(pieces):
+        combine(z, piece)
     copies += [to_team(d_kv_mine, d_kv_out.at[my_slot], o) for o in team.others]
     own_kv = pltpu.make_async_copy(d_kv_mine.at[my_slot], d_kv_out.at[my_slot], own_sem.at[2])
     own_kv.start()
@@ -945,13 +1046,13 @@
     z = dims[0]
     rows = kv.shape[2]
     amount = team.size * rows
-    pieces = 2
+    pieces, key_step = 2, 256
     piece = (pieces, amount // pieces, LANES)
     count = 3 * (team.size - 1) + pieces * (z + z * len(team.sides))
     others = max(len(team.sides), 1)
     ring_steps, side_steps = max(z - 1, 1), z if team.sides else 1
     return pl.pallas_call(
-        functools.partial(attend_back_kernel, team, 256, pieces),
+        functools.partial(attend_back_kernel, team, key_step, 512, pieces),
         out_shape=(
             jax.ShapeDtypeStruct(q.shape, low),
             jax.ShapeDtypeStruct(kv.shape[1:], low),
@@ -960,14 +1061,21 @@
         out_specs=[VMEM_SPEC] * 2,
         scratch_shapes=[
             pltpu.VMEM(q.shape, low),
+            pltpu.VMEM((LANES, amount // pieces), low),
+            pltpu.VMEM((LANES, amount // pieces), low),
             pltpu.VMEM((amount // pieces, LANES), low),
-            pltpu.VMEM((HD, amount // pieces), low),
+            pltpu.VMEM((LANES, amount // pieces), low),
+            pltpu.VMEM((LANES, amount // pieces), low),
             pltpu.VMEM((amount // pieces, LANES), low),
-            pltpu.VMEM((LANES, amount), low),
-            pltpu.VMEM((LANES, amount), low),
-            pltpu.VMEM((HD, amount), jnp.float32),
+            pltpu.VMEM((amount, LANES), low),
+            pltpu.VMEM((amount, LANES), low),
+            pltpu.VMEM((amount, LANES), jnp.float32),
             pltpu.VMEM((HD, amount), low),
             pltpu.VMEM((HD, amount), low),
+            pltpu.VMEM((amount, key_step), low),
+            pltpu.VMEM((amount, key_step), low),
+            pltpu.VMEM((amount, key_step), low),
+            pltpu.VMEM((amount, key_step), low),
             pltpu.VMEM((side_steps, others) + piece, low),
             pltpu.VMEM((side_steps, others) + piece, low),
             pltpu.VMEM((ring_steps,) + piece, low),

time: 325 us -> 309 us (0.951)
  Pallas kernels: 310 us -> 295 us
    pallas_call x2, Pallas kernels: 144 us -> 129 us  [the longest x1 66.2 us: attend_back(): pl.pallas_call(functools.partial(attend_back_kernel, team, key_step, 512,...]
where the time goes in v7:
time: 309 us; the launch traced here: 304 us
  Pallas kernels  295 us (95%)
  other arithmetic  5.47 us (2%)
    pallas_call x1, Pallas kernels, attend_back(): pl.pallas_call(functools.partial(attend_back_kernel, team, key_step, 512,...  66.2 us
    pallas_call x1, Pallas kernels, reduce_all(): pl.pallas_call(functools.partial(reduce_kernel, dims, parts), out_shape=[...  65.4 us
    pallas_call x1, Pallas kernels, attend(): pl.pallas_call(functools.partial(attend_kernel, team, query_step, 256, pi...  62.5 us
    pallas_call x1, Pallas kernels, gather_all(): pl.pallas_call(functools.partial(gather_kernel, dims, parts), out_shape=[...  53.6 us
    pallas_call x1, Pallas kernels, ending(): pl.pallas_call(functools.partial(ending_kernel, n_head, shard_rows, valid...  18.2 us
    pallas_call x1, Pallas kernels, middle(): pl.pallas_call(functools.partial(middle_kernel, n_head, shard_rows, valid...  18.1 us
    pallas_call x1, Pallas kernels, encode(): pl.pallas_call(functools.partial(encode_kernel, n_head, shard_rows, valid...  10.6 us

profile of v7, /device:TPU:0, one launch (start us, length us, event | category | flops | bytes accessed | tf_op | source)
XLA Modules:
  0.0 303.7 jit_solution(11606991055775268642)
XLA Ops:
  0.6 53.6 %gather_weights.1 = (bf16[8,4,1168,128]{3,2,1,0:T(8,128)(2,1)}, bf16[8,4,240,128]{3,2,1,0:T(8,128)(2,1)}) custom-call(s32[8,128]{1,0:T(8,128)} %bitcast.29, s32[8,128]{1,0:T(8,128)} %bitcast.31, s32[8,128]{1,0:T(8,128)} %bitcast.33, f32[1160,128]{1,0:T(8,128)} %bitcast.25, f32[907,128]{1,0:T(8,128)} %bitcast.27), custom_call_target="tpu_custom_call" | custom-call | tf_op jit(solution)/shard_map/gather_weights/pallas_call | solution.py:286
  54.2 10.6 %encode.1 = (bf16[512,512]{1,0:T(8,128)(2,1)}, bf16[704,1024]{1,0:T(8,128)(2,1)}, bf16[512,512]{1,0:T(8,128)(2,1)}, bf16[512,1536]{1,0:T(8,128)(2,1)}, f32[4,512...) custom-call(s32[6]{0:T(128)} %lengths.7, ...), custom_call_target="tpu_custom_call" | custom-call | tf_op jit(solution)/shard_map/encode/pallas_call | solution.py:1381
  64.9 62.5 %attend.1 = (bf16[8,128,128]{2,1,0:T(8,128)(2,1)}, f32[1,2048]{1,0:T(1,128)}, f32[64,2048]{1,0:T(8,128)}, bf16[8,128,128]{2,1,0:T(8,128)(2,1)}, bf16[4,8,256,128]{3,2,1,0:T(8,128)(2,1)}) custom-call(s32[6]{0:T(128)} %lengths.7, bf16[8,128,128]{2,1,0:T(8,128)(2,1)} %get-tuple-element.54.q_in, bf16[8,256,128]{2,1,0:T(8,128)(2,1)} %get-tuple-element.55.kv_in), custom_call_target="tpu_custom_call" | custom-call | tf_op jit(solution)/shard_map/attend/pallas_call | solution.py:813
  127.4 18.1 %middle.1 = (bf16[8,128,128]{2,1,0:T(8,128)(2,1)}, f32[256,512]{1,0:T(8,128)}, f32[8,128]{1,0:T(8,128)}, f32[4104,128]{1,0:T(8,128)}, f32[2,512]{1,0:T(2,128)}, /*index=5*/bf16[8,4,1168,128]{3,2,1,0:T(8,128)(2,1)}) custom-call(f32[8,128]{1,0:T(8,128)} %get-tuple-element.52.counts, bf16[8,4,1168,128]{3,2,1,0:T(8,128)(2,1)} %get-tuple-element.50.weights, ...), custom_call_target="tpu_custom_call" | custom-call | tf_op jit(solution)/shard_map/middle/pallas_call | solution.py:1559
  145.5 66.2 %attend_back.1 = (bf16[8,128,128]{2,1,0:T(8,128)(2,1)}, bf16[8,256,128]{2,1,0:T(8,128)(2,1)}) custom-call(s32[6]{0:T(128)} %lengths.7, bf16[8,128,128]{2,1,0:T(8,128)(2,1)} %get-tuple-element.59.q_all, bf16[4,8,256,128]{3,2,1,0:T(8,128)(2,1)} %get-tuple-element.60.kv_all, bf16[8,128,128]{2,1,0:T(8,128)(2,1)} %get-tuple-element.61.do_in, ...), custom_call_target="tpu_custom_call" | custom-call | tf_op jit(solution)/shard_map/attend_back/pallas_call | solution.py:1054
  211.7 18.2 %ending.1 = (bf16[8,4,1168,128]{3,2,1,0:T(8,128)(2,1)}, bf16[8,4,240,128]{3,2,1,0:T(8,128)(2,1)}) custom-call(s32[6]{0:T(128)} %lengths.7, bf16[8,4,1168,128]{3,2,1,0:T(8,128)(2,1)} %get-tuple-element.58.grads_in, bf16[8,128,128]{2,1,0:T(8,128)(2,1)} %get-tuple-element.64.d_q_self, ...), custom_call_target="tpu_custom_call", output_to_operand_aliasing={{0}: (1, {})} | custom-call | tf_op jit(solution)/shard_map/ending/pallas_call | solution.py:1730
  229.9 0.0 copy-start
  229.9 0.0 copy-start.2
  229.9 0.0 copy-start.3
  230.0 65.4 %reduce_gradients.1 = (f32[1160,128]{1,0:T(8,128)}, f32[907,128]{1,0:T(8,128)}, f32[1,3]{1,0:T(1,128)}, f32[1,1]{1,0:T(1,128)}, f32[1,1]{1,0:T(1,128)}) custom-call(bf16[8,4,1168,128]{3,2,1,0:T(8,128)(2,1)} %get-tuple-element.80.refs_0_, bf16[8,4,240,128]{3,2,1,0:T(8,128)(2,1)} %get-tuple-element.81.refs_1_, f32[8,128]{1,0:T(8,128)} %get-tuple-element.82.refs_2_), custom_call_target="tpu_custom_call" | custom-call | tf_op jit(solution)/shard_map/reduce_gradients/pallas_call | solution.py:474
  295.4 0.0 copy-done
  295.4 0.0 copy-done.2
  295.4 0.0 copy-done.3
  295.4 0.0 copy-start.1
  295.4 0.0 copy-start.4
  295.4 0.0 copy-start.5
  295.4 0.0 copy-start.6
  295.4 3.4 %fusion.7 = (bf16[148480]{0:T(1024)(128)(2,1)}, f32[148480]{0:T(1024)}, f32[148480]{0:T(1024)}, f32[148480]{0:T(1024)}) fusion(f32[148480]{0:T(1024)S(1)} %copy-done, f32[1160,128]{1,0:T(8,128)} %get-tuple-element.83, f32[]{:T(128)} %bitcast.7, f32[148480]{0:T(1024)S(1)} %copy-done.2, f32[148480]{0:T(1024)S(1)} %copy-done.3), kind=kLoop, calls=%fused_computation.11 | loop fusion | flops 2524160 | bytes 4454404 | tf_op jit(solution)/shard_map/convert_element_type | solution.py:1758
  298.9 0.0 copy-start.7
  298.9 0.0 copy-done.1
  298.9 0.0 copy-done.4
  298.9 0.0 copy-done.5
  298.9 0.0 copy-done.6
  298.9 2.0 fusion.4
  300.9 0.0 copy-done.7
  300.9 0.5 copy.27
Async XLA Ops:
  229.9 65.4 %copy-start = (f32[148480]{0:T(1024)S(1)}, f32[148480]{0:T(1024)}, u32[]{:S(2)}) copy-start(f32[148480]{0:T(1024)} %param.18) | copy-start | bytes 1781764
  229.9 65.4 %copy-start.2 = (f32[148480]{0:T(1024)S(1)}, f32[148480]{0:T(1024)}, u32[]{:S(2)}) copy-start(f32[148480]{0:T(1024)} %param.19) | copy-start | bytes 1781764
  229.9 65.4 %copy-start.3 = (f32[148480]{0:T(1024)S(1)}, f32[148480]{0:T(1024)}, u32[]{:S(2)}) copy-start(f32[148480]{0:T(1024)} %param.20) | copy-start | bytes 1781764
  295.4 3.5 %copy-start.1 = (f32[116096]{0:T(1024)S(1)}, f32[116096]{0:T(1024)}, u32[]{:S(2)}) copy-start(f32[116096]{0:T(1024)} %param.21) | copy-start | bytes 1393156
  295.4 3.5 %copy-start.4 = (f32[116096]{0:T(1024)S(1)}, f32[116096]{0:T(1024)}, u32[]{:S(2)}) copy-start(f32[116096]{0:T(1024)} %param.22) | copy-start | bytes 1393156
  295.4 3.5 %copy-start.5 = (f32[116096]{0:T(1024)S(1)}, f32[116096]{0:T(1024)}, u32[]{:S(2)}) copy-start(f32[116096]{0:T(1024)} %param.23) | copy-start | bytes 1393156
  295.4 3.5 %copy-start.6 = (f32[907,128]{1,0:T(8,128)S(1)}, f32[907,128]{1,0:T(8,128)}, u32[]{:S(2)}) copy-start(f32[907,128]{1,0:T(8,128)} %get-tuple-element.85) | copy-start | bytes 1393156
  298.9 2.1 copy-start.7

commit v8 on v7

--- a/solution.py
+++ b/solution.py
@@ -620,12 +620,16 @@
         self.dims, self.me, self.send_sem, self.recv_sem = dims, me, send_sem, recv_sem
         self.started = []
 
-    def __call__(self, src, dst, offset):
+    def later(self, src, dst, offset):
         i = len(self.started)
         place = shifted(self.dims, self.me, offset, 1)
         copy = remote(src, dst, self.send_sem.at[i], self.recv_sem.at[i], place, self.dims)
+        self.started.append(copy)
+        return copy
+
+    def __call__(self, src, dst, offset):
+        copy = self.later(src, dst, offset)
         copy.start()
-        self.started.append(copy)
         return copy
 
     def finish(self):
@@ -651,6 +655,7 @@
     lse,
     out_t,
     q_all,
+    kv_out,
     kv_all,
     even_keys,
     even_values_t,
@@ -689,14 +694,23 @@
 
     kv_copies = {o: to_team(kv_in, kv_all.at[my_group, my_slot], o) for o in team.others}
     q_copies = [to_team(q_in, q_all.at[my_slot], o) for o in team.others]
-    ring, side = {}, {}
+    ring, side, slot_copies = {}, {}, []
 
     def group_at(offset):
         return team.group(shifted(dims, me, offset, -1))
 
+    def send_slot(o):
+        if z > 1:
+            block = kv_all.at[my_group, team.slot(shifted(dims, me, o, -1))]
+            slot_copies.append(push(block, block, along(0, 1)))
+
+    def slot_arrived():
+        for copy in slot_copies:
+            copy.wait_recv()
+
     def send_on(s, piece):
         block = kv_all.at[group_at(along(0, s)), pl.ds(piece * slots, slots)]
-        if s < z - 1:
+        if 0 < s < z - 1:
             ring[(s + 1, piece)] = push(block, block, along(0, 1))
         for o in team.sides:
             side[(s, o, piece)] = push(block, block, o)
@@ -769,8 +783,10 @@
     top[...] = jnp.full(top.shape, -1e38, jnp.float32)
     accum[...] = jnp.zeros(accum.shape, jnp.float32)
     own_kv.wait()
+    send_slot((0, 0, 0, 0))
     for o in team.others:
         kv_copies[o].wait_recv()
+        send_slot(o)
     for piece in range(pieces):
         send_on(0, piece)
     own_q.wait()
@@ -780,15 +796,29 @@
         queries[:, n * rows : (n + 1) * rows] = with_query_tail(
             bounds, my_group * amount + n * rows, unpack_t(q_all[n]), None
         )
+    stores = []
+
+    def store(offset):
+        group = group_at(offset)
+        copy = pltpu.make_async_copy(kv_all.at[group], kv_out.at[group], own_sem.at[3 + len(stores)])
+        copy.start()
+        stores.append(copy)
+
     for s in range(z):
+        store(along(0, s))
         for piece in range(pieces):
             compute(along(0, s), piece)
             if s < z - 1:
-                ring[(s + 1, piece)].wait_recv()
+                if s:
+                    ring[(s + 1, piece)].wait_recv()
+                elif piece == 0:
+                    slot_arrived()
                 send_on(s + 1, piece)
             for o in team.sides:
                 side[(s, o, piece)].wait_recv()
                 compute((s, o[1], 0, 0), piece)
+        for o in team.sides:
+            store((s, o[1], 0, 0))
     both(pending[0], None)
     total = accum[HD : HD + 1, :]
     out_t[...] = accum[:HD, :] / total
@@ -801,6 +831,8 @@
     own_o.wait()
     for copy in o_copies:
         copy.wait_recv()
+    for copy in stores:
+        copy.wait()
     push.finish()
 
 
@@ -809,7 +841,7 @@
     z = dims[0]
     amount = team.size * kv.shape[1]
     pieces, query_step = 2, 256
-    count = 3 * (team.size - 1) + pieces * (z + z * len(team.sides))
+    count = 4 * team.size + pieces * (z + z * len(team.sides))
     return pl.pallas_call(
         functools.partial(attend_kernel, team, query_step, 256, pieces),
         out_shape=(
@@ -820,8 +852,9 @@
             jax.ShapeDtypeStruct((team.groups,) + kv.shape, low),
         ),
         in_specs=[SMEM_SPEC, VMEM_SPEC, VMEM_SPEC],
-        out_specs=[VMEM_SPEC] * 5,
+        out_specs=[VMEM_SPEC] * 4 + [ANY_SPEC],
         scratch_shapes=[
+            pltpu.VMEM((team.groups,) + kv.shape, low),
             pltpu.VMEM((amount // pieces, LANES), low),
             pltpu.VMEM((HD + TILE, amount // pieces), low),
             pltpu.VMEM((amount // pieces, LANES), low),
@@ -836,7 +869,7 @@
             pltpu.VMEM(q.shape, low),
             pltpu.SemaphoreType.DMA((count,)),
             pltpu.SemaphoreType.DMA((count,)),
-            pltpu.SemaphoreType.DMA((3,)),
+            pltpu.SemaphoreType.DMA((3 + team.groups,)),
         ],
         compiler_params=pltpu.CompilerParams(
             collective_id=collective_id, has_side_effects=True, vmem_limit_bytes=56 * MIB
@@ -852,12 +885,13 @@
     pieces,
     lengths,
     q_all,
-    kv_all,
+    kv_in,
     do_in,
     out_t,
     lse,
     d_q_out,
     d_kv_out,
+    kv_all,
     do_all,
     even_keys_t,
     even_values_t,
@@ -891,6 +925,15 @@
     bounds = clip_bounds(lengths)
     rows = kv_all.shape[2]
     amount = team.size * rows
+    loads = {}
+    for s in range(1, z + 1):
+        for o in team.sides + [(0, 0, 0, 0)]:
+            offset = ((z - s) % z, o[1], 0, 0)
+            group = team.group(shifted(dims, me, offset, 1))
+            loads[offset] = pltpu.make_async_copy(
+                kv_in.at[group], kv_all.at[group], own_sem.at[3 + len(loads)]
+            )
+            loads[offset].start()
     slots = team.size // pieces
     piece_rows = slots * rows
     my_group, my_slot = team.group(me), team.slot(me)
@@ -963,6 +1006,8 @@
         group = team.group(shifted(dims, me, offset, 1))
         keys = sides_of_keys[len(computed) % 2]
         computed.append(offset)
+        if offset in loads:
+            loads.pop(offset).wait()
 
         @pl.loop(0, slots)
         def build(n):
@@ -996,7 +1041,7 @@
             def send(o=o, target=target):
                 side[(s, o, piece)] = push(target, side_in.at[s - 1, o[1] - 1, piece], o)
 
-            compute((z - s, o[1], 0, 0), piece, target, send)
+            compute(((z - s) % z, o[1], 0, 0), piece, target, send)
 
     def combine(s, piece):
         for o in team.sides:
@@ -1014,13 +1059,20 @@
                 ring_out[s - 1, piece, at, :] = total.astype(low)
             else:
                 d_kv_mine[piece * slots + n] = total.astype(low)
+        if s == z:
+            for copy, slot in d_kv_copies:
+                pl.when((slot >= piece * slots) & (slot < (piece + 1) * slots))(copy.start)
         if s < z:
             ring[(s, piece)] = push(ring_out.at[s - 1, piece], ring_in.at[s - 1, piece], along(0, 1))
 
+    d_kv_copies = []
+    for o in team.others:
+        slot = team.slot(shifted(dims, me, o, 1))
+        d_kv_copies.append((push.later(d_kv_mine.at[slot], d_kv_out.at[my_slot], o), slot))
     for s in range(1, z + 1):
         for piece in range(pieces):
             send_sides(s, piece)
-            after = functools.partial(combine, s, piece) if s < z else lambda: None
+            after = functools.partial(combine, s, piece)
             compute((z - s if s < z else 0, 0, 0, 0), piece, mine.at[piece], after)
     flush()
     for n in range(team.size):
@@ -1029,9 +1081,7 @@
     copies = [to_team(d_q_mine, d_q_out.at[my_slot], o) for o in team.others]
     own_q = pltpu.make_async_copy(d_q_mine.at[my_slot], d_q_out.at[my_slot], own_sem.at[1])
     own_q.start()
-    for piece in range(pieces):
-        combine(z, piece)
-    copies += [to_team(d_kv_mine, d_kv_out.at[my_slot], o) for o in team.others]
+    copies += [copy for copy, slot in d_kv_copies]
     own_kv = pltpu.make_async_copy(d_kv_mine.at[my_slot], d_kv_out.at[my_slot], own_sem.at[2])
     own_kv.start()
     own_q.wait()
@@ -1057,9 +1107,10 @@
             jax.ShapeDtypeStruct(q.shape, low),
             jax.ShapeDtypeStruct(kv.shape[1:], low),
         ),
-        in_specs=[SMEM_SPEC] + [VMEM_SPEC] * 5,
+        in_specs=[SMEM_SPEC, VMEM_SPEC, ANY_SPEC] + [VMEM_SPEC] * 3,
         out_specs=[VMEM_SPEC] * 2,
         scratch_shapes=[
+            pltpu.VMEM(kv.shape, low),
             pltpu.VMEM(q.shape, low),
             pltpu.VMEM((LANES, amount // pieces), low),
             pltpu.VMEM((LANES, amount // pieces), low),
@@ -1085,7 +1136,7 @@
             pltpu.VMEM(kv.shape[1:], low),
             pltpu.SemaphoreType.DMA((count,)),
             pltpu.SemaphoreType.DMA((count,)),
-            pltpu.SemaphoreType.DMA((3,)),
+            pltpu.SemaphoreType.DMA((3 + team.groups,)),
         ],
         compiler_params=pltpu.CompilerParams(
             collective_id=collective_id, has_side_effects=True, vmem_limit_bytes=60 * MIB
@@ -1218,6 +1269,17 @@
             target[row : row + rows, column + j : column + j + size] = value.astype(target.dtype)
 
 
+class Moves:
+    def __init__(self, sems):
+        self.sems, self.going = sems, []
+
+    def __call__(self, src, dst):
+        copy = pltpu.make_async_copy(src, dst, self.sems.at[len(self.going)])
+        copy.start()
+        self.going.append(copy)
+        return copy
+
+
 def normalized(x):
     centre = x - jnp.mean(x, -1, keepdims=True)
     rate = lax.rsqrt(jnp.mean(centre * centre, -1, keepdims=True) + norm_eps)
@@ -1276,11 +1338,27 @@
     weights,
     common,
     inputs_t,
+    enc_query_out,
+    enc_keyval_out,
+    enc_output_out,
+    self_project_out,
+    gains,
+    z_zero_out,
+    h_zero_out,
+    x_norm_out,
+    q_enc_out,
+    kv_enc_out,
+    o_enc_out,
+    z_one_out,
+    h_one_out,
+    q_self,
+    kv_self,
+    counts,
+    label_counts,
     enc_query,
     enc_keyval,
     enc_output,
     self_project,
-    gains,
     z_zero,
     h_zero,
     x_norm_t,
@@ -1289,10 +1367,6 @@
     o_enc,
     z_one,
     h_one,
-    q_self,
-    kv_self,
-    counts,
-    label_counts,
     held,
     held_common,
     held_counts,
@@ -1309,18 +1383,16 @@
     first = DQ * D // LANES
     block, blocks = common_blocks(first, first + (LAT + 4) * D // LANES, valid)
     tail = shard_rows // TILE * TILE
-    copies = [
-        pltpu.make_async_copy(common.at[pl.ds(block, blocks)], held_common, sems.at[0]),
-        pltpu.make_async_copy(weights.at[pl.ds(0, shards)], held, sems.at[1]),
-        pltpu.make_async_copy(weights.at[:, :, pl.ds(tail, TILE)], held_counts, sems.at[2]),
-    ]
-    for copy in copies:
-        copy.start()
+    move = Moves(sems)
+    common_here = move(common.at[pl.ds(block, blocks)], held_common)
+    counts_here = move(weights.at[:, :, pl.ds(tail, TILE)], held_counts)
+    weights_here = [move(weights.at[pl.ds(0, shards), g], held.at[:, g]) for g in range(n_head)]
     centre = inputs_t[...].astype(jnp.float32)
     centre = centre - jnp.mean(centre, 0, keepdims=True)
     rate = lax.rsqrt(jnp.mean(centre * centre, 0, keepdims=True) + norm_eps)
     x_norm_t[...] = (centre * rate).astype(low)
-    copies[0].wait()
+    stored = [move(x_norm_t, x_norm_out)]
+    common_here.wait()
     load_common(stage_common, held_common, valid)
     first = first - block * valid
     for j, value in matrix_of(stage_common, first, LAT, D, line):
@@ -1330,18 +1402,22 @@
     picked = picked_rows(bounds, rows, n_head)
     z_zero[...] = product(picked, latent_table[...])
     h_zero[...] = layer_norm(z_zero[...], gains[0:1, :]).astype(low)
-    copies[2].wait()
+    stored += [move(z_zero, z_zero_out), move(h_zero, h_zero_out)]
+    counts_here.wait()
     counted = held_counts[...].astype(jnp.float32)[:, :, shard_rows - tail : shard_rows - tail + 1]
     counts[...] = jnp.broadcast_to(jnp.sum(counted, (0, 1)), counts.shape)
     label_counts[...] = counts[:1, :MODES]
-    copies[1].wait()
     for g in range(n_head):
+        weights_here[g].wait()
         load_stage(stage, held, 0, shard_rows, g)
         load_matrices(
             stage, 0, n_head, g, (0, 1, 2, 3), (enc_query, enc_keyval, enc_output, self_project), line
         )
+    stored += [move(enc_query, enc_query_out), move(enc_keyval, enc_keyval_out)]
+    stored += [move(enc_output, enc_output_out), move(self_project, self_project_out)]
     q_enc[...] = product(h_zero[...], enc_query[...]).astype(low)
     kv_enc[...] = contract_first(x_norm_t[...], enc_keyval[...]).astype(low)
+    stored += [move(q_enc, q_enc_out), move(kv_enc, kv_enc_out)]
     for g in range(n_head):
         keys = kv_enc[:, 2 * g * width : (2 * g + 1) * width]
         values = kv_enc[:, (2 * g + 1) * width : (2 * g + 2) * width]
@@ -1354,6 +1430,7 @@
         o_enc[:, g * width : (g + 1) * width] = outcome.astype(low)
     z_one[...] = z_zero[...] + product(o_enc[...], enc_output[...])
     h_one[...] = layer_norm(z_one[...], gains[1:2, :]).astype(low)
+    stored += [move(o_enc, o_enc_out), move(z_one, z_one_out), move(h_one, h_one_out)]
     projected = product(h_one[...], self_project[...]).astype(low)
     for slot, (g, a) in enumerate(heads_of(n_head, q_self.shape[0])):
         query, key, value = (
@@ -1362,6 +1439,8 @@
         )
         q_self[slot] = pack(query)
         kv_self[slot] = jnp.concatenate([key, value], 1)
+    for copy in stored:
+        copy.wait()
 
 
 LINE = pltpu.VMEM((4, round_up(max(D, DI), 8), LANES), jnp.float32)
@@ -1378,30 +1457,35 @@
     query_rows = DQ * D // LANES
     block, blocks = common_blocks(query_rows, query_rows + (LAT + 4) * D // LANES, valid)
     keys = inputs_t.shape[1]
+    kept = [
+        shape_of((D, D)),
+        shape_of((DI, 2 * D)),
+        shape_of((D, D)),
+        shape_of((D, 3 * D)),
+        shape_of((rows, D), jnp.float32),
+        shape_of((rows, D)),
+        shape_of(inputs_t.shape),
+        shape_of((rows, D)),
+        shape_of((keys, 2 * D)),
+        shape_of((rows, D)),
+        shape_of((rows, D), jnp.float32),
+        shape_of((rows, D)),
+    ]
     return pl.pallas_call(
         functools.partial(encode_kernel, n_head, shard_rows, valid, rows),
-        out_shape=[
-            shape_of((D, D)),
-            shape_of((DI, 2 * D)),
-            shape_of((D, D)),
-            shape_of((D, 3 * D)),
-            shape_of((4, D), jnp.float32),
-            shape_of((rows, D), jnp.float32),
-            shape_of((rows, D)),
-            shape_of(inputs_t.shape),
-            shape_of((rows, D)),
-            shape_of((keys, 2 * D)),
-            shape_of((rows, D)),
-            shape_of((rows, D), jnp.float32),
-            shape_of((rows, D)),
+        out_shape=kept[:4]
+        + [shape_of((4, D), jnp.float32)]
+        + kept[4:]
+        + [
             shape_of((slots, rows // 2, LANES)),
             shape_of((slots, rows, LANES)),
             shape_of((8, LANES), jnp.float32),
             shape_of((1, MODES), jnp.float32),
         ],
         in_specs=[SMEM_SPEC, ANY_SPEC, ANY_SPEC, VMEM_SPEC],
-        out_specs=[VMEM_SPEC] * 17,
-        scratch_shapes=[
+        out_specs=[ANY_SPEC] * 4 + [VMEM_SPEC] + [ANY_SPEC] * 8 + [VMEM_SPEC] * 4,
+        scratch_shapes=[pltpu.VMEM(a.shape, a.dtype) for a in kept]
+        + [
             pltpu.VMEM((shards,) + weights.shape[1:], low),
             pltpu.VMEM((blocks,) + common.shape[1:], low),
             pltpu.VMEM(weights.shape[:2] + (TILE, LANES), low),
@@ -1409,7 +1493,7 @@
             pltpu.VMEM((blocks * valid, LANES), jnp.float32),
             LINE,
             pltpu.VMEM((LAT, D), low),
-            pltpu.SemaphoreType.DMA((3,)),
+            pltpu.SemaphoreType.DMA((2 + n_head + len(kept),)),
         ],
         compiler_params=pltpu.CompilerParams(vmem_limit_bytes=56 * MIB),
         name="encode",
@@ -1455,7 +1539,7 @@
     dout,
     d_two_out,
     tile,
-    query_grad,
+    query_grad_out,
     gain_grads,
     grads,
     held,
@@ -1463,6 +1547,7 @@
     stage,
     stage_common,
     line,
+    query_grad,
     self_output,
     hidden_in,
     hidden_out,
@@ -1477,18 +1562,16 @@
     shards = held.shape[0]
     first_row = first_shard * shard_rows
     starts = borders(n_head)
-    copies = [
-        pltpu.make_async_copy(common.at[pl.ds(0, held_common.shape[0])], held_common, sems.at[0]),
-        pltpu.make_async_copy(weights.at[pl.ds(first_shard, shards)], held, sems.at[1]),
-    ]
-    for copy in copies:
-        copy.start()
-    copies[0].wait()
+    move = Moves(sems)
+    shards_here = pl.ds(first_shard, shards)
+    common_here = move(common.at[pl.ds(0, held_common.shape[0])], held_common)
+    weights_here = [move(weights.at[shards_here, g], held.at[:, g]) for g in range(n_head)]
+    common_here.wait()
     load_common(stage_common, held_common, valid)
     for j, value in matrix_of(stage_common, 0, DQ, D, line):
         query_table[:, j : j + LANES] = value.astype(low)
-    copies[1].wait()
     for g in range(n_head):
+        weights_here[g].wait()
         load_stage(stage, held, first_shard, shard_rows, g)
         load_matrices(
             stage, first_row, n_head, g, (4, 5, 6, 7), (self_output, hidden_in, hidden_out, class_table), line
@@ -1524,6 +1607,7 @@
     dlogits = (weight * (jnp.exp2((logits - row_lse) * LOG2E) - is_target)).astype(low)
     d_decoded = against(dlogits, class_table[...])
     matrix_into(query_grad, 0, product(queries_t, d_decoded.astype(low)), line)
+    stored = [move(query_grad, query_grad_out)]
     d_three, gain_three_grad = norm_pullback(z_three, gain_three, d_decoded)
     d_branch = d_three.astype(low)
     d_pre = (slope[...] * against(d_branch, hidden_out[...])).astype(low)
@@ -1546,9 +1630,9 @@
             matrix_into(stage, starts[m] - first_row, result, line)
         for b in range(shards):
             held[b, g, :shard_rows, :] = stage[pl.ds(b * shard_rows, shard_rows), :].astype(low)
-    back = pltpu.make_async_copy(held, grads.at[pl.ds(first_shard, shards)], sems.at[2])
-    back.start()
-    back.wait()
+        stored.append(move(held.at[:, g], grads.at[shards_here, g]))
+    for copy in stored:
+        copy.wait()
 
 
 def middle(counts, weights, common, z_one, o_self, out_queries_t, marks, gains, valid, n_head, shard_rows):
@@ -1579,13 +1663,14 @@
             VMEM_SPEC,
             VMEM_SPEC,
         ],
-        out_specs=[VMEM_SPEC] * 5 + [ANY_SPEC],
+        out_specs=[VMEM_SPEC] * 3 + [ANY_SPEC, VMEM_SPEC, ANY_SPEC],
         scratch_shapes=[
             pltpu.VMEM((shards,) + weights.shape[1:], low),
             pltpu.VMEM((blocks,) + common.shape[1:], low),
             pltpu.VMEM((shards * shard_rows, LANES), jnp.float32),
             pltpu.VMEM((blocks * valid, LANES), jnp.float32),
             LINE,
+            pltpu.VMEM((query_rows, LANES), jnp.float32),
             pltpu.VMEM((D, D), low),
             pltpu.VMEM((D, FF), low),
             pltpu.VMEM((FF, D), low),
@@ -1593,7 +1678,7 @@
             pltpu.VMEM((DQ, D), low),
             pltpu.VMEM((rows, FF), jnp.float32),
             pltpu.VMEM((rows, FF), low),
-            pltpu.SemaphoreType.DMA((3,)),
+            pltpu.SemaphoreType.DMA((2 + 2 * n_head,)),
         ],
         compiler_params=pltpu.CompilerParams(vmem_limit_bytes=56 * MIB),
         name="middle",
@@ -1609,38 +1694,41 @@
     grads_in,
     d_q_self,
     d_kv_self,
-    d_two,
     gains,
     gain_grads,
-    query_grad,
-    enc_query,
-    enc_keyval,
-    enc_output,
-    self_project,
-    z_zero,
-    h_zero,
-    x_norm_t,
-    q_enc,
-    kv_enc,
-    o_enc,
-    z_one,
-    h_one,
-    grads,
-    common_grad,
-    held,
-    stage,
-    stage_common,
-    line,
-    d_q,
-    d_kv,
-    sems,
+    *refs,
 ):
+    kept_in, (grads, common_grad), kept = refs[:14], refs[14:16], refs[16:30]
+    held, stage, stage_common, line, d_q, d_kv, sems = refs[30:]
+    (
+        d_two,
+        query_grad,
+        enc_query,
+        enc_keyval,
+        enc_output,
+        self_project,
+        z_zero,
+        h_zero,
+        x_norm_t,
+        q_enc,
+        kv_enc,
+        o_enc,
+        z_one,
+        h_one,
+    ) = kept
+    move = Moves(sems)
+    first_used = (12, 5, 0, 4, 10, 9, 2, 6, 1, 7, 8, 11, 3, 13)
+    loads = {i: move(kept_in[i], kept[i]) for i in first_used}
+
+    def need(*which):
+        for i in which:
+            loads[i].wait()
+
     heads = HEADS // n_head
     width = heads * HD
     shards = held.shape[0]
     starts = borders(n_head)
-    shared = pltpu.make_async_copy(grads_in.at[pl.ds(shards - 1, 1)], held.at[pl.ds(shards - 1, 1)], sems.at[0])
-    shared.start()
+    shared = move(grads_in.at[pl.ds(shards - 1, 1)], held.at[pl.ds(shards - 1, 1)])
     d_heads = {}
     for slot, head in enumerate(heads_of(n_head, d_kv_self.shape[0])):
         d_kv_head = d_kv_self[slot]
@@ -1650,11 +1738,13 @@
         for g in range(n_head)
     ]
     whole = jnp.concatenate(d_projected, 1)
+    need(12, 5, 0)
     d_middle, gain_one_grad = norm_pullback(
         z_one[...], gains[1:2, :], against(whole, self_project[...])
     )
     d_one = d_two[...] + d_middle
     d_one_low = d_one.astype(low)
+    need(4, 10, 9)
     d_o = against(d_one_low, enc_output[...]).astype(low)
     for g in range(n_head):
         keys = kv_enc[:, 2 * g * width : (2 * g + 1) * width]
@@ -1678,6 +1768,7 @@
         d_q[:, g * width : (g + 1) * width] = (d_query * SCORE_SCALE).astype(low)
         d_kv[:, 2 * g * width : (2 * g + 1) * width] = (d_key * SCORE_SCALE).astype(low)
         d_kv[:, (2 * g + 1) * width : (2 * g + 2) * width] = d_value.astype(low)
+    need(2, 6)
     d_middle, gain_zero_grad = norm_pullback(
         z_zero[...], gains[0:1, :], against(d_q[...], enc_query[...])
     )
@@ -1686,6 +1777,7 @@
     d_zero_rest = (d_zero - d_zero_top.astype(jnp.float32)).astype(low)
     picked = picked_rows(clip_bounds(lengths), rows, n_head)
     latent_grad = contract_first(picked, d_zero_top) + contract_first(picked, d_zero_rest)
+    need(1, 7, 8, 11, 3, 13)
     query_rows = query_grad.shape[0]
     stage_common[:query_rows] = query_grad[...]
     matrix_into(stage_common, query_rows, latent_grad, line)
@@ -1700,7 +1792,8 @@
                 block = jnp.concatenate([block, jnp.zeros((piece - amount, LANES), jnp.float32)], 0)
             common_grad[b, k] = block.astype(low)
     shared.wait()
-    kept = shards * shard_rows - starts[4]
+    shared_rows = shards * shard_rows - starts[4]
+    stored = []
     for g in range(n_head):
         results = (
             contract_first(h_zero[...], d_q[:, g * width : (g + 1) * width]),
@@ -1708,7 +1801,7 @@
             contract_first(o_enc[:, g * width : (g + 1) * width], d_one_low),
             contract_first(h_one[...], d_projected[g]),
         )
-        if kept:
+        if shared_rows:
             stage[pl.ds((shards - 1) * shard_rows, shard_rows), :] = held[
                 shards - 1, g, :shard_rows, :
             ].astype(jnp.float32)
@@ -1716,35 +1809,37 @@
             matrix_into(stage, starts[m], result, line)
         for b in range(shards):
             held[b, g, :shard_rows, :] = stage[pl.ds(b * shard_rows, shard_rows), :].astype(low)
-    back = pltpu.make_async_copy(held, grads.at[pl.ds(0, shards)], sems.at[1])
-    back.start()
-    back.wait()
+        stored.append(move(held.at[:, g], grads.at[pl.ds(0, shards), g]))
+    for copy in stored:
+        copy.wait()
 
 
 def ending(lengths, grads, d_self, d_two, gains, gain_grads, query_grad, kept, common_shape, valid, shard_rows):
     rows = d_two.shape[0]
     n_head = grads.shape[1]
     begin, shards = shards_of(n_head, shard_rows, 0, 4)
-    keys = kept[6].shape[1]
+    kept = (d_two, query_grad) + tuple(kept)
+    keys = kept[8].shape[1]
     common_rows = (DQ + LAT + 4) * D // LANES
     return pl.pallas_call(
         functools.partial(ending_kernel, n_head, shard_rows, valid, rows),
         out_shape=[shape_of(grads.shape), shape_of(common_shape)],
-        in_specs=[SMEM_SPEC, ANY_SPEC] + [VMEM_SPEC] * 18,
+        in_specs=[SMEM_SPEC, ANY_SPEC] + [VMEM_SPEC] * 4 + [ANY_SPEC] * len(kept),
         out_specs=[ANY_SPEC, VMEM_SPEC],
         input_output_aliases={1: 0},
-        scratch_shapes=[
+        scratch_shapes=[pltpu.VMEM(a.shape, a.dtype) for a in kept]
+        + [
             pltpu.VMEM((shards,) + grads.shape[1:], low),
             pltpu.VMEM((shards * shard_rows, LANES), jnp.float32),
             pltpu.VMEM((common_rows, LANES), jnp.float32),
             LINE,
             pltpu.VMEM((rows, D), low),
             pltpu.VMEM((keys, 2 * D), low),
-            pltpu.SemaphoreType.DMA((2,)),
+            pltpu.SemaphoreType.DMA((len(kept) + 1 + n_head,)),
         ],
         compiler_params=pltpu.CompilerParams(vmem_limit_bytes=56 * MIB),
         name="ending",
-    )(lengths, grads, *d_self, d_two, gains, gain_grads, query_grad, *kept)
+    )(lengths, grads, *d_self, gains, gain_grads, *kept)
 
 
 def adam_step(weight, first, second, grad):

time: 309 us -> 301 us (0.974)
  Pallas kernels: 295 us -> 286 us
    pallas_call x1, Pallas kernels: 62.5 us -> 56.5 us  [attend(): pl.pallas_call(functools.partial(attend_kernel, team, query_step, 256, pi...]
where the time goes in v8:
time: 301 us; the launch traced here: 295 us
  Pallas kernels  286 us (95%)
  other arithmetic  5.47 us (2%)
    pallas_call x1, Pallas kernels, reduce_all(): pl.pallas_call(functools.partial(reduce_kernel, dims, parts), out_shape=[...  67.2 us
    pallas_call x1, Pallas kernels, attend_back(): pl.pallas_call(functools.partial(attend_back_kernel, team, key_step, 512,...  64.2 us
    pallas_call x1, Pallas kernels, attend(): pl.pallas_call(functools.partial(attend_kernel, team, query_step, 256, pi...  56.5 us
    pallas_call x1, Pallas kernels, gather_all(): pl.pallas_call(functools.partial(gather_kernel, dims, parts), out_shape=[...  53.6 us
    pallas_call x1, Pallas kernels, middle(): pl.pallas_call(functools.partial(middle_kernel, n_head, shard_rows, valid...  16.3 us
    pallas_call x1, Pallas kernels, ending(): pl.pallas_call(functools.partial(ending_kernel, n_head, shard_rows, valid...  16.3 us
    pallas_call x1, Pallas kernels, encode(): pl.pallas_call(functools.partial(encode_kernel, n_head, shard_rows, valid...  11.7 us

profile of v8, /device:TPU:0, one launch (start us, length us, event | category | flops | bytes accessed | tf_op | source)
XLA Modules:
  0.0 294.8 jit_solution(8062482604059368951)
XLA Ops:
  0.6 53.6 %gather_weights.1 = (bf16[8,4,1168,128]{3,2,1,0:T(8,128)(2,1)}, bf16[8,4,240,128]{3,2,1,0:T(8,128)(2,1)}) custom-call(s32[8,128]{1,0:T(8,128)} %bitcast.29, s32[8,128]{1,0:T(8,128)} %bitcast.31, s32[8,128]{1,0:T(8,128)} %bitcast.33, f32[1160,128]{1,0:T(8,128)} %bitcast.25, f32[907,128]{1,0:T(8,128)} %bitcast.27), custom_call_target="tpu_custom_call" | custom-call | tf_op jit(solution)/shard_map/gather_weights/pallas_call | solution.py:286
  54.2 11.7 %encode.1 = (bf16[512,512]{1,0:T(8,128)(2,1)}, bf16[704,1024]{1,0:T(8,128)(2,1)}, bf16[512,512]{1,0:T(8,128)(2,1)}, bf16[512,1536]{1,0:T(8,128)(2,1)}, f32[4,512...) custom-call(s32[6]{0:T(128)} %lengths.7, ...), custom_call_target="tpu_custom_call" | custom-call | tf_op jit(solution)/shard_map/encode/pallas_call | solution.py:1474
  66.0 56.5 %attend.1 = (bf16[8,128,128]{2,1,0:T(8,128)(2,1)}, f32[1,2048]{1,0:T(1,128)}, f32[64,2048]{1,0:T(8,128)}, bf16[8,128,128]{2,1,0:T(8,128)(2,1)}, bf16[4,8,256,128]{3,2,1,0:T(8,128)(2,1)}) custom-call(s32[6]{0:T(128)} %lengths.7, bf16[8,128,128]{2,1,0:T(8,128)(2,1)} %get-tuple-element.54.q_in, bf16[8,256,128]{2,1,0:T(8,128)(2,1)} %get-tuple-element.55.kv_in), custom_call_target="tpu_custom_call" | custom-call | tf_op jit(solution)/shard_map/attend/pallas_call | solution.py:845
  122.5 16.3 %middle.1 = (bf16[8,128,128]{2,1,0:T(8,128)(2,1)}, f32[256,512]{1,0:T(8,128)}, f32[8,128]{1,0:T(8,128)}, f32[4104,128]{1,0:T(8,128)}, f32[2,512]{1,0:T(2,128)}, /*index=5*/bf16[8,4,1168,128]{3,2,1,0:T(8,128)(2,1)}) custom-call(f32[8,128]{1,0:T(8,128)} %get-tuple-element.52.counts, bf16[8,4,1168,128]{3,2,1,0:T(8,128)(2,1)} %get-tuple-element.50.weights, ...), custom_call_target="tpu_custom_call" | custom-call | tf_op jit(solution)/shard_map/middle/pallas_call | solution.py:1643
  138.8 64.2 %attend_back.1 = (bf16[8,128,128]{2,1,0:T(8,128)(2,1)}, bf16[8,256,128]{2,1,0:T(8,128)(2,1)}) custom-call(s32[6]{0:T(128)} %lengths.7, bf16[8,128,128]{2,1,0:T(8,128)(2,1)} %get-tuple-element.59.q_all, bf16[4,8,256,128]{3,2,1,0:T(8,128)(2,1)} %get-tuple-element.60.kv_in, bf16[8,128,128]{2,1,0:T(8,128)(2,1)} %get-tuple-element.61.do_in, ...), custom_call_target="tpu_custom_call" | custom-call | tf_op jit(solution)/shard_map/attend_back/pallas_call | solution.py:1104
  203.0 16.3 %ending.1 = (bf16[8,4,1168,128]{3,2,1,0:T(8,128)(2,1)}, bf16[8,4,240,128]{3,2,1,0:T(8,128)(2,1)}) custom-call(s32[6]{0:T(128)} %lengths.7, bf16[8,4,1168,128]{3,2,1,0:T(8,128)(2,1)} %get-tuple-element.58.grads_in, bf16[8,128,128]{2,1,0:T(8,128)(2,1)} %get-tuple-element.64.d_q_self, ...), custom_call_target="tpu_custom_call", output_to_operand_aliasing={{0}: (1, {})} | custom-call | tf_op jit(solution)/shard_map/ending/pallas_call | solution.py:1824
  219.3 0.0 copy-start
  219.3 0.0 copy-start.2
  219.3 0.0 copy-start.3
  219.3 67.2 %reduce_gradients.1 = (f32[1160,128]{1,0:T(8,128)}, f32[907,128]{1,0:T(8,128)}, f32[1,3]{1,0:T(1,128)}, f32[1,1]{1,0:T(1,128)}, f32[1,1]{1,0:T(1,128)}) custom-call(bf16[8,4,1168,128]{3,2,1,0:T(8,128)(2,1)} %get-tuple-element.80.refs_0_, bf16[8,4,240,128]{3,2,1,0:T(8,128)(2,1)} %get-tuple-element.81.refs_1_, f32[8,128]{1,0:T(8,128)} %get-tuple-element.82.refs_2_), custom_call_target="tpu_custom_call" | custom-call | tf_op jit(solution)/shard_map/reduce_gradients/pallas_call | solution.py:474
  286.5 0.0 copy-done
  286.5 0.0 copy-done.2
  286.5 0.0 copy-done.3
  286.5 0.0 copy-start.1
  286.6 0.0 copy-start.4
  286.6 0.0 copy-start.5
  286.6 0.0 copy-start.6
  286.6 3.4 %fusion.7 = (bf16[148480]{0:T(1024)(128)(2,1)}, f32[148480]{0:T(1024)}, f32[148480]{0:T(1024)}, f32[148480]{0:T(1024)}) fusion(f32[148480]{0:T(1024)S(1)} %copy-done, f32[1160,128]{1,0:T(8,128)} %get-tuple-element.83, f32[]{:T(128)} %bitcast.7, f32[148480]{0:T(1024)S(1)} %copy-done.2, f32[148480]{0:T(1024)S(1)} %copy-done.3), kind=kLoop, calls=%fused_computation.11 | loop fusion | flops 2524160 | bytes 4454404 | tf_op jit(solution)/shard_map/convert_element_type | solution.py:1853
  290.0 0.0 copy-start.7
  290.0 0.0 copy-done.1
  290.0 0.0 copy-done.4
  290.1 0.0 copy-done.5
  290.1 0.0 copy-done.6
  290.1 2.0 fusion.4
  292.1 0.0 copy-done.7
  292.1 0.5 copy.27
Async XLA Ops:
  219.3 67.2 %copy-start = (f32[148480]{0:T(1024)S(1)}, f32[148480]{0:T(1024)}, u32[]{:S(2)}) copy-start(f32[148480]{0:T(1024)} %param.18) | copy-start | bytes 1781764
  219.3 67.2 %copy-start.2 = (f32[148480]{0:T(1024)S(1)}, f32[148480]{0:T(1024)}, u32[]{:S(2)}) copy-start(f32[148480]{0:T(1024)} %param.19) | copy-start | bytes 1781764
  219.3 67.2 %copy-start.3 = (f32[148480]{0:T(1024)S(1)}, f32[148480]{0:T(1024)}, u32[]{:S(2)}) copy-start(f32[148480]{0:T(1024)} %param.20) | copy-start | bytes 1781764
  286.5 3.5 %copy-start.1 = (f32[116096]{0:T(1024)S(1)}, f32[116096]{0:T(1024)}, u32[]{:S(2)}) copy-start(f32[116096]{0:T(1024)} %param.21) | copy-start | bytes 1393156
  286.6 3.5 %copy-start.4 = (f32[116096]{0:T(1024)S(1)}, f32[116096]{0:T(1024)}, u32[]{:S(2)}) copy-start(f32[116096]{0:T(1024)} %param.22) | copy-start | bytes 1393156
  286.6 3.5 %copy-start.5 = (f32[116096]{0:T(1024)S(1)}, f32[116096]{0:T(1024)}, u32[]{:S(2)}) copy-start(f32[116096]{0:T(1024)} %param.23) | copy-start | bytes 1393156
  286.6 3.5 %copy-start.6 = (f32[907,128]{1,0:T(8,128)S(1)}, f32[907,128]{1,0:T(8,128)}, u32[]{:S(2)}) copy-start(f32[907,128]{1,0:T(8,128)} %get-tuple-element.85) | copy-start | bytes 1393156
  290.0 2.1 copy-start.7

commit v9 on v8

--- a/solution.py
+++ b/solution.py
@@ -275,13 +275,13 @@
 
 
 ZYXC, ZXYC, YXZC, XYZC = (0, 1, 2, 3), (0, 2, 1, 3), (1, 2, 0, 3), (2, 1, 0, 3)
-GATHER_SHARES = ((8, ZYXC), (6, ZXYC), (2, YXZC), (2, XYZC))
-REDUCE_SHARES = ((7, ZYXC), (7, ZXYC), (2, YXZC), (2, XYZC))
+HEAD_SHARES = ((15, ZYXC), (13, ZXYC), (4, YXZC), (5, XYZC))
+COMMON_SHARES = ((1, ZYXC), (1, ZXYC))
 
 
 def gather_all(dims, marks, params, rows, collective_id):
     z, y, x, cores = dims
-    parts = cut(0, rows[0], GATHER_SHARES) + cut(1, rows[1], ((1, ZXYC),))
+    parts = cut(0, rows[0], HEAD_SHARES) + cut(1, rows[1], COMMON_SHARES)
     count = len(parts) * (z * y * x * cores - 1)
     return pl.pallas_call(
         functools.partial(gather_kernel, dims, parts),
@@ -360,10 +360,16 @@
     head_out, common_out, losses, norm, factor = refs[3:8]
     places = len(parts) * 4
     buffers = refs[8 : 8 + places]
-    head_sum, common_sum, shares, send_sem, recv_sem, near_tiles, far_tiles = refs[8 + places :]
+    head_sum, common_sum, shares, send_sem, recv_sem, near_tiles, far_tiles = refs[8 + places : 15 + places]
+    held, held_sem = refs[15 + places : 17 + places], refs[17 + places]
     sums = (head_sum, common_sum)
     me = my_place(dims)
     z, y, x, cores = dims
+    loads = [
+        pltpu.make_async_copy(srcs[k].at[:, :, me[3]], held[k], held_sem.at[k]) for k in range(2)
+    ]
+    for load in loads:
+        load.start()
     across = peers_across(dims)
     others = [o for o in all_offsets(dims, (0, 1)) if any(o)]
     met = ring_and_others(dims)
@@ -382,7 +388,13 @@
         array, first, rows, order = parts[p]
         if position == 0:
             place = shifted(dims, me, offset, 1)
-            return srcs[array].at[blk_of(dims, place), head_of(dims, place), pl.ds(first, rows)]
+            at = (blk_of(dims, place), place[2])
+            if offset[3]:
+                return srcs[array].at[(*at, place[3], pl.ds(first, rows))]
+            if loads[array] is not None:
+                loads[array].wait()
+                loads[array] = None
+            return held[array].at[(*at, pl.ds(first, rows))]
         return slot(p, position - 1, offset)
 
     def ring_slot(p, position, offset):
@@ -402,10 +414,14 @@
         @pl.loop(0, rows // step)
         def some_rows(n):
             at = pl.ds(pl.multiple_of(n * step, step), step)
+            last = position == 3 and not any(offset)
+            if len(arrivals) == 1 and not last:
+                arrivals[0][at] = mine[at] + arrivals[0][at]
+                return
             total = mine[at].astype(jnp.float32)
             for arrival in arrivals:
                 total = total + arrival[at].astype(jnp.float32)
-            if position == 3 and not any(offset):
+            if last:
                 sums[array][pl.ds(pl.multiple_of(first + n * step, TILE), step)] = total
             else:
                 arrivals[0][at] = total.astype(low)
@@ -463,8 +479,10 @@
 def reduce_all(dims, arrays, valid, tile, collective_id):
     z, y, x, cores = dims
     rows = [array.shape[2] for array in arrays]
-    parts = cut(0, rows[0], [(share, order[::-1]) for share, order in REDUCE_SHARES])
-    parts = parts + cut(1, rows[1], ((1, ZXYC[::-1]),))
+    arrays = [array.reshape(z * y, x, cores, *array.shape[2:]) for array in arrays]
+    parts = ()
+    for array, shares in enumerate((HEAD_SHARES, COMMON_SHARES)):
+        parts += cut(array, rows[array], [(share, order[::-1]) for share, order in shares])
     scratch = []
     for array, first, amount, order in parts:
         for position, axis in enumerate(order):
@@ -480,7 +498,7 @@
             shape_of((1, 1), jnp.float32),
             shape_of((1, 1), jnp.float32),
         ],
-        in_specs=[VMEM_SPEC] * 3,
+        in_specs=[ANY_SPEC] * 2 + [VMEM_SPEC],
         out_specs=[VMEM_SPEC] * 5,
         scratch_shapes=scratch
         + [pltpu.VMEM((n, LANES), jnp.float32) for n in rows]
@@ -490,7 +508,9 @@
             pltpu.SemaphoreType.DMA((count,)),
             pltpu.VMEM((x * cores, 8, LANES), jnp.float32),
             pltpu.VMEM((z * y, 8, LANES), jnp.float32),
-        ],
+        ]
+        + [pltpu.VMEM((z * y, x, n, LANES), low) for n in rows]
+        + [pltpu.SemaphoreType.DMA((2,))],
         compiler_params=pltpu.CompilerParams(
             collective_id=collective_id, has_side_effects=True, vmem_limit_bytes=60 * MIB
         ),
@@ -1338,27 +1358,11 @@
     weights,
     common,
     inputs_t,
-    enc_query_out,
-    enc_keyval_out,
-    enc_output_out,
-    self_project_out,
-    gains,
-    z_zero_out,
-    h_zero_out,
-    x_norm_out,
-    q_enc_out,
-    kv_enc_out,
-    o_enc_out,
-    z_one_out,
-    h_one_out,
-    q_self,
-    kv_self,
-    counts,
-    label_counts,
     enc_query,
     enc_keyval,
     enc_output,
     self_project,
+    gains,
     z_zero,
     h_zero,
     x_norm_t,
@@ -1367,6 +1371,10 @@
     o_enc,
     z_one,
     h_one,
+    q_self,
+    kv_self,
+    counts,
+    label_counts,
     held,
     held_common,
     held_counts,
@@ -1383,16 +1391,18 @@
     first = DQ * D // LANES
     block, blocks = common_blocks(first, first + (LAT + 4) * D // LANES, valid)
     tail = shard_rows // TILE * TILE
-    move = Moves(sems)
-    common_here = move(common.at[pl.ds(block, blocks)], held_common)
-    counts_here = move(weights.at[:, :, pl.ds(tail, TILE)], held_counts)
-    weights_here = [move(weights.at[pl.ds(0, shards), g], held.at[:, g]) for g in range(n_head)]
+    copies = [
+        pltpu.make_async_copy(common.at[pl.ds(block, blocks)], held_common, sems.at[0]),
+        pltpu.make_async_copy(weights.at[pl.ds(0, shards)], held, sems.at[1]),
+        pltpu.make_async_copy(weights.at[:, :, pl.ds(tail, TILE)], held_counts, sems.at[2]),
+    ]
+    for copy in copies:
+        copy.start()
     centre = inputs_t[...].astype(jnp.float32)
     centre = centre - jnp.mean(centre, 0, keepdims=True)
     rate = lax.rsqrt(jnp.mean(centre * centre, 0, keepdims=True) + norm_eps)
     x_norm_t[...] = (centre * rate).astype(low)
-    stored = [move(x_norm_t, x_norm_out)]
-    common_here.wait()
+    copies[0].wait()
     load_common(stage_common, held_common, valid)
     first = first - block * valid
     for j, value in matrix_of(stage_common, first, LAT, D, line):
@@ -1402,22 +1412,18 @@
     picked = picked_rows(bounds, rows, n_head)
     z_zero[...] = product(picked, latent_table[...])
     h_zero[...] = layer_norm(z_zero[...], gains[0:1, :]).astype(low)
-    stored += [move(z_zero, z_zero_out), move(h_zero, h_zero_out)]
-    counts_here.wait()
+    copies[2].wait()
     counted = held_counts[...].astype(jnp.float32)[:, :, shard_rows - tail : shard_rows - tail + 1]
     counts[...] = jnp.broadcast_to(jnp.sum(counted, (0, 1)), counts.shape)
     label_counts[...] = counts[:1, :MODES]
+    copies[1].wait()
     for g in range(n_head):
-        weights_here[g].wait()
         load_stage(stage, held, 0, shard_rows, g)
         load_matrices(
             stage, 0, n_head, g, (0, 1, 2, 3), (enc_query, enc_keyval, enc_output, self_project), line
         )
-    stored += [move(enc_query, enc_query_out), move(enc_keyval, enc_keyval_out)]
-    stored += [move(enc_output, enc_output_out), move(self_project, self_project_out)]
     q_enc[...] = product(h_zero[...], enc_query[...]).astype(low)
     kv_enc[...] = contract_first(x_norm_t[...], enc_keyval[...]).astype(low)
-    stored += [move(q_enc, q_enc_out), move(kv_enc, kv_enc_out)]
     for g in range(n_head):
         keys = kv_enc[:, 2 * g * width : (2 * g + 1) * width]
         values = kv_enc[:, (2 * g + 1) * width : (2 * g + 2) * width]
@@ -1430,7 +1436,6 @@
         o_enc[:, g * width : (g + 1) * width] = outcome.astype(low)
     z_one[...] = z_zero[...] + product(o_enc[...], enc_output[...])
     h_one[...] = layer_norm(z_one[...], gains[1:2, :]).astype(low)
-    stored += [move(o_enc, o_enc_out), move(z_one, z_one_out), move(h_one, h_one_out)]
     projected = product(h_one[...], self_project[...]).astype(low)
     for slot, (g, a) in enumerate(heads_of(n_head, q_self.shape[0])):
         query, key, value = (
@@ -1439,8 +1444,6 @@
         )
         q_self[slot] = pack(query)
         kv_self[slot] = jnp.concatenate([key, value], 1)
-    for copy in stored:
-        copy.wait()
 
 
 LINE = pltpu.VMEM((4, round_up(max(D, DI), 8), LANES), jnp.float32)
@@ -1457,35 +1460,30 @@
     query_rows = DQ * D // LANES
     block, blocks = common_blocks(query_rows, query_rows + (LAT + 4) * D // LANES, valid)
     keys = inputs_t.shape[1]
-    kept = [
-        shape_of((D, D)),
-        shape_of((DI, 2 * D)),
-        shape_of((D, D)),
-        shape_of((D, 3 * D)),
-        shape_of((rows, D), jnp.float32),
-        shape_of((rows, D)),
-        shape_of(inputs_t.shape),
-        shape_of((rows, D)),
-        shape_of((keys, 2 * D)),
-        shape_of((rows, D)),
-        shape_of((rows, D), jnp.float32),
-        shape_of((rows, D)),
-    ]
     return pl.pallas_call(
         functools.partial(encode_kernel, n_head, shard_rows, valid, rows),
-        out_shape=kept[:4]
-        + [shape_of((4, D), jnp.float32)]
-        + kept[4:]
-        + [
+        out_shape=[
+            shape_of((D, D)),
+            shape_of((DI, 2 * D)),
+            shape_of((D, D)),
+            shape_of((D, 3 * D)),
+            shape_of((4, D), jnp.float32),
+            shape_of((rows, D), jnp.float32),
+            shape_of((rows, D)),
+            shape_of(inputs_t.shape),
+            shape_of((rows, D)),
+            shape_of((keys, 2 * D)),
+            shape_of((rows, D)),
+            shape_of((rows, D), jnp.float32),
+            shape_of((rows, D)),
             shape_of((slots, rows // 2, LANES)),
             shape_of((slots, rows, LANES)),
             shape_of((8, LANES), jnp.float32),
             shape_of((1, MODES), jnp.float32),
         ],
         in_specs=[SMEM_SPEC, ANY_SPEC, ANY_SPEC, VMEM_SPEC],
-        out_specs=[ANY_SPEC] * 4 + [VMEM_SPEC] + [ANY_SPEC] * 8 + [VMEM_SPEC] * 4,
-        scratch_shapes=[pltpu.VMEM(a.shape, a.dtype) for a in kept]
-        + [
+        out_specs=[VMEM_SPEC] * 17,
+        scratch_shapes=[
             pltpu.VMEM((shards,) + weights.shape[1:], low),
             pltpu.VMEM((blocks,) + common.shape[1:], low),
             pltpu.VMEM(weights.shape[:2] + (TILE, LANES), low),
@@ -1493,7 +1491,7 @@
             pltpu.VMEM((blocks * valid, LANES), jnp.float32),
             LINE,
             pltpu.VMEM((LAT, D), low),
-            pltpu.SemaphoreType.DMA((2 + n_head + len(kept),)),
+            pltpu.SemaphoreType.DMA((3,)),
         ],
         compiler_params=pltpu.CompilerParams(vmem_limit_bytes=56 * MIB),
         name="encode",

time: 301 us -> 294 us (0.977)
  Pallas kernels: 286 us -> 279 us
    pallas_call x1, Pallas kernels: 67.2 us -> 60.8 us  [reduce_all(): pl.pallas_call(functools.partial(reduce_kernel, dims, parts), out_shape=[...]
where the time goes in v9:
time: 294 us; the launch traced here: 288 us
  Pallas kernels  279 us (95%)
  other arithmetic  5.47 us (2%)
  between operations  3.06 us (1%)
    pallas_call x1, Pallas kernels, attend_back(): pl.pallas_call(functools.partial(attend_back_kernel, team, key_step, 512,...  64.2 us
    pallas_call x1, Pallas kernels, reduce_all(): pl.pallas_call(functools.partial(reduce_kernel, dims, parts), out_shape=[...  60.8 us
    pallas_call x1, Pallas kernels, attend(): pl.pallas_call(functools.partial(attend_kernel, team, query_step, 256, pi...  56.7 us
    pallas_call x1, Pallas kernels, gather_all(): pl.pallas_call(functools.partial(gather_kernel, dims, parts), out_shape=[...  53.9 us
    pallas_call x1, Pallas kernels, middle(): pl.pallas_call(functools.partial(middle_kernel, n_head, shard_rows, valid...  16.3 us
    pallas_call x1, Pallas kernels, ending(): pl.pallas_call(functools.partial(ending_kernel, n_head, shard_rows, valid...  16.3 us
    pallas_call x1, Pallas kernels, encode(): pl.pallas_call(functools.partial(encode_kernel, n_head, shard_rows, valid...  10.6 us

profile of v9, /device:TPU:0, one launch (start us, length us, event | category | flops | bytes accessed | tf_op | source)
XLA Modules:
  0.0 287.9 jit_solution(2908484632911859313)
XLA Ops:
  0.6 53.9 %gather_weights.1 = (bf16[8,4,1168,128]{3,2,1,0:T(8,128)(2,1)}, bf16[8,4,240,128]{3,2,1,0:T(8,128)(2,1)}) custom-call(s32[8,128]{1,0:T(8,128)} %bitcast.33, s32[8,128]{1,0:T(8,128)} %bitcast.35, s32[8,128]{1,0:T(8,128)} %bitcast.37, f32[1160,128]{1,0:T(8,128)} %bitcast.28, f32[907,128]{1,0:T(8,128)} %bitcast.31), custom_call_target="tpu_custom_call" | custom-call | tf_op jit(solution)/shard_map/gather_weights/pallas_call | solution.py:286
  54.5 10.6 %encode.1 = (bf16[512,512]{1,0:T(8,128)(2,1)}, bf16[704,1024]{1,0:T(8,128)(2,1)}, bf16[512,512]{1,0:T(8,128)(2,1)}, bf16[512,1536]{1,0:T(8,128)(2,1)}, f32[4,512...) custom-call(s32[6]{0:T(128)} %lengths.7, ...), custom_call_target="tpu_custom_call" | custom-call | tf_op jit(solution)/shard_map/encode/pallas_call | solution.py:1463
  65.2 56.7 %attend.1 = (bf16[8,128,128]{2,1,0:T(8,128)(2,1)}, f32[1,2048]{1,0:T(1,128)}, f32[64,2048]{1,0:T(8,128)}, bf16[8,128,128]{2,1,0:T(8,128)(2,1)}, bf16[4,8,256,128]{3,2,1,0:T(8,128)(2,1)}) custom-call(s32[6]{0:T(128)} %lengths.7, bf16[8,128,128]{2,1,0:T(8,128)(2,1)} %get-tuple-element.54.q_in, bf16[8,256,128]{2,1,0:T(8,128)(2,1)} %get-tuple-element.55.kv_in), custom_call_target="tpu_custom_call" | custom-call | tf_op jit(solution)/shard_map/attend/pallas_call | solution.py:865
  121.9 16.3 %middle.1 = (bf16[8,128,128]{2,1,0:T(8,128)(2,1)}, f32[256,512]{1,0:T(8,128)}, f32[8,128]{1,0:T(8,128)}, f32[4104,128]{1,0:T(8,128)}, f32[2,512]{1,0:T(2,128)}, /*index=5*/bf16[8,4,1168,128]{3,2,1,0:T(8,128)(2,1)}) custom-call(f32[8,128]{1,0:T(8,128)} %get-tuple-element.52.counts, bf16[8,4,1168,128]{3,2,1,0:T(8,128)(2,1)} %get-tuple-element.50.weights, ...), custom_call_target="tpu_custom_call" | custom-call | tf_op jit(solution)/shard_map/middle/pallas_call | solution.py:1641
  138.2 64.2 %attend_back.1 = (bf16[8,128,128]{2,1,0:T(8,128)(2,1)}, bf16[8,256,128]{2,1,0:T(8,128)(2,1)}) custom-call(s32[6]{0:T(128)} %lengths.7, bf16[8,128,128]{2,1,0:T(8,128)(2,1)} %get-tuple-element.59.q_all, bf16[4,8,256,128]{3,2,1,0:T(8,128)(2,1)} %get-tuple-element.60.kv_in, bf16[8,128,128]{2,1,0:T(8,128)(2,1)} %get-tuple-element.61.do_in, ...), custom_call_target="tpu_custom_call" | custom-call | tf_op jit(solution)/shard_map/attend_back/pallas_call | solution.py:1124
  202.4 16.3 %ending.1 = (bf16[8,4,1168,128]{3,2,1,0:T(8,128)(2,1)}, bf16[8,4,240,128]{3,2,1,0:T(8,128)(2,1)}) custom-call(s32[6]{0:T(128)} %lengths.7, bf16[8,4,1168,128]{3,2,1,0:T(8,128)(2,1)} %get-tuple-element.58.grads_in, bf16[8,128,128]{2,1,0:T(8,128)(2,1)} %get-tuple-element.64.d_q_self, ...), custom_call_target="tpu_custom_call", output_to_operand_aliasing={{0}: (1, {})} | custom-call | tf_op jit(solution)/shard_map/ending/pallas_call | solution.py:1822
  218.7 0.0 copy-start
  218.7 0.0 copy-start.2
  218.7 0.0 copy-start.3
  218.7 60.8 %reduce_gradients.1 = (f32[1160,128]{1,0:T(8,128)}, f32[907,128]{1,0:T(8,128)}, f32[1,3]{1,0:T(1,128)}, f32[1,1]{1,0:T(1,128)}, f32[1,1]{1,0:T(1,128)}) custom-call(bf16[8,2,2,1168,128]{4,3,2,1,0:T(8,128)(2,1)} %bitcast.27, bf16[8,2,2,240,128]{4,3,2,1,0:T(8,128)(2,1)} %bitcast.30, f32[8,128]{1,0:T(8,128)} %get-tuple-element.82.refs_2_), custom_call_target="tpu_custom_call" | custom-call | tf_op jit(solution)/shard_map/reduce_gradients/pallas_call | solution.py:492
  279.5 0.0 copy-done
  279.5 0.0 copy-done.2
  279.5 0.0 copy-done.3
  279.5 0.0 copy-start.1
  279.5 0.0 copy-start.4
  279.6 0.0 copy-start.5
  279.6 0.0 copy-start.6
  279.6 3.4 %fusion.7 = (bf16[148480]{0:T(1024)(128)(2,1)}, f32[148480]{0:T(1024)}, f32[148480]{0:T(1024)}, f32[148480]{0:T(1024)}) fusion(f32[148480]{0:T(1024)S(1)} %copy-done, f32[1160,128]{1,0:T(8,128)} %get-tuple-element.83, f32[]{:T(128)} %bitcast.9, f32[148480]{0:T(1024)S(1)} %copy-done.2, f32[148480]{0:T(1024)S(1)} %copy-done.3), kind=kLoop, calls=%fused_computation.11 | loop fusion | flops 2524160 | bytes 4454404 | tf_op jit(solution)/shard_map/convert_element_type | solution.py:1851
  283.0 0.0 copy-start.7
  283.0 0.0 copy-done.1
  283.0 0.0 copy-done.4
  283.0 0.0 copy-done.5
  283.0 0.0 copy-done.6
  283.1 2.0 fusion.4
  285.1 0.0 copy-done.7
  285.1 0.5 copy.27
Async XLA Ops:
  218.7 60.8 %copy-start = (f32[148480]{0:T(1024)S(1)}, f32[148480]{0:T(1024)}, u32[]{:S(2)}) copy-start(f32[148480]{0:T(1024)} %param.18) | copy-start | bytes 1781764
  218.7 60.8 %copy-start.2 = (f32[148480]{0:T(1024)S(1)}, f32[148480]{0:T(1024)}, u32[]{:S(2)}) copy-start(f32[148480]{0:T(1024)} %param.19) | copy-start | bytes 1781764
  218.7 60.8 %copy-start.3 = (f32[148480]{0:T(1024)S(1)}, f32[148480]{0:T(1024)}, u32[]{:S(2)}) copy-start(f32[148480]{0:T(1024)} %param.20) | copy-start | bytes 1781764
  279.5 3.5 %copy-start.1 = (f32[116096]{0:T(1024)S(1)}, f32[116096]{0:T(1024)}, u32[]{:S(2)}) copy-start(f32[116096]{0:T(1024)} %param.21) | copy-start | bytes 1393156
  279.5 3.5 %copy-start.4 = (f32[116096]{0:T(1024)S(1)}, f32[116096]{0:T(1024)}, u32[]{:S(2)}) copy-start(f32[116096]{0:T(1024)} %param.22) | copy-start | bytes 1393156
  279.6 3.5 %copy-start.5 = (f32[116096]{0:T(1024)S(1)}, f32[116096]{0:T(1024)}, u32[]{:S(2)}) copy-start(f32[116096]{0:T(1024)} %param.23) | copy-start | bytes 1393156
  279.6 3.5 %copy-start.6 = (f32[907,128]{1,0:T(8,128)S(1)}, f32[907,128]{1,0:T(8,128)}, u32[]{:S(2)}) copy-start(f32[907,128]{1,0:T(8,128)} %get-tuple-element.85) | copy-start | bytes 1393156
  283.0 2.1 copy-start.7

commit v10 on v9

--- a/solution.py
+++ b/solution.py
@@ -1122,7 +1122,7 @@
     others = max(len(team.sides), 1)
     ring_steps, side_steps = max(z - 1, 1), z if team.sides else 1
     return pl.pallas_call(
-        functools.partial(attend_back_kernel, team, key_step, 512, pieces),
+        functools.partial(attend_back_kernel, team, key_step, 256, pieces),
         out_shape=(
             jax.ShapeDtypeStruct(q.shape, low),
             jax.ShapeDtypeStruct(kv.shape[1:], low),
@@ -1318,6 +1318,10 @@
     return d_x, jnp.sum(grad * unit, 0, keepdims=True)
 
 
+def turned(value):
+    return value.astype(jnp.float32).T.astype(low)
+
+
 def head_lanes(group, heads, value):
     width = heads * HD
     block = value[:, group * width : (group + 1) * width]
@@ -1329,9 +1333,10 @@
     return result
 
 
-def place_of(bounds, first, amount):
-    row = first + lax.broadcasted_iota(jnp.int32, (amount, 1), 0)
-    opening = jnp.zeros((amount, 1), jnp.int32)
+def place_of(bounds, first, amount, axis):
+    shape = (1, amount) if axis else (amount, 1)
+    row = first + lax.broadcasted_iota(jnp.int32, shape, axis)
+    opening = jnp.zeros(shape, jnp.int32)
     for begin, end in bounds:
         opening = jnp.where((row >= begin) & (row < end), begin, opening)
     offset = row - opening
@@ -1339,10 +1344,11 @@
     return offset - turns * LAT
 
 
-def picked_rows(bounds, rows, n_head):
+def picked_rows(bounds, rows, n_head, axis=0):
     first = lax.axis_index("blk") * (rows * n_head) + lax.axis_index("head") * rows
-    lane = lax.broadcasted_iota(jnp.int32, (rows, LAT), 1)
-    return jnp.where(lane == place_of(bounds, first, rows), 1.0, 0.0).astype(low)
+    shape = (LAT, rows) if axis else (rows, LAT)
+    latent = lax.broadcasted_iota(jnp.int32, shape, 1 - axis)
+    return jnp.where(latent == place_of(bounds, first, rows, axis), 1.0, 0.0).astype(low)
 
 
 def enc_scores(q_head, keys):
@@ -1617,12 +1623,13 @@
     d_o = against(d_two_low, self_output[...]).astype(low)
     for slot, (g, a) in enumerate(heads_of(n_head, o_self.shape[0])):
         dout[slot] = pack(d_o[:, g * width + a * HD : g * width + (a + 1) * HD])
+    h_two_t, decoded_t = turned(h_two), turned(decoded)
     for g in range(n_head):
         results = (
             contract_first(o_groups[g], d_two_low),
-            contract_first(h_two, d_pre[:, g * hidden : (g + 1) * hidden]),
+            product(h_two_t, d_pre[:, g * hidden : (g + 1) * hidden]),
             contract_first(activ[:, g * hidden : (g + 1) * hidden], d_branch),
-            contract_first(decoded, dlogits[:, g * classes : (g + 1) * classes]),
+            product(decoded_t, dlogits[:, g * classes : (g + 1) * classes]),
         )
         for m, result in zip((4, 5, 6, 7), results):
             matrix_into(stage, starts[m] - first_row, result, line)
@@ -1749,7 +1756,8 @@
         values = kv_enc[:, (2 * g + 1) * width : (2 * g + 2) * width]
         d_key = jnp.zeros(keys.shape, jnp.float32)
         d_value = jnp.zeros(keys.shape, jnp.float32)
-        d_query = jnp.zeros((rows, width), jnp.float32)
+        d_query_t = []
+        keys_t = turned(keys)
         for (here, q_head), (unused, do_head) in zip(
             head_lanes(g, heads, q_enc[...]), head_lanes(g, heads, d_o)
         ):
@@ -1762,7 +1770,9 @@
             d_scores = (probs * (d_probs - delta)).astype(low)
             d_value = d_value + product(probs.astype(low), do_head)
             d_key = d_key + product(d_scores, q_head)
-            d_query = jnp.where(here, contract_first(d_scores, keys), d_query)
+            a = len(d_query_t)
+            d_query_t.append(product(keys_t[a * HD : (a + 1) * HD], d_scores))
+        d_query = jnp.concatenate(d_query_t, 0).T
         d_q[:, g * width : (g + 1) * width] = (d_query * SCORE_SCALE).astype(low)
         d_kv[:, 2 * g * width : (2 * g + 1) * width] = (d_key * SCORE_SCALE).astype(low)
         d_kv[:, (2 * g + 1) * width : (2 * g + 2) * width] = d_value.astype(low)
@@ -1773,8 +1783,8 @@
     d_zero = d_one + d_middle
     d_zero_top = d_zero.astype(low)
     d_zero_rest = (d_zero - d_zero_top.astype(jnp.float32)).astype(low)
-    picked = picked_rows(clip_bounds(lengths), rows, n_head)
-    latent_grad = contract_first(picked, d_zero_top) + contract_first(picked, d_zero_rest)
+    picked_t = picked_rows(clip_bounds(lengths), rows, n_head, 1)
+    latent_grad = product(picked_t, d_zero_top) + product(picked_t, d_zero_rest)
     need(1, 7, 8, 11, 3, 13)
     query_rows = query_grad.shape[0]
     stage_common[:query_rows] = query_grad[...]
@@ -1792,12 +1802,13 @@
     shared.wait()
     shared_rows = shards * shard_rows - starts[4]
     stored = []
+    h_zero_t, h_one_t = turned(h_zero[...]), turned(h_one[...])
     for g in range(n_head):
         results = (
-            contract_first(h_zero[...], d_q[:, g * width : (g + 1) * width]),
+            product(h_zero_t, d_q[:, g * width : (g + 1) * width]),
             product(x_norm_t[...], d_kv[:, 2 * g * width : (2 * g + 2) * width]),
             contract_first(o_enc[:, g * width : (g + 1) * width], d_one_low),
-            contract_first(h_one[...], d_projected[g]),
+            product(h_one_t, d_projected[g]),
         )
         if shared_rows:
             stage[pl.ds((shards - 1) * shard_rows, shard_rows), :] = held[

time: 294 us -> 292 us (level)
  no operation moved by 1% of the time
where the time goes in v10:
time: 292 us; the launch traced here: 287 us
  Pallas kernels  278 us (95%)
  other arithmetic  5.47 us (2%)
  between operations  3.06 us (1%)
    pallas_call x1, Pallas kernels, attend_back(): pl.pallas_call(functools.partial(attend_back_kernel, team, key_step, 256,...  63.3 us
    pallas_call x1, Pallas kernels, reduce_all(): pl.pallas_call(functools.partial(reduce_kernel, dims, parts), out_shape=[...  60.8 us
    pallas_call x1, Pallas kernels, attend(): pl.pallas_call(functools.partial(attend_kernel, team, query_step, 256, pi...  56.7 us
    pallas_call x1, Pallas kernels, gather_all(): pl.pallas_call(functools.partial(gather_kernel, dims, parts), out_shape=[...  53.9 us
    pallas_call x1, Pallas kernels, middle(): pl.pallas_call(functools.partial(middle_kernel, n_head, shard_rows, valid...  16.4 us
    pallas_call x1, Pallas kernels, ending(): pl.pallas_call(functools.partial(ending_kernel, n_head, shard_rows, valid...  15.8 us
    pallas_call x1, Pallas kernels, encode(): pl.pallas_call(functools.partial(encode_kernel, n_head, shard_rows, valid...  10.6 us

profile of v10, /device:TPU:0, one launch (start us, length us, event | category | flops | bytes accessed | tf_op | source)
XLA Modules:
  0.0 286.6 jit_solution(17465624476337851095)
XLA Ops:
  0.6 53.9 %gather_weights.1 = (bf16[8,4,1168,128]{3,2,1,0:T(8,128)(2,1)}, bf16[8,4,240,128]{3,2,1,0:T(8,128)(2,1)}) custom-call(s32[8,128]{1,0:T(8,128)} %bitcast.33, s32[8,128]{1,0:T(8,128)} %bitcast.35, s32[8,128]{1,0:T(8,128)} %bitcast.37, f32[1160,128]{1,0:T(8,128)} %bitcast.28, f32[907,128]{1,0:T(8,128)} %bitcast.31), custom_call_target="tpu_custom_call" | custom-call | tf_op jit(solution)/shard_map/gather_weights/pallas_call | solution.py:286
  54.5 10.6 %encode.1 = (bf16[512,512]{1,0:T(8,128)(2,1)}, bf16[704,1024]{1,0:T(8,128)(2,1)}, bf16[512,512]{1,0:T(8,128)(2,1)}, bf16[512,1536]{1,0:T(8,128)(2,1)}, f32[4,512...) custom-call(s32[6]{0:T(128)} %lengths.7, ...), custom_call_target="tpu_custom_call" | custom-call | tf_op jit(solution)/shard_map/encode/pallas_call | solution.py:1469
  65.2 56.7 %attend.1 = (bf16[8,128,128]{2,1,0:T(8,128)(2,1)}, f32[1,2048]{1,0:T(1,128)}, f32[64,2048]{1,0:T(8,128)}, bf16[8,128,128]{2,1,0:T(8,128)(2,1)}, bf16[4,8,256,128]{3,2,1,0:T(8,128)(2,1)}) custom-call(s32[6]{0:T(128)} %lengths.7, bf16[8,128,128]{2,1,0:T(8,128)(2,1)} %get-tuple-element.54.q_in, bf16[8,256,128]{2,1,0:T(8,128)(2,1)} %get-tuple-element.55.kv_in), custom_call_target="tpu_custom_call" | custom-call | tf_op jit(solution)/shard_map/attend/pallas_call | solution.py:865
  121.9 16.4 %middle.1 = (bf16[8,128,128]{2,1,0:T(8,128)(2,1)}, f32[256,512]{1,0:T(8,128)}, f32[8,128]{1,0:T(8,128)}, f32[4104,128]{1,0:T(8,128)}, f32[2,512]{1,0:T(2,128)}, /*index=5*/bf16[8,4,1168,128]{3,2,1,0:T(8,128)(2,1)}) custom-call(f32[8,128]{1,0:T(8,128)} %get-tuple-element.52.counts, bf16[8,4,1168,128]{3,2,1,0:T(8,128)(2,1)} %get-tuple-element.50.weights, ...), custom_call_target="tpu_custom_call" | custom-call | tf_op jit(solution)/shard_map/middle/pallas_call | solution.py:1648
  138.2 63.3 %attend_back.1 = (bf16[8,128,128]{2,1,0:T(8,128)(2,1)}, bf16[8,256,128]{2,1,0:T(8,128)(2,1)}) custom-call(s32[6]{0:T(128)} %lengths.7, bf16[8,128,128]{2,1,0:T(8,128)(2,1)} %get-tuple-element.59.q_all, bf16[4,8,256,128]{3,2,1,0:T(8,128)(2,1)} %get-tuple-element.60.kv_in, bf16[8,128,128]{2,1,0:T(8,128)(2,1)} %get-tuple-element.61.do_in, ...), custom_call_target="tpu_custom_call" | custom-call | tf_op jit(solution)/shard_map/attend_back/pallas_call | solution.py:1124
  201.6 15.8 %ending.1 = (bf16[8,4,1168,128]{3,2,1,0:T(8,128)(2,1)}, bf16[8,4,240,128]{3,2,1,0:T(8,128)(2,1)}) custom-call(s32[6]{0:T(128)} %lengths.7, bf16[8,4,1168,128]{3,2,1,0:T(8,128)(2,1)} %get-tuple-element.58.grads_in, bf16[8,128,128]{2,1,0:T(8,128)(2,1)} %get-tuple-element.64.d_q_self, ...), custom_call_target="tpu_custom_call", output_to_operand_aliasing={{0}: (1, {})} | custom-call | tf_op jit(solution)/shard_map/ending/pallas_call | solution.py:1833
  217.4 0.0 copy-start
  217.4 0.0 copy-start.2
  217.4 0.0 copy-start.3
  217.4 60.8 %reduce_gradients.1 = (f32[1160,128]{1,0:T(8,128)}, f32[907,128]{1,0:T(8,128)}, f32[1,3]{1,0:T(1,128)}, f32[1,1]{1,0:T(1,128)}, f32[1,1]{1,0:T(1,128)}) custom-call(bf16[8,2,2,1168,128]{4,3,2,1,0:T(8,128)(2,1)} %bitcast.27, bf16[8,2,2,240,128]{4,3,2,1,0:T(8,128)(2,1)} %bitcast.30, f32[8,128]{1,0:T(8,128)} %get-tuple-element.82.refs_2_), custom_call_target="tpu_custom_call" | custom-call | tf_op jit(solution)/shard_map/reduce_gradients/pallas_call | solution.py:492
  278.2 0.0 copy-done
  278.2 0.0 copy-done.2
  278.3 0.0 copy-done.3
  278.3 0.0 copy-start.1
  278.3 0.0 copy-start.4
  278.3 0.0 copy-start.5
  278.3 0.0 copy-start.6
  278.3 3.4 %fusion.7 = (bf16[148480]{0:T(1024)(128)(2,1)}, f32[148480]{0:T(1024)}, f32[148480]{0:T(1024)}, f32[148480]{0:T(1024)}) fusion(f32[148480]{0:T(1024)S(1)} %copy-done, f32[1160,128]{1,0:T(8,128)} %get-tuple-element.83, f32[]{:T(128)} %bitcast.9, f32[148480]{0:T(1024)S(1)} %copy-done.2, f32[148480]{0:T(1024)S(1)} %copy-done.3), kind=kLoop, calls=%fused_computation.11 | loop fusion | flops 2524160 | bytes 4454404 | tf_op jit(solution)/shard_map/convert_element_type | solution.py:1862
  281.8 0.0 copy-start.7
  281.8 0.0 copy-done.1
  281.8 0.0 copy-done.4
  281.8 0.0 copy-done.5
  281.8 0.0 copy-done.6
  281.8 2.0 fusion.4
  283.8 0.0 copy-done.7
  283.8 0.5 copy.27
Async XLA Ops:
  217.4 60.8 %copy-start = (f32[148480]{0:T(1024)S(1)}, f32[148480]{0:T(1024)}, u32[]{:S(2)}) copy-start(f32[148480]{0:T(1024)} %param.18) | copy-start | bytes 1781764
  217.4 60.8 %copy-start.2 = (f32[148480]{0:T(1024)S(1)}, f32[148480]{0:T(1024)}, u32[]{:S(2)}) copy-start(f32[148480]{0:T(1024)} %param.19) | copy-start | bytes 1781764
  217.4 60.8 %copy-start.3 = (f32[148480]{0:T(1024)S(1)}, f32[148480]{0:T(1024)}, u32[]{:S(2)}) copy-start(f32[148480]{0:T(1024)} %param.20) | copy-start | bytes 1781764
  278.3 3.5 %copy-start.1 = (f32[116096]{0:T(1024)S(1)}, f32[116096]{0:T(1024)}, u32[]{:S(2)}) copy-start(f32[116096]{0:T(1024)} %param.21) | copy-start | bytes 1393156
  278.3 3.5 %copy-start.4 = (f32[116096]{0:T(1024)S(1)}, f32[116096]{0:T(1024)}, u32[]{:S(2)}) copy-start(f32[116096]{0:T(1024)} %param.22) | copy-start | bytes 1393156
  278.3 3.5 %copy-start.5 = (f32[116096]{0:T(1024)S(1)}, f32[116096]{0:T(1024)}, u32[]{:S(2)}) copy-start(f32[116096]{0:T(1024)} %param.23) | copy-start | bytes 1393156
  278.3 3.5 %copy-start.6 = (f32[907,128]{1,0:T(8,128)S(1)}, f32[907,128]{1,0:T(8,128)}, u32[]{:S(2)}) copy-start(f32[907,128]{1,0:T(8,128)} %get-tuple-element.85) | copy-start | bytes 1393156
  281.8 2.1 copy-start.7

commit v11 on v10

--- a/solution.py
+++ b/solution.py
@@ -82,6 +82,11 @@
 
 
 def greet(dims, me, offsets):
+    announce(dims, me, offsets)
+    pl.semaphore_wait(pltpu.get_barrier_semaphore(), len(offsets))
+
+
+def announce(dims, me, offsets):
     barrier = pltpu.get_barrier_semaphore()
     for offset in offsets:
         pl.semaphore_signal(
@@ -90,7 +95,6 @@
             device_id=device_of(dims, shifted(dims, me, offset, 1)),
             device_id_type=MESH,
         )
-    pl.semaphore_wait(barrier, len(offsets))
 
 
 def axis_peers(dims, axes):
@@ -192,6 +196,8 @@
     own_sem,
 ):
     me = my_place(dims)
+    met = ring_and_others(dims)
+    announce(dims, me, met)
     my_head = head_of(dims, me)
     n_head = dims[2] * dims[3]
     shard_rows, common_rows = head_params.shape[0], common_params.shape[0]
@@ -215,7 +221,7 @@
     piece = common_low.shape[0]
     common_low[...] = common_wide[pl.ds(pl.multiple_of(my_head * piece, TILE), piece)].astype(low)
 
-    greet(dims, me, ring_and_others(dims))
+    pl.semaphore_wait(pltpu.get_barrier_semaphore(), len(met))
     srcs, outs = (head_low, common_low), (head_all, common_all)
     copies = {}
 

time: 292 us -> 292 us (level)
  no operation moved by 1% of the time
where the time goes in v11:
time: 292 us; the launch traced here: 286 us
  Pallas kernels  277 us (95%)
  other arithmetic  5.47 us (2%)
  between operations  3.06 us (1%)
    pallas_call x1, Pallas kernels, attend_back(): pl.pallas_call(functools.partial(attend_back_kernel, team, key_step, 256,...  63.3 us
    pallas_call x1, Pallas kernels, reduce_all(): pl.pallas_call(functools.partial(reduce_kernel, dims, parts), out_shape=[...  60.8 us
    pallas_call x1, Pallas kernels, attend(): pl.pallas_call(functools.partial(attend_kernel, team, query_step, 256, pi...  56.7 us
    pallas_call x1, Pallas kernels, gather_all(): pl.pallas_call(functools.partial(gather_kernel, dims, parts), out_shape=[...  53.7 us
    pallas_call x1, Pallas kernels, middle(): pl.pallas_call(functools.partial(middle_kernel, n_head, shard_rows, valid...  16.4 us
    pallas_call x1, Pallas kernels, ending(): pl.pallas_call(functools.partial(ending_kernel, n_head, shard_rows, valid...  15.8 us
    pallas_call x1, Pallas kernels, encode(): pl.pallas_call(functools.partial(encode_kernel, n_head, shard_rows, valid...  10.6 us

profile of v11, /device:TPU:0, one launch (start us, length us, event | category | flops | bytes accessed | tf_op | source)
XLA Modules:
  0.0 286.4 jit_solution(17189759612139769274)
XLA Ops:
  0.6 53.7 %gather_weights.1 = (bf16[8,4,1168,128]{3,2,1,0:T(8,128)(2,1)}, bf16[8,4,240,128]{3,2,1,0:T(8,128)(2,1)}) custom-call(s32[8,128]{1,0:T(8,128)} %bitcast.33, s32[8,128]{1,0:T(8,128)} %bitcast.35, s32[8,128]{1,0:T(8,128)} %bitcast.37, f32[1160,128]{1,0:T(8,128)} %bitcast.28, f32[907,128]{1,0:T(8,128)} %bitcast.31), custom_call_target="tpu_custom_call" | custom-call | tf_op jit(solution)/shard_map/gather_weights/pallas_call | solution.py:292
  54.4 10.6 %encode.1 = (bf16[512,512]{1,0:T(8,128)(2,1)}, bf16[704,1024]{1,0:T(8,128)(2,1)}, bf16[512,512]{1,0:T(8,128)(2,1)}, bf16[512,1536]{1,0:T(8,128)(2,1)}, f32[4,512...) custom-call(s32[6]{0:T(128)} %lengths.7, ...), custom_call_target="tpu_custom_call" | custom-call | tf_op jit(solution)/shard_map/encode/pallas_call | solution.py:1475
  65.0 56.7 %attend.1 = (bf16[8,128,128]{2,1,0:T(8,128)(2,1)}, f32[1,2048]{1,0:T(1,128)}, f32[64,2048]{1,0:T(8,128)}, bf16[8,128,128]{2,1,0:T(8,128)(2,1)}, bf16[4,8,256,128]{3,2,1,0:T(8,128)(2,1)}) custom-call(s32[6]{0:T(128)} %lengths.7, bf16[8,128,128]{2,1,0:T(8,128)(2,1)} %get-tuple-element.54.q_in, bf16[8,256,128]{2,1,0:T(8,128)(2,1)} %get-tuple-element.55.kv_in), custom_call_target="tpu_custom_call" | custom-call | tf_op jit(solution)/shard_map/attend/pallas_call | solution.py:871
  121.7 16.4 %middle.1 = (bf16[8,128,128]{2,1,0:T(8,128)(2,1)}, f32[256,512]{1,0:T(8,128)}, f32[8,128]{1,0:T(8,128)}, f32[4104,128]{1,0:T(8,128)}, f32[2,512]{1,0:T(2,128)}, /*index=5*/bf16[8,4,1168,128]{3,2,1,0:T(8,128)(2,1)}) custom-call(f32[8,128]{1,0:T(8,128)} %get-tuple-element.52.counts, bf16[8,4,1168,128]{3,2,1,0:T(8,128)(2,1)} %get-tuple-element.50.weights, ...), custom_call_target="tpu_custom_call" | custom-call | tf_op jit(solution)/shard_map/middle/pallas_call | solution.py:1654
  138.1 63.3 %attend_back.1 = (bf16[8,128,128]{2,1,0:T(8,128)(2,1)}, bf16[8,256,128]{2,1,0:T(8,128)(2,1)}) custom-call(s32[6]{0:T(128)} %lengths.7, bf16[8,128,128]{2,1,0:T(8,128)(2,1)} %get-tuple-element.59.q_all, bf16[4,8,256,128]{3,2,1,0:T(8,128)(2,1)} %get-tuple-element.60.kv_in, bf16[8,128,128]{2,1,0:T(8,128)(2,1)} %get-tuple-element.61.do_in, ...), custom_call_target="tpu_custom_call" | custom-call | tf_op jit(solution)/shard_map/attend_back/pallas_call | solution.py:1130
  201.4 15.8 %ending.1 = (bf16[8,4,1168,128]{3,2,1,0:T(8,128)(2,1)}, bf16[8,4,240,128]{3,2,1,0:T(8,128)(2,1)}) custom-call(s32[6]{0:T(128)} %lengths.7, bf16[8,4,1168,128]{3,2,1,0:T(8,128)(2,1)} %get-tuple-element.58.grads_in, bf16[8,128,128]{2,1,0:T(8,128)(2,1)} %get-tuple-element.64.d_q_self, ...), custom_call_target="tpu_custom_call", output_to_operand_aliasing={{0}: (1, {})} | custom-call | tf_op jit(solution)/shard_map/ending/pallas_call | solution.py:1839
  217.2 0.0 copy-start
  217.2 0.0 copy-start.2
  217.3 0.0 copy-start.3
  217.3 60.8 %reduce_gradients.1 = (f32[1160,128]{1,0:T(8,128)}, f32[907,128]{1,0:T(8,128)}, f32[1,3]{1,0:T(1,128)}, f32[1,1]{1,0:T(1,128)}, f32[1,1]{1,0:T(1,128)}) custom-call(bf16[8,2,2,1168,128]{4,3,2,1,0:T(8,128)(2,1)} %bitcast.27, bf16[8,2,2,240,128]{4,3,2,1,0:T(8,128)(2,1)} %bitcast.30, f32[8,128]{1,0:T(8,128)} %get-tuple-element.82.refs_2_), custom_call_target="tpu_custom_call" | custom-call | tf_op jit(solution)/shard_map/reduce_gradients/pallas_call | solution.py:498
  278.1 0.0 copy-done
  278.1 0.0 copy-done.2
  278.1 0.0 copy-done.3
  278.1 0.0 copy-start.1
  278.1 0.0 copy-start.4
  278.1 0.0 copy-start.5
  278.1 0.0 copy-start.6
  278.1 3.4 %fusion.7 = (bf16[148480]{0:T(1024)(128)(2,1)}, f32[148480]{0:T(1024)}, f32[148480]{0:T(1024)}, f32[148480]{0:T(1024)}) fusion(f32[148480]{0:T(1024)S(1)} %copy-done, f32[1160,128]{1,0:T(8,128)} %get-tuple-element.83, f32[]{:T(128)} %bitcast.9, f32[148480]{0:T(1024)S(1)} %copy-done.2, f32[148480]{0:T(1024)S(1)} %copy-done.3), kind=kLoop, calls=%fused_computation.11 | loop fusion | flops 2524160 | bytes 4454404 | tf_op jit(solution)/shard_map/convert_element_type | solution.py:1868
  281.6 0.0 copy-start.7
  281.6 0.0 copy-done.1
  281.6 0.0 copy-done.4
  281.6 0.0 copy-done.5
  281.6 0.0 copy-done.6
  281.6 2.0 fusion.4
  283.7 0.0 copy-done.7
  283.7 0.5 copy.27
Async XLA Ops:
  217.2 60.8 %copy-start = (f32[148480]{0:T(1024)S(1)}, f32[148480]{0:T(1024)}, u32[]{:S(2)}) copy-start(f32[148480]{0:T(1024)} %param.18) | copy-start | bytes 1781764
  217.2 60.8 %copy-start.2 = (f32[148480]{0:T(1024)S(1)}, f32[148480]{0:T(1024)}, u32[]{:S(2)}) copy-start(f32[148480]{0:T(1024)} %param.19) | copy-start | bytes 1781764
  217.3 60.8 %copy-start.3 = (f32[148480]{0:T(1024)S(1)}, f32[148480]{0:T(1024)}, u32[]{:S(2)}) copy-start(f32[148480]{0:T(1024)} %param.20) | copy-start | bytes 1781764
  278.1 3.5 %copy-start.1 = (f32[116096]{0:T(1024)S(1)}, f32[116096]{0:T(1024)}, u32[]{:S(2)}) copy-start(f32[116096]{0:T(1024)} %param.21) | copy-start | bytes 1393156
  278.1 3.5 %copy-start.4 = (f32[116096]{0:T(1024)S(1)}, f32[116096]{0:T(1024)}, u32[]{:S(2)}) copy-start(f32[116096]{0:T(1024)} %param.22) | copy-start | bytes 1393156
  278.1 3.5 %copy-start.5 = (f32[116096]{0:T(1024)S(1)}, f32[116096]{0:T(1024)}, u32[]{:S(2)}) copy-start(f32[116096]{0:T(1024)} %param.23) | copy-start | bytes 1393156
  278.1 3.5 %copy-start.6 = (f32[907,128]{1,0:T(8,128)S(1)}, f32[907,128]{1,0:T(8,128)}, u32[]{:S(2)}) copy-start(f32[907,128]{1,0:T(8,128)} %get-tuple-element.85) | copy-start | bytes 1393156
  281.6 2.1 copy-start.7
